TPU v7x, 32 devices: a whole 2x2x4 slice. The times are simulated.
32 devices in a mesh: wave: 4 (over y, x), pix: 8 (over z, core).
Axes of the slice: x: 2, y: 2, z: 4, core: 2. Of those that a mesh axis runs over, the one named last changes fastest.
Arguments:
- raw_spectra: bfloat16 [2, 2, 16384, 2048], P(None, None, 'wave', 'pix'), may hold values from -6 to 6
- background: float32 [16384], P('wave'), may hold values from -6 to 6
- dispersion: float32 [16384], P('wave'), may hold values from -3.140625 to 3.140625
- propagator: bfloat16 [2, 2048, 2048], P(None, None, 'pix'), may hold values from -0.09375 to 0.09375
Outputs:
- image: float32 [2, 2, 16384, 2048], P(None, None, ('wave', 'pix'))
All inputs are finite; a program needn't handle non-finite values.
Results may differ from a plain program's by a relative error of at most 0.0029.
Values may be sent and summed in bfloat16 or wider, within the bound.
No kernel may reach another device: no remote copies, remote signals or barrier semaphores. Data moves between devices by JAX's collectives and lax.ppermute only.
A program may use at most 192 MiB of HBM per device.

v0:
```python
import math

import jax
import jax.numpy as jnp
from jax import lax
from jax.sharding import PartitionSpec as P

BLOCK = 1024


HIGHEST_PRECISION = lax.Precision.HIGHEST


def from_partner(value, axis, apart):
    mask = 2**apart
    pairs = [(source, source ^ mask) for source in range(lax.axis_size(axis))]
    return lax.ppermute(value, axis, pairs)


def twiddle_table(left_index, right_index, modulus):
    product = left_index[:, None] * right_index[None, :] % modulus
    phase_angle = -2.0 * math.pi / modulus * product.astype(jnp.float32)
    return (jnp.cos(phase_angle), jnp.sin(phase_angle))


def rotate(values, cosine, sine_part):
    return jnp.stack(
        (values[0] * cosine - values[1] * sine_part, values[0] * sine_part + values[1] * cosine)
    )


def local_transform(spectrum, block_size):
    length = spectrum.shape[2]
    radix_size = length // block_size
    shaped = spectrum.reshape(spectrum.shape[:2] + (radix_size, block_size) + spectrum.shape[3:])
    small_cos, small_sin = twiddle_table(
        jnp.arange(radix_size, dtype=jnp.int32), jnp.arange(radix_size, dtype=jnp.int32), radix_size
    )
    real_sum = jnp.einsum(
        "xrbp,ru->xubp", shaped[0], small_cos, precision=HIGHEST_PRECISION
    ) - jnp.einsum("xrbp,ru->xubp", shaped[1], small_sin, precision=HIGHEST_PRECISION)
    imag_sum = jnp.einsum(
        "xrbp,ru->xubp", shaped[0], small_sin, precision=HIGHEST_PRECISION
    ) + jnp.einsum("xrbp,ru->xubp", shaped[1], small_cos, precision=HIGHEST_PRECISION)
    turn_cos, turn_sin = twiddle_table(
        jnp.arange(radix_size, dtype=jnp.int32), jnp.arange(block_size, dtype=jnp.int32), length
    )
    mixed_terms = rotate(
        jnp.stack((real_sum, imag_sum)), turn_cos[:, :, None], turn_sin[:, :, None]
    )
    big_cos, big_sin = twiddle_table(
        jnp.arange(block_size, dtype=jnp.int32), jnp.arange(block_size, dtype=jnp.int32), block_size
    )
    out_real = jnp.einsum(
        "xubp,bv->xuvp", mixed_terms[0], big_cos, precision=HIGHEST_PRECISION
    ) - jnp.einsum("xubp,bv->xuvp", mixed_terms[1], big_sin, precision=HIGHEST_PRECISION)
    out_imag = jnp.einsum(
        "xubp,bv->xuvp", mixed_terms[0], big_sin, precision=HIGHEST_PRECISION
    ) + jnp.einsum("xubp,bv->xuvp", mixed_terms[1], big_cos, precision=HIGHEST_PRECISION)
    return jnp.stack((out_real, out_imag))


def on_device(raw_spectra, background, dispersion, propagator):
    row_count = raw_spectra.shape[1]
    wave_span = raw_spectra.shape[2]
    pix_local = raw_spectra.shape[3]
    wave_count = lax.axis_size("wave")
    pix_count = lax.axis_size("pix")
    devices = wave_count * pix_count
    length = wave_span * wave_count
    wave_pos = lax.axis_index("wave")
    bit_count = wave_count.bit_length() - 1
    real_part = raw_spectra[0].astype(jnp.float32) - background[None, :, None]
    imag_part = raw_spectra[1].astype(jnp.float32)
    spectrum = rotate(
        jnp.stack((real_part, imag_part)),
        jnp.cos(dispersion)[None, :, None],
        jnp.sin(dispersion)[None, :, None],
    )
    for section_index in range(bit_count):
        bit_index = bit_count - 1 - section_index
        half_span = 1 << bit_index
        partner = from_partner(spectrum, "wave", bit_index)
        upper_half = wave_pos // half_span % 2 == 1
        phase_angle = -math.pi / half_span * (wave_pos % half_span).astype(jnp.float32)
        turned = rotate(partner - spectrum, jnp.cos(phase_angle), jnp.sin(phase_angle))
        spectrum = jnp.where(upper_half, turned, spectrum + partner)
    owner_index = jnp.int32(0)
    for bit_index in range(bit_count):
        owner_index = owner_index + wave_pos // (1 << bit_index) % 2 * (
            1 << bit_count - 1 - bit_index
        )
    positions = jnp.arange(wave_span, dtype=jnp.int32)
    phase_angle = -2.0 * math.pi / length * (positions * owner_index % length).astype(jnp.float32)
    spectrum = rotate(
        spectrum, jnp.cos(phase_angle)[None, :, None], jnp.sin(phase_angle)[None, :, None]
    )
    transform = local_transform(spectrum, BLOCK)
    radix_size = transform.shape[2]
    depth_bf = (transform * (1.0 / math.sqrt(length))).astype(jnp.bfloat16)
    depth_width = BLOCK // devices
    outgoing = depth_bf.reshape(
        2, row_count, radix_size, wave_count, pix_count, depth_width, pix_local
    )
    merged = outgoing.reshape(2, row_count, radix_size, devices, depth_width, pix_local)
    arrived = lax.all_to_all(
        merged, ("wave", "pix"), split_axis=3, concat_axis=3, tiled=True
    ).reshape(outgoing.shape)
    bit_shape = (2,) * bit_count
    dim_count = len(bit_shape)
    spread = arrived.reshape(
        (2, row_count, radix_size) + bit_shape + (pix_count, depth_width, pix_local)
    )
    wave_axes = tuple(range(3, 3 + dim_count))
    wave_axes = wave_axes[::-1]
    axis_order = (0, 1, 4 + dim_count, 2) + wave_axes + (3 + dim_count, 5 + dim_count)
    depth_field = jnp.transpose(spread, axis_order).reshape(
        2, row_count, depth_width * radix_size * wave_count, pix_count * pix_local
    )
    column_piece = lax.all_gather(propagator, "pix", axis=2, tiled=True)
    image_real = jnp.dot(
        depth_field[0], column_piece[0], preferred_element_type=jnp.float32
    ) - jnp.dot(depth_field[1], column_piece[1], preferred_element_type=jnp.float32)
    image_imag = jnp.dot(
        depth_field[0], column_piece[1], preferred_element_type=jnp.float32
    ) + jnp.dot(depth_field[1], column_piece[0], preferred_element_type=jnp.float32)
    return jnp.stack((image_real, image_imag))


def solution(mesh):
    in_specs = (P(None, None, "wave", "pix"), P("wave"), P("wave"), P(None, None, "pix"))
    out_specs = P(None, None, ("wave", "pix"), None)
    return jax.shard_map(
        on_device, mesh=mesh, in_specs=in_specs, out_specs=out_specs, check_vma=False
    )
```

profile of v0, /device:TPU:0, one launch (start us, length us, event | category | flops | bytes accessed | tf_op | source)
XLA Modules:
  0.0 1537.6 jit_solution(7462445002151492449)
XLA Ops:
  6.5 0.0 all-gather.2.cloned.1.call-start
  6.5 0.8 fusion.101
  7.3 7.7 fusion.1
  15.0 0.0 copy-start
  15.0 0.0 copy-start.2
  15.0 6.7 pad_maximum_fusion
  21.8 1.5 copy-done
  23.3 2.5 copy-done.2
  25.8 3.0 collective-permute-start
  28.9 360.3 %collective-permute-done = f32[2,2,4096,256]{3,2,1,0:T(8,128)} collective-permute-done((f32[2,2,4096,256]{3,2,1,0:T(8,128)}, f32[2,2,4096,256]{3,2,1,0:T(8,128)}, u32[]{:S(2)}, u32[]{:S(2)}) %collective-permute-start) | collective-permute-done | bytes 16777248 | tf_op jit(solution)/shard_map/ppermute | solution.py:17
  389.3 17.9 %fusion.98 = f32[2,2,4096,256]{3,2,1,0:T(8,128)} fusion(f32[2,2,4096,256]{3,2,1,0:T(8,128)} %collective-permute-done, f32[1,2,4096,256]{3,2,1,0:T(8,128)} %copy-done.2, f32[1,2,4096,256]{3,2,1,0:T(8,128)} %copy-done), kind=kLoop, calls=%fused_computation.118 | loop fusion | flops 8388608 | bytes 50331648 | tf_op jit(solution)/shard_map/sub | solution.py:86
  407.2 0.0 copy-start.1
  407.2 0.0 copy-start.3
  407.2 12.7 multiply_subtract_fusion.2
  419.9 1.3 copy-done.1
  421.2 2.4 copy-done.3
  423.6 17.8 %maximum_select_fusion = f32[2,2,4096,256]{3,2,1,0:T(8,128)} fusion(f32[1,2,4096,256]{3,2,1,0:T(8,128)} %get-tuple-element.12, f32[1,2,4096,256]{3,2,1,0:T(8,128)} %get-tuple-element.11, f32[2,2,4096,256]{3,2,1,0:T(8,128)} %collective-permute-done, pred[]{:T(512)S(6)} %eq.22, f32[1,2,4096,256]{3,2,1,0:T(8,128)S(1)} %copy-done.3, ...), kind=kLoop, calls=%fused_computation.1 | loop fusion | flops 16777216 | bytes 67108864 | tf_op jit(solution)/shard_map/jit(_where)/select_n | solution.py:87
  441.4 1.7 collective-permute-start.1
  443.1 0.0 all-gather.2.cloned.1.call-update
  443.1 0.2 fusion.49
  443.3 0.2 copy.25
  443.5 0.2 copy.27
  443.8 0.1 fusion.48
  443.9 0.2 copy.31
  444.1 0.1 fusion.47
  444.3 0.2 copy.32
  444.5 358.6 %collective-permute-done.1 = f32[2,2,4096,256]{3,2,1,0:T(8,128)} collective-permute-done((f32[2,2,4096,256]{3,2,1,0:T(8,128)}, f32[2,2,4096,256]{3,2,1,0:T(8,128)}, u32[]{:S(2)}, u32[]{:S(2)}) %collective-permute-start.1) | collective-permute-done | bytes 16777248 | tf_op jit(solution)/shard_map/ppermute | solution.py:17
  803.1 27.9 %fusion.108 = f32[2,2,4096,256]{3,2,1,0:T(8,128)} fusion(f32[2,2,4096,256]{3,2,1,0:T(8,128)} %collective-permute-done.1, f32[2,2,4096,256]{3,2,1,0:T(8,128)} %collective-permute-done, f32[1,2,4096,256]{3,2,1,0:T(8,128)} %copy-done.2, f32[1,2,4096,256]{3,2,1,0:T(8,128)} %copy-done, f32[1,2,4096,256]{3,2,1,0:T(8,128)} %get-tuple-element.12, ...), kind=kLoop, calls=%fused_computation.122 | loop fusion | flops 20971520 | bytes 83886080 | tf_op jit(solution)/shard_map/sub | solution.py:86
  831.0 11.6 multiply_subtract_fusion.1
  842.6 33.1 %maximum_select_fusion.1 = f32[2,2,4096,256]{3,2,1,0:T(8,128)} fusion(f32[1,2,4096,256]{3,2,1,0:T(8,128)} %get-tuple-element.10, f32[1,2,4096,256]{3,2,1,0:T(8,128)} %get-tuple-element.9, f32[2,2,4096,256]{3,2,1,0:T(8,128)} %collective-permute-done.1, pred[]{:T(512)S(6)} %eq.21, f32[2,2,4096,256]{3,2,1,0:T(8,128)} %collective-permute-done, ...), kind=kLoop, calls=%fused_computation.2 | loop fusion | flops 29360128 | bytes 100663296 | tf_op jit(solution)/shard_map/jit(_where)/select_n | solution.py:87
  875.7 6.4 fusion.99
  882.1 28.1 %fusion.54 = f32[4,2,1024,256]{3,0,2,1:T(4,128)} fusion(f32[2,4,1024,256]{3,2,1,0:T(8,128)S(1)} %bitcast.84, f32[2,4,1024,256]{3,2,1,0:T(8,128)S(1)} %bitcast.80, f32[4,1024]{0,1:T(8,128)S(1)} %copy.27, f32[4,1024]{0,1:T(8,128)S(1)} %copy.25), kind=kOutput, calls=%fused_computation.78 | convolution fusion | flops 106954976 | bytes 25198592 | tf_op jit(solution)/shard_map/xrbp,ru->xubp/dot_general | solution.py:44
  910.3 27.6 %fusion.58 = f32[4,2,1024,256]{3,0,2,1:T(4,128)} fusion(f32[2,4,1024,256]{3,2,1,0:T(8,128)S(1)} %bitcast.85, f32[2,4,1024,256]{3,2,1,0:T(8,128)S(1)} %bitcast.81, f32[4,1024]{0,1:T(8,128)S(1)} %copy.27, f32[4,1024]{0,1:T(8,128)S(1)} %copy.25), kind=kOutput, calls=%fused_computation.82 | convolution fusion | flops 106954976 | bytes 25198592 | tf_op jit(solution)/shard_map/xrbp,ru->xubp/dot_general | solution.py:41
  937.9 30.0 %convolution_subtract_fusion = f32[4,2,1024,256]{3,0,2,1:T(4,128)} fusion(f32[4,2,1024,256]{3,0,2,1:T(4,128)} %fusion.58, f32[2,4,1024,256]{3,2,1,0:T(8,128)S(1)} %bitcast.86, f32[2,4,1024,256]{3,2,1,0:T(8,128)S(1)} %bitcast.82, f32[4,1024]{0,1:T(8,128)S(1)} %copy.27, f32[4,1024]{0,1:T(8,128)S(1)} %copy.25), kind=kOutput, calls=%fused_computation.41 | convolution fusion | flops 109052128 | bytes 33587200 | tf_op jit(solution)/shard_map/xrbp,ru->xubp/dot_general | solution.py:39
  967.9 34.7 %subtract_bitcast_fusion.1 = (f32[2,4,1024,256]{3,1,2,0:T(4,128)}, f32[2,4,1024,256]{3,1,2,0:T(4,128)}) fusion(f32[4,2,1024,256]{3,0,2,1:T(4,128)} %convolution_subtract_fusion, f32[4,1024]{0,1:T(8,128)S(1)} %copy.32, f32[4,1024]{0,1:T(8,128)S(1)} %copy.31, f32[4,2,1024,256]{3,0,2,1:T(4,128)} %fusion.54, f32[2,4,1024,256]{3,2,1,0:T(8,128)S(1)} %bitcast.87, ...), kind=kOutput, calls=%fused_computation.17 | convolution fusion | flops 121635040 | bytes 50397184 | tf_op jit(solution)/shard_map/xrbp,ru->xubp/dot_general | solution.py:42
  1002.6 0.0 copy-start.6
  1002.6 0.0 slice-start
  1002.6 62.0 %fusion.5 = f32[1024,2,4,256]{3,0,2,1:T(8,128)} fusion(f32[2,4,1024,256]{3,1,2,0:T(4,128)} %get-tuple-element.6), kind=kOutput, calls=%fused_computation.27 | convolution fusion | flops 25784483840 | bytes 16777216 | tf_op jit(solution)/shard_map/xubp,bv->xuvp/dot_general | solution.py:56
  1064.7 0.0 copy-done.6
  1064.7 0.0 slice-start.1
  1064.7 72.2 %fusion.3 = f32[1024,2,4,256]{3,0,2,1:T(8,128)} fusion(f32[2,4,1024,256]{3,1,2,0:T(4,128)S(1)} %copy-done.6), kind=kOutput, calls=%fused_computation.25 | convolution fusion | flops 25784483840 | bytes 16777216 | tf_op jit(solution)/shard_map/xubp,bv->xuvp/dot_general | solution.py:59
  1136.9 0.0 slice-done
  1136.9 0.0 slice-done.1
  1136.9 59.3 %fusion.25 = f32[1024,2,4,256]{3,0,2,1:T(8,128)S(1)} fusion(f32[1024,2,4,256]{3,0,2,1:T(8,128)} %fusion.5, f32[2,4,1024,256]{3,1,2,0:T(4,128)S(1)} %bitcast.89), kind=kOutput, calls=%fused_computation.52 | convolution fusion | flops 25786580992 | bytes 25165824 | tf_op jit(solution)/shard_map/xubp,bv->xuvp/dot_general | solution.py:54
  1196.3 48.6 %fusion.30 = f32[1024,2,4,256]{3,0,2,1:T(8,128)S(1)} fusion(f32[1024,2,4,256]{3,0,2,1:T(8,128)} %fusion.3, f32[2,4,1024,256]{3,1,2,0:T(4,128)} %get-tuple-element.5), kind=kOutput, calls=%fused_computation.53 | convolution fusion | flops 25786580992 | bytes 25165824 | tf_op jit(solution)/shard_map/xubp,bv->xuvp/dot_general | solution.py:57
  1244.9 2.7 fusion
  1247.6 190.6 %all_to_all.5 = bf16[2,2,4,32,32,256]{5,4,2,1,0,3:T(8,128)(2,1)} all-to-all(bf16[2,2,4,32,32,256]{5,4,2,1,0,3:T(8,128)(2,1)S(1)} %fusion), channel_id=1, replica_groups=mesh['wave'=4,'pix'=8] {'wave','pix'}, dimensions={3} | all-to-all | bytes 16777216 | tf_op jit(solution)/shard_map/all_to_all | solution.py:106
  1438.2 11.7 copy.77
  1449.9 6.3 fusion.100
  1456.1 7.4 squeeze.14
  1463.5 7.4 squeeze.16
  1470.9 0.0 all-gather.2.cloned.1.call-done
  1470.9 0.0 copy-start.5
  1470.9 14.6 fusion.12
  1485.5 0.0 copy-done.5
  1485.5 13.4 fusion.11
  1498.9 0.0 copy-start.4
  1498.9 12.7 subtract_bitcast_fusion
  1511.7 0.0 copy-done.4
  1511.7 12.6 add_bitcast_fusion
  1524.3 6.2 pad_maximum_fusion.2
  (1 shorter events, 0.0 us)
Async XLA Ops:
  6.5 1464.4 %all-gather.2.cloned.1.call-start = ((), (), s32[]{:S(2)}) async-start(), calls=%async_computation.1 | async-start | bytes 18874368 | tf_op jit(solution)/shard_map/all_gather | solution.py:120
  15.0 8.3 copy-start
  15.0 10.8 copy-start.2
  25.8 363.5 %collective-permute-start = (f32[2,2,4096,256]{3,2,1,0:T(8,128)}, f32[2,2,4096,256]{3,2,1,0:T(8,128)}, u32[]{:S(2)}, u32[]{:S(2)}) collective-permute-start(f32[2,2,4096,256]{3,2,1,0:T(8,128)} %pad_maximum_fusion), channel_id=1, source_target_pairs={{0,16},{8,24},{16,0},{24,8},{1,17},{9,25},{17,1},{25,9},{2,18},{10... | collective-permute-start | bytes 50331656 | tf_op jit(solution)/shard_map/ppermute | solution.py:17
  407.2 14.0 copy-start.1
  407.2 16.4 %copy-start.3 = (f32[1,2,4096,256]{3,2,1,0:T(8,128)S(1)}, f32[1,2,4096,256]{3,2,1,0:T(8,128)}, u32[]{:S(2)}) copy-start(f32[1,2,4096,256]{3,2,1,0:T(8,128)} %copy-done.2) | copy-start | bytes 25165828
  441.4 361.7 %collective-permute-start.1 = (f32[2,2,4096,256]{3,2,1,0:T(8,128)}, f32[2,2,4096,256]{3,2,1,0:T(8,128)}, u32[]{:S(2)}, u32[]{:S(2)}) collective-permute-start(f32[2,2,4096,256]{3,2,1,0:T(8,128)} %maximum_select_fusion), channel_id=1, source_target_pairs={{0,8},{8,0},{16,24},{24,16},{1,9},{9,1},{17,25},{25,17},{2,10},{10... | collective-permute-start | bytes 50331656 | tf_op jit(solution)/shard_map/ppermute | solution.py:17
  1002.6 62.1 %copy-start.6 = (f32[2,4,1024,256]{3,1,2,0:T(4,128)S(1)}, f32[2,4,1024,256]{3,1,2,0:T(4,128)}, u32[]{:S(2)}) copy-start(f32[2,4,1024,256]{3,1,2,0:T(4,128)} %get-tuple-element.6) | copy-start | bytes 25165828
  1002.6 134.3 %slice-start = ((s8[8388608]{0:T(1024)(128)(4,1)}), s8[4194304]{0:T(1024)(128)(4,1)S(1)}, s32[]{:S(2)}) async-start(s8[8388608]{0:T(1024)(128)(4,1)} %bitcast.88), calls=%async_computation.2 | async-start | bytes 8388608
  1064.7 72.2 %slice-start.1 = ((s8[8388608]{0:T(1024)(128)(4,1)}), s8[4194304]{0:T(1024)(128)(4,1)S(1)}, s32[]{:S(2)}) async-start(s8[8388608]{0:T(1024)(128)(4,1)} %bitcast.88), calls=%async_computation.3 | async-start | bytes 8388608
  1470.9 14.6 copy-start.5
  1498.9 12.8 copy-start.4
Sparse Core Ops, SparseCore 0:
  443.3 152.1 all-gather.1
where the time goes:
time: 1540 us
  waiting for transfers between devices  719 us (47%)
  matrix products  416 us (27%)
  blocking collectives  191 us (12%)
  other arithmetic  145 us (9%)
  local copies, waits for them, and re-layouts  48.6 us (3%)
    ppermute x2, waiting for transfers between devices, from_partner(): return lax.ppermute(value, axis, pairs)  719 us
    all_to_all x1, blocking collectives, on_device(): lax.all_to_all(merged, ('wave', 'pix'), split_axis=3, concat_axis=3, tile...  191 us
    dot_general x1, matrix products, local_transform(): jnp.einsum('xubp,bv->xuvp', mixed_terms[1], big_cos, precision=HIGHEST_PR...  72.2 us
    dot_general x1, matrix products, local_transform(): jnp.einsum('xubp,bv->xuvp', mixed_terms[1], big_sin, precision=HIGHEST_PR...  62 us
    dot_general x1, matrix products, local_transform(): jnp.einsum('xubp,bv->xuvp', mixed_terms[0], big_cos, precision=HIGHEST_PR...  59.3 us
    select_n x2, other arithmetic, on_device(): spectrum = jnp.where(upper_half, turned, spectrum + partner)  50.9 us
    dot_general x1, matrix products, local_transform(): jnp.einsum('xubp,bv->xuvp', mixed_terms[0], big_sin, precision=HIGHEST_PR...  48.6 us
    sub x2, other arithmetic, on_device(): partner - spectrum  45.8 us
  transfers between devices with their start and end apart: 3, of which 2 were waited for; matrix products, arithmetic and copies ran while one was open for 31% of the time, Pallas kernels for 0%

commit v1 on v0

v1 whole, which is shorter than its diff:
```python
import functools
import math

import jax
import jax.numpy as jnp
import numpy as np
from jax import lax
from jax.experimental import pallas as pl
from jax.experimental.pallas import tpu as pltpu
from jax.sharding import PartitionSpec as P

CHUNK = 16
VMEM_BYTES = 56 * 1024 * 1024


def unit_roots(rows, columns, modulus):
    product = np.outer(np.arange(rows), np.arange(columns)) % modulus
    angle = -2.0 * np.pi / modulus * product
    return np.cos(angle), np.sin(angle)


def split(value):
    high = value.astype(jnp.bfloat16)
    return high, (value - high.astype(jnp.float32)).astype(jnp.bfloat16)


def transform_kernel(
    steps, x_ref, phase_ref, small_ref, turn_ref, fine_ref, out_ref, data, high, low, part
):
    step = pl.program_id(0)
    k1_count, pixels = data.shape[2], data.shape[3]

    @pl.when(step < steps)
    def _():
        for c in range(2):
            block = x_ref[:, c].reshape(k1_count, CHUNK, pixels).astype(jnp.float32)
            data[c] = jnp.swapaxes(block, 0, 1).astype(jnp.bfloat16)
        for i in range(CHUNK):
            turn_real = turn_ref[0, 0, :, i : i + 1]
            turn_imag = turn_ref[1, 0, :, i : i + 1]
            cosine = phase_ref[0, i : i + 1, :]
            sine = phase_ref[1, i : i + 1, :]
            background = phase_ref[2, i : i + 1, :]
            small_real = small_ref[0] * turn_real - small_ref[1] * turn_imag
            small_imag = small_ref[0] * turn_imag + small_ref[1] * turn_real
            real = small_real * cosine - small_imag * sine
            imag = small_real * sine + small_imag * cosine
            base_real = jnp.sum(real * background, axis=1, keepdims=True)
            base_imag = jnp.sum(imag * background, axis=1, keepdims=True)
            real_high, real_low = split(real)
            imag_high, imag_low = split(imag)
            matrix = jnp.concatenate((real_high, imag_high, real_low, imag_low), axis=0)
            columns = jnp.concatenate((data[0, i], data[1, i]), axis=1)
            both = jnp.dot(matrix, columns, preferred_element_type=jnp.float32)
            half = 2 * k1_count
            both = both[:half] + both[half:]
            by_real, by_imag = both[:k1_count], both[k1_count:]
            part[0, i] = by_real[:, :pixels] - by_imag[:, pixels:] - base_real
            part[1, i] = by_real[:, pixels:] + by_imag[:, :pixels] - base_imag
        at = pl.ds(pl.multiple_of(step * CHUNK, CHUNK), CHUNK)
        for c in range(2):
            turned = jnp.swapaxes(part[c], 0, 1)
            turned_high, turned_low = split(turned)
            high[c, :, at, :] = turned_high
            low[c, :, at, :] = turned_low

    @pl.when(step >= steps)
    def _():
        first = (step - steps) * CHUNK
        for i in range(CHUNK):
            at = first + i
            columns = jnp.concatenate((high[0, at], high[1, at]), axis=1)
            rest = jnp.concatenate((low[0, at], low[1, at]), axis=1)
            both = jnp.dot(fine_ref[...], columns, preferred_element_type=jnp.float32)
            half = both.shape[0] // 2
            both = (
                both[:half]
                + both[half:]
                + jnp.dot(fine_ref[:half], rest, preferred_element_type=jnp.float32)
            )
            by_real, by_imag = both[: half // 2], both[half // 2 :]
            part[0, i] = by_real[:, :pixels] - by_imag[:, pixels:]
            part[1, i] = by_real[:, pixels:] + by_imag[:, :pixels]
        for c in range(2):
            turned = jnp.swapaxes(part[c], 0, 1).astype(jnp.bfloat16)
            out_ref[:, c] = turned.reshape(out_ref.shape[:1] + out_ref.shape[2:])


def depth_transform(blocks, phases, devices):
    wave_count, _, k1_part, k0_count, pixels = blocks.shape
    k1_count = wave_count * k1_part
    length = k1_count * k0_count
    z0_count, z1_count = k1_count, k0_count
    steps = k0_count // CHUNK
    small = np.stack(unit_roots(z0_count, k1_count, k1_count)).astype(np.float32)
    turn = np.stack(unit_roots(z0_count, k0_count, length)).astype(np.float32)
    turn = turn.reshape(2, z0_count, steps, CHUNK).transpose(0, 2, 1, 3)
    fine = np.concatenate(unit_roots(z1_count, k0_count, k0_count), axis=0) / math.sqrt(length)
    fine_high = fine.astype(jnp.bfloat16)
    fine_low = (fine - fine_high.astype(np.float64)).astype(jnp.bfloat16)
    fine = np.concatenate((fine_high, fine_low), axis=0)
    out_shape = (devices, 2, z1_count // devices, z0_count, pixels)
    return pl.pallas_call(
        functools.partial(transform_kernel, steps),
        out_shape=jax.ShapeDtypeStruct(out_shape, jnp.bfloat16),
        grid=(2 * steps,),
        in_specs=[
            pl.BlockSpec(
                (wave_count, 2, k1_part, CHUNK, pixels),
                lambda i: (0, 0, 0, jnp.minimum(i, steps - 1), 0),
            ),
            pl.BlockSpec((3, CHUNK, k1_count), lambda i: (0, jnp.minimum(i, steps - 1), 0)),
            pl.BlockSpec(small.shape, lambda i: (0, 0, 0)),
            pl.BlockSpec(
                (2, 1, z0_count, CHUNK), lambda i: (0, jnp.minimum(i, steps - 1), 0, 0)
            ),
            pl.BlockSpec(fine.shape, lambda i: (0, 0)),
        ],
        out_specs=pl.BlockSpec(
            out_shape[:3] + (CHUNK, pixels), lambda i: (0, 0, 0, jnp.maximum(i - steps, 0), 0)
        ),
        scratch_shapes=[
            pltpu.VMEM((2, CHUNK, k1_count, pixels), jnp.bfloat16),
            pltpu.VMEM((2, z0_count, k0_count, pixels), jnp.bfloat16),
            pltpu.VMEM((2, z0_count, k0_count, pixels), jnp.bfloat16),
            pltpu.VMEM((2, CHUNK, z0_count, pixels), jnp.float32),
        ],
        compiler_params=pltpu.CompilerParams(vmem_limit_bytes=VMEM_BYTES),
        cost_estimate=pl.CostEstimate(
            flops=2 * 5 * 4 * 128 * length * pixels,
            bytes_accessed=8 * length * pixels,
            transcendentals=0,
        ),
    )(blocks, phases, jnp.asarray(small), jnp.asarray(turn), jnp.asarray(fine))


def refocus_kernel(row_count, pix_count, tile, depth_ref, prop_ref, out_ref):
    senders = depth_ref.shape[0]
    pieces = senders // (row_count * pix_count)
    depths = depth_ref.shape[2]
    for r in range(row_count):
        for t in range(depths // tile):
            rows = pl.ds(t * tile, tile)
            parts = []
            for c in range(2):
                parts.append(
                    jnp.concatenate(
                        [
                            depth_ref[(r * pieces + h) * pix_count + p, c, rows, :]
                            for p in range(pix_count)
                            for h in range(pieces)
                        ],
                        axis=1,
                    )
                )
            dot = functools.partial(jnp.dot, preferred_element_type=jnp.float32)
            real, imag = parts
            out_ref[0, r, rows, :] = dot(real, prop_ref[0, 0]) - dot(imag, prop_ref[0, 1])
            out_ref[1, r, rows, :] = dot(real, prop_ref[0, 1]) + dot(imag, prop_ref[0, 0])


def refocus(depth, propagator, row_count):
    pix_count, _, span, width = propagator.shape
    depths = depth.shape[2]
    tile = min(256, depths)
    return pl.pallas_call(
        functools.partial(refocus_kernel, row_count, pix_count, tile),
        out_shape=jax.ShapeDtypeStruct(
            (2, row_count, depths, pix_count * width), jnp.float32
        ),
        grid=(pix_count,),
        in_specs=[
            pl.BlockSpec(depth.shape, lambda q: (0, 0, 0, 0)),
            pl.BlockSpec((1, 2, span, width), lambda q: (q, 0, 0, 0)),
        ],
        out_specs=pl.BlockSpec((2, row_count, depths, width), lambda q: (0, 0, 0, q)),
        compiler_params=pltpu.CompilerParams(vmem_limit_bytes=VMEM_BYTES),
        cost_estimate=pl.CostEstimate(
            flops=8 * row_count * depths * span * pix_count * width,
            bytes_accessed=32 * 1024 * 1024,
            transcendentals=0,
        ),
    )(depth, propagator)


def on_device(raw_spectra, background, dispersion, propagator):
    _, row_count, wave_span, pix_local = raw_spectra.shape
    wave_count = lax.axis_size("wave")
    pix_count = lax.axis_size("pix")
    devices = wave_count * pix_count
    pieces = wave_count // row_count
    pixels = pix_local // pieces
    k0_count = 128
    k1_part = wave_span // k0_count

    columns = lax.all_gather(propagator, "pix", axis=0, tiled=False)
    phases = jnp.stack((jnp.cos(dispersion), jnp.sin(dispersion), background))
    phases = lax.all_gather(phases.reshape(3, k1_part, k0_count), "wave", axis=1, tiled=True)
    phases = jnp.swapaxes(phases, 1, 2)

    outgoing = raw_spectra.reshape(2, row_count, wave_span, pieces, pixels)
    outgoing = jnp.transpose(outgoing, (1, 3, 0, 2, 4)).reshape(
        wave_count, 2, wave_span, pixels
    )
    blocks = lax.all_to_all(outgoing, "wave", split_axis=0, concat_axis=0, tiled=True)
    blocks = blocks.reshape(wave_count, 2, k1_part, k0_count, pixels)
    depth = depth_transform(blocks, phases, devices)
    depth = depth.reshape(devices, 2, -1, pixels)
    depth = lax.all_to_all(depth, ("wave", "pix"), split_axis=0, concat_axis=0, tiled=True)
    return refocus(depth, columns, row_count)


def solution(mesh):
    in_specs = (P(None, None, "wave", "pix"), P("wave"), P("wave"), P(None, None, "pix"))
    out_specs = P(None, None, ("wave", "pix"), None)
    return jax.shard_map(
        on_device, mesh=mesh, in_specs=in_specs, out_specs=out_specs, check_vma=False
    )
```

time: 1540 us -> 419 us (0.27)
  waiting for transfers between devices: 719 us -> 0.71 us
  matrix products: 416 us -> 0 us
  other arithmetic: 145 us -> 0.01 us
  blocking collectives: 191 us -> 288 us
  Pallas kernels: 0 us -> 87.7 us
  local copies, waits for them, and re-layouts: 48.6 us -> 22.6 us
    ppermute x2 -> x0, waiting for transfers between devices: 719 us -> none  [from_partner(): return lax.ppermute(value, axis, pairs)]
    dot_general x12 -> x0, matrix products: 416 us -> none  [the longest x1 72.2 us: local_transform(): jnp.einsum('xubp,bv->xuvp', mixed_terms[1], big_cos, precision=HIGHEST_PR...]
    all_gather x0 -> x1, blocking collectives: none -> 97.9 us  [on_device(): lax.all_gather(phases.reshape(3, k1_part, k0_count), 'wave', axis=1, tile...]
    pallas_call x0 -> x2, Pallas kernels: none -> 87.7 us  [the longest x1 46.3 us: depth_transform(): pl.pallas_call(functools.partial(transform_kernel, steps), out_shape=jax....]
    sub x5 -> x0, other arithmetic: 77.8 us -> none  [the longest x2 45.8 us: on_device(): partner - spectrum]
    select_n x2 -> x0, other arithmetic: 50.9 us -> none  [on_device(): spectrum = jnp.where(upper_half, turned, spectrum + partner)]
  transfers between devices with their start and end apart: 3 -> 2, of which waited for: 2 -> 0; matrix products, arithmetic and copies ran while one was open for 31% -> 5% of each run, Pallas kernels for 0% -> 11%
where the time goes in v1:
time: 419 us; the launch traced here: 418 us
  blocking collectives  288 us (69%)
  Pallas kernels  87.7 us (21%)
  local copies, waits for them, and re-layouts  22.6 us (5%)
  between operations  13.4 us (3%)
  starting transfers between devices  5.8 us (1%)
    all_to_all x1, blocking collectives, on_device(): lax.all_to_all(depth, ('wave', 'pix'), split_axis=0, concat_axis=0, tiled...  190 us
    all_gather x1, blocking collectives, on_device(): lax.all_gather(phases.reshape(3, k1_part, k0_count), 'wave', axis=1, tile...  97.9 us
    pallas_call x1, Pallas kernels, depth_transform(): pl.pallas_call(functools.partial(transform_kernel, steps), out_shape=jax....  46.3 us
    pallas_call x1, Pallas kernels, refocus(): pl.pallas_call(functools.partial(refocus_kernel, row_count, pix_count, ti...  41.4 us
    reshape x1, local copies, waits for them, and re-layouts, on_device(): outgoing = raw_spectra.reshape(2, row_count, wave_span, pieces, pixels)  12.6 us
    transpose x1, local copies, waits for them, and re-layouts, on_device(): jnp.transpose(outgoing, (1, 3, 0, 2, 4))  9.14 us
  transfers between devices with their start and end apart: 2, of which 0 were waited for; matrix products, arithmetic and copies ran while one was open for 5% of the time, Pallas kernels for 11%

profile of v1, /device:TPU:0, one launch (start us, length us, event | category | flops | bytes accessed | tf_op | source)
XLA Modules:
  0.0 418.2 jit_solution(17908230043478502276)
XLA Ops:
  6.5 0.0 all-gather.3.cloned.1.call-start
  6.5 0.7 all-gather.3.cloned.1.call-update
  7.3 12.6 %reshape.19 = bf16[2,2,4096,2,128]{4,3,2,1,0:T(2,128)(2,1)} reshape(bf16[2,2,4096,256]{3,2,1,0:T(8,128)(2,1)} %param.7) | data formatting | bytes 16777216 | tf_op jit(solution)/shard_map/reshape | solution.py:201
  19.9 9.1 %copy.13 = bf16[2,2,2,4096,128]{4,3,2,1,0:T(8,128)(2,1)} copy(bf16[2,2,2,4096,128]{4,1,3,0,2:T(2,128)(2,1)} %bitcast.14) | data formatting | bytes 16777216 | tf_op jit(solution)/shard_map/transpose | solution.py:202
  29.0 0.0 copy-start
  29.0 0.0 copy-start.1
  29.0 5.8 %all-to-all-start = ((bf16[4,2,4096,128]{3,2,1,0:T(8,128)(2,1)}), bf16[4,2,4096,128]{3,2,1,0:T(8,128)(2,1)}, u32[]{:S(2)}, u32[]{:S(2)}) async-start(bf16[4,2,4096,128]{3,2,1,0:T(8,128)(2,1)} %bitcast.13), calls=%async_computation | async-start | bytes 16777216 | tf_op jit(solution)/shard_map/all_to_all | solution.py:205
  34.8 0.0 copy-done
  34.8 0.1 cosine_bitcast_fusion
  34.9 0.0 copy-done.1
  34.9 97.9 %all_gather.9 = f32[3,128,128]{2,1,0:T(8,128)S(1)} all-gather(f32[3,32,128]{2,1,0:T(8,128)S(1)} %pad_maximum_fusion), channel_id=1, replica_groups=mesh['wave'=4,'pix'=8] {'wave'}, dimensions={1}, use_global_device_ids=true | all-gather | bytes 245760 | tf_op jit(solution)/shard_map/all_gather | solution.py:198
  132.8 0.8 copy.14
  133.6 0.0 all-to-all-done
  133.6 46.3 %shard_map.73 = bf16[32,2,4,128,128]{4,3,2,1,0:T(8,128)(2,1)} custom-call(bf16[4,2,32,128,128]{4,3,2,1,0:T(8,128)(2,1)} %bitcast.2.x_ref, f32[3,128,128]{2,1,0:T(8,128)} %bitcast.16, f32[2,128,128]{2,1,0:T(8,128)} %constant.6.clone.small_ref, f32[2,8,128,16]{3,2,1,0:T(8,128)} %constant.7.clone.turn_ref, bf16[512,128]{1,0:T(8,128)(2,1)} %constant.8.clone.fine_ref), custom_call_target="tpu_custom_call" | custom-call | flops 10737418240 | bytes 16777216 | tf_op jit(solution)/shard_map/pallas_call | solution.py:103
  179.9 190.1 %all_to_all.10.depth_ref = bf16[32,2,512,128]{3,2,1,0:T(8,128)(2,1)} all-to-all(bf16[32,2,512,128]{3,2,1,0:T(8,128)(2,1)} %bitcast.15), channel_id=1, replica_groups=mesh['wave'=4,'pix'=8] {'wave','pix'}, dimensions={0} | all-to-all | bytes 16777216 | tf_op jit(solution)/shard_map/all_to_all | solution.py:209
  369.9 0.0 all-gather.3.cloned.1.call-done
  369.9 41.4 %shard_map.74 = f32[2,2,512,2048]{3,2,1,0:T(8,128)} custom-call(bf16[32,2,512,128]{3,2,1,0:T(8,128)(2,1)} %all_to_all.10.depth_ref, bf16[8,2,2048,256]{3,2,1,0:T(8,128)(2,1)} %bitcast.18), custom_call_target="tpu_custom_call" | custom-call | flops 34359738368 | bytes 33554432 | tf_op jit(solution)/shard_map/pallas_call | solution.py:166
  (1 shorter events, 0.0 us)
Async XLA Ops:
  6.5 363.4 %all-gather.3.cloned.1.call-start = ((), (), s32[]{:S(2)}) async-start(), calls=%async_computation.2 | async-start | bytes 18874368 | tf_op jit(solution)/shard_map/all_gather | solution.py:196
  29.0 5.8 %copy-start = (f32[4096]{0:T(1024)S(1)}, f32[4096]{0:T(1024)}, u32[]{:S(2)}) copy-start(f32[4096]{0:T(1024)} %param.9) | copy-start | bytes 49156
  29.0 5.9 %copy-start.1 = (f32[4096]{0:T(1024)S(1)}, f32[4096]{0:T(1024)}, u32[]{:S(2)}) copy-start(f32[4096]{0:T(1024)} %param.8) | copy-start | bytes 49156
  29.0 104.6 %all-to-all-start = ((bf16[4,2,4096,128]{3,2,1,0:T(8,128)(2,1)}), bf16[4,2,4096,128]{3,2,1,0:T(8,128)(2,1)}, u32[]{:S(2)}, u32[]{:S(2)}) async-start(bf16[4,2,4096,128]{3,2,1,0:T(8,128)(2,1)} %bitcast.13), calls=%async_computation | async-start | bytes 16777216 | tf_op jit(solution)/shard_map/all_to_all | solution.py:205
Sparse Core Ops, SparseCore 0:
  9.0 153.7 all-gather.2

commit v2 on v0

v2 whole, which is shorter than its diff:
```python
import functools
import math

import jax
import jax.numpy as jnp
import numpy as np
from jax import lax
from jax.experimental import pallas as pl
from jax.experimental.pallas import tpu as pltpu
from jax.sharding import PartitionSpec as P

CHUNK = 16
SEND_CHUNKS = 2
DEPTH_CHUNKS = 2
VMEM_BYTES = 56 * 1024 * 1024


def unit_roots(rows, columns, modulus):
    product = np.outer(np.arange(rows), np.arange(columns)) % modulus
    angle = -2.0 * np.pi / modulus * product
    return np.cos(angle), np.sin(angle)


def split(value):
    high = value.astype(jnp.bfloat16)
    return high, (value - high.astype(jnp.float32)).astype(jnp.bfloat16)


def pack_kernel(raw_ref, out_ref):
    pixels = out_ref.shape[4]
    for h in range(out_ref.shape[0]):
        out_ref[h] = raw_ref[:, 0, :, :, h * pixels : (h + 1) * pixels]


def pack(raw, wave_count, chunk, width):
    _, row_count, k1_part, _, pix_local = raw.shape
    pieces = wave_count // row_count
    pixels = pix_local // pieces
    split_k1 = min(8, k1_part)
    return pl.pallas_call(
        pack_kernel,
        out_shape=jax.ShapeDtypeStruct((wave_count, 2, k1_part, width, pixels), raw.dtype),
        grid=(row_count, k1_part // split_k1),
        in_specs=[
            pl.BlockSpec((2, 1, split_k1, width, pix_local), lambda r, k: (0, r, k, chunk, 0))
        ],
        out_specs=pl.BlockSpec(
            (pieces, 2, split_k1, width, pixels), lambda r, k: (r, 0, k, 0, 0)
        ),
        compiler_params=pltpu.CompilerParams(vmem_limit_bytes=VMEM_BYTES),
        cost_estimate=pl.CostEstimate(
            flops=0,
            bytes_accessed=8 * row_count * k1_part * width * pix_local,
            transcendentals=0,
        ),
    )(raw)


def coarse_kernel(x_ref, phase_ref, small_ref, turn_ref, high_ref, low_ref, data, part):
    k1_count, pixels = data.shape[2], data.shape[3]
    for c in range(2):
        block = x_ref[:, c].reshape(k1_count, CHUNK, pixels).astype(jnp.float32)
        data[c] = jnp.swapaxes(block, 0, 1).astype(jnp.bfloat16)
    for i in range(CHUNK):
        turn_real = turn_ref[0, 0, :, i : i + 1]
        turn_imag = turn_ref[1, 0, :, i : i + 1]
        cosine = phase_ref[0, i : i + 1, :]
        sine = phase_ref[1, i : i + 1, :]
        background = phase_ref[2, i : i + 1, :]
        small_real = small_ref[0] * turn_real - small_ref[1] * turn_imag
        small_imag = small_ref[0] * turn_imag + small_ref[1] * turn_real
        real = small_real * cosine - small_imag * sine
        imag = small_real * sine + small_imag * cosine
        base_real = jnp.sum(real * background, axis=1, keepdims=True)
        base_imag = jnp.sum(imag * background, axis=1, keepdims=True)
        real_high, real_low = split(real)
        imag_high, imag_low = split(imag)
        matrix = jnp.concatenate((real_high, imag_high, real_low, imag_low), axis=0)
        columns = jnp.concatenate((data[0, i], data[1, i]), axis=1)
        both = jnp.dot(matrix, columns, preferred_element_type=jnp.float32)
        half = 2 * k1_count
        both = both[:half] + both[half:]
        by_real, by_imag = both[:k1_count], both[k1_count:]
        part[0, i] = by_real[:, :pixels] - by_imag[:, pixels:] - base_real
        part[1, i] = by_real[:, pixels:] + by_imag[:, :pixels] - base_imag
    for c in range(2):
        turned_high, turned_low = split(jnp.swapaxes(part[c], 0, 1))
        high_ref[c] = turned_high
        low_ref[c] = turned_low


def coarse_stage(blocks, phases, chunk):
    wave_count, _, k1_part, width, pixels = blocks.shape
    k1_count, k0_count = wave_count * k1_part, phases.shape[1]
    length = k1_count * k0_count
    steps = width // CHUNK
    small = np.stack(unit_roots(k1_count, k1_count, k1_count)).astype(np.float32)
    turn = np.stack(unit_roots(k1_count, k0_count, length)).astype(np.float32)
    turn = turn.reshape(2, k1_count, k0_count // CHUNK, CHUNK).transpose(0, 2, 1, 3)
    out_shape = jax.ShapeDtypeStruct((2, k1_count, width, pixels), jnp.bfloat16)
    out_spec = pl.BlockSpec((2, k1_count, CHUNK, pixels), lambda i: (0, 0, i, 0))
    return pl.pallas_call(
        coarse_kernel,
        out_shape=(out_shape, out_shape),
        grid=(steps,),
        in_specs=[
            pl.BlockSpec((wave_count, 2, k1_part, CHUNK, pixels), lambda i: (0, 0, 0, i, 0)),
            pl.BlockSpec((3, CHUNK, k1_count), lambda i: (0, chunk * steps + i, 0)),
            pl.BlockSpec(small.shape, lambda i: (0, 0, 0)),
            pl.BlockSpec((2, 1, k1_count, CHUNK), lambda i: (0, chunk * steps + i, 0, 0)),
        ],
        out_specs=(out_spec, out_spec),
        scratch_shapes=[
            pltpu.VMEM((2, CHUNK, k1_count, pixels), jnp.bfloat16),
            pltpu.VMEM((2, CHUNK, k1_count, pixels), jnp.float32),
        ],
        compiler_params=pltpu.CompilerParams(vmem_limit_bytes=VMEM_BYTES),
        cost_estimate=pl.CostEstimate(
            flops=16 * k1_count * k1_count * width * pixels * 2,
            bytes_accessed=12 * k1_count * width * pixels,
            transcendentals=0,
        ),
    )(blocks, phases, jnp.asarray(small), jnp.asarray(turn))


def fine_kernel(chunks, *refs):
    highs, lows = refs[:chunks], refs[chunks : 2 * chunks]
    fine_ref, out_ref, part = refs[2 * chunks :]
    pixels = out_ref.shape[4]

    def gathered(sources, i):
        return jnp.concatenate(
            [jnp.concatenate([ref[c, i] for ref in sources], axis=0) for c in range(2)], axis=1
        )

    for i in range(CHUNK):
        both = jnp.dot(fine_ref[...], gathered(highs, i), preferred_element_type=jnp.float32)
        half = both.shape[0] // 2
        both = (
            both[:half]
            + both[half:]
            + jnp.dot(fine_ref[:half], gathered(lows, i), preferred_element_type=jnp.float32)
        )
        by_real, by_imag = both[: half // 2], both[half // 2 :]
        part[0, i] = by_real[:, :pixels] - by_imag[:, pixels:]
        part[1, i] = by_real[:, pixels:] + by_imag[:, :pixels]
    for c in range(2):
        turned = jnp.swapaxes(part[c], 0, 1).astype(jnp.bfloat16)
        out_ref[:, c] = turned.reshape(out_ref.shape[:1] + out_ref.shape[2:])


def fine_stage(highs, lows, devices, chunk, width):
    _, z0_count, k0_part, pixels = highs[0].shape
    chunks = len(highs)
    k0_count = chunks * k0_part
    steps = width // CHUNK
    length = k0_count * z0_count
    fine = np.concatenate(unit_roots(k0_count, k0_count, k0_count), axis=0) / math.sqrt(length)
    fine_high = fine.astype(jnp.bfloat16)
    fine_low = (fine - fine_high.astype(np.float64)).astype(jnp.bfloat16)
    fine = np.concatenate((fine_high, fine_low), axis=0)
    out_shape = (devices, 2, k0_count // devices, width, pixels)
    in_spec = pl.BlockSpec(
        (2, CHUNK, k0_part, pixels), lambda i: (0, chunk * steps + i, 0, 0)
    )
    return pl.pallas_call(
        functools.partial(fine_kernel, chunks),
        out_shape=jax.ShapeDtypeStruct(out_shape, jnp.bfloat16),
        grid=(steps,),
        in_specs=[in_spec] * (2 * chunks) + [pl.BlockSpec(fine.shape, lambda i: (0, 0))],
        out_specs=pl.BlockSpec(out_shape[:3] + (CHUNK, pixels), lambda i: (0, 0, 0, i, 0)),
        scratch_shapes=[pltpu.VMEM((2, CHUNK, k0_count, pixels), jnp.float32)],
        compiler_params=pltpu.CompilerParams(vmem_limit_bytes=VMEM_BYTES),
        cost_estimate=pl.CostEstimate(
            flops=24 * k0_count * k0_count * width * pixels * 2,
            bytes_accessed=12 * k0_count * width * pixels,
            transcendentals=0,
        ),
    )(*highs, *lows, jnp.asarray(fine))


def refocus_kernel(row_count, pix_count, depth_ref, prop_ref, *rest):
    out_ref = rest[-1]
    senders, _, z1_part, width, pixels = depth_ref.shape
    pieces = senders // (row_count * pix_count)
    dot = functools.partial(jnp.dot, preferred_element_type=jnp.float32)
    for r in range(row_count):
        real, imag = [
            jnp.concatenate(
                [
                    depth_ref[(r * pieces + h) * pix_count + p, c].reshape(z1_part * width, pixels)
                    for p in range(pix_count)
                    for h in range(pieces)
                ],
                axis=1,
            )
            for c in range(2)
        ]
        shape = (z1_part, width, out_ref.shape[4])
        image_real = dot(real, prop_ref[0, 0]) - dot(imag, prop_ref[0, 1])
        out_ref[0, r] = image_real.reshape(shape)
        image_imag = dot(real, prop_ref[0, 1]) + dot(imag, prop_ref[0, 0])
        out_ref[1, r] = image_imag.reshape(shape)


def refocus(depth, propagator, row_count, chunk, chunks, image):
    pix_count, _, span, columns = propagator.shape
    _, _, z1_part, width, _ = depth.shape
    out_shape = (2, row_count, z1_part, width * chunks, pix_count * columns)
    earlier = () if image is None else (image,)
    return pl.pallas_call(
        functools.partial(refocus_kernel, row_count, pix_count),
        out_shape=jax.ShapeDtypeStruct(out_shape, jnp.float32),
        grid=(pix_count,),
        in_specs=[
            pl.BlockSpec(depth.shape, lambda q: (0,) * 5),
            pl.BlockSpec((1, 2, span, columns), lambda q: (q, 0, 0, 0)),
        ]
        + [pl.BlockSpec(memory_space=pl.ANY)] * len(earlier),
        out_specs=pl.BlockSpec(
            (2, row_count, z1_part, width, columns), lambda q: (0, 0, 0, chunk, q)
        ),
        input_output_aliases={2: 0} if earlier else {},
        compiler_params=pltpu.CompilerParams(vmem_limit_bytes=VMEM_BYTES),
        cost_estimate=pl.CostEstimate(
            flops=8 * row_count * z1_part * width * span * pix_count * columns,
            bytes_accessed=28 * 1024 * 1024,
            transcendentals=0,
        ),
    )(depth, propagator, *earlier)


def on_device(raw_spectra, background, dispersion, propagator):
    _, row_count, wave_span, pix_local = raw_spectra.shape
    wave_count = lax.axis_size("wave")
    pix_count = lax.axis_size("pix")
    devices = wave_count * pix_count
    k0_count = 128
    k1_part = wave_span // k0_count
    k1_count = k1_part * wave_count
    width = k0_count // SEND_CHUNKS
    depth_width = k1_count // DEPTH_CHUNKS

    columns = lax.all_gather(propagator, "pix", axis=0, tiled=False)
    phases = jnp.stack((jnp.cos(dispersion), jnp.sin(dispersion), background))
    phases = phases.reshape(1, 3, k1_part, k0_count)
    phases = jnp.broadcast_to(phases, (wave_count,) + phases.shape[1:])
    phases = lax.all_to_all(phases, "wave", split_axis=0, concat_axis=0, tiled=True)
    phases = jnp.transpose(phases, (1, 3, 0, 2)).reshape(3, k0_count, k1_count)

    raw = raw_spectra.reshape(2, row_count, k1_part, k0_count, pix_local)
    highs, lows = [], []
    for chunk in range(SEND_CHUNKS):
        blocks = pack(raw, wave_count, chunk, width)
        blocks = lax.all_to_all(blocks, "wave", split_axis=0, concat_axis=0, tiled=True)
        high, low = coarse_stage(blocks, phases, chunk)
        highs.append(high)
        lows.append(low)
    image = None
    for chunk in range(DEPTH_CHUNKS):
        depth = fine_stage(highs, lows, devices, chunk, depth_width)
        depth = lax.all_to_all(depth, ("wave", "pix"), split_axis=0, concat_axis=0, tiled=True)
        image = refocus(depth, columns, row_count, chunk, DEPTH_CHUNKS, image)
    return image.reshape(2, row_count, -1, image.shape[4])


def solution(mesh):
    in_specs = (P(None, None, "wave", "pix"), P("wave"), P("wave"), P(None, None, "pix"))
    out_specs = P(None, None, ("wave", "pix"), None)
    return jax.shard_map(
        on_device, mesh=mesh, in_specs=in_specs, out_specs=out_specs, check_vma=False
    )
```

time: 1540 us -> 382 us (0.25)
  waiting for transfers between devices: 719 us -> 228 us
  matrix products: 416 us -> 0 us
  blocking collectives: 191 us -> 0 us
  other arithmetic: 145 us -> 0.72 us
  Pallas kernels: 0 us -> 113 us
  local copies, waits for them, and re-layouts: 48.6 us -> 2.31 us
  starting transfers between devices: 4.68 us -> 23.7 us
    ppermute x2 -> x0, waiting for transfers between devices: 719 us -> none  [from_partner(): return lax.ppermute(value, axis, pairs)]
    dot_general x12 -> x0, matrix products: 416 us -> none  [the longest x1 72.2 us: local_transform(): jnp.einsum('xubp,bv->xuvp', mixed_terms[1], big_cos, precision=HIGHEST_PR...]
    all_to_all x0 -> x5, waiting for transfers between devices: none -> 227 us  [the longest x2 156 us: on_device(): lax.all_to_all(depth, ('wave', 'pix'), split_axis=0, concat_axis=0, tiled...]
    all_to_all x1 -> x0, blocking collectives: 191 us -> none  [on_device(): lax.all_to_all(merged, ('wave', 'pix'), split_axis=3, concat_axis=3, tile...]
    pallas_call x0 -> x8, Pallas kernels: none -> 113 us  [the longest x2 45.2 us: refocus(): pl.pallas_call(functools.partial(refocus_kernel, row_count, pix_count), o...]
    sub x5 -> x0, other arithmetic: 77.8 us -> none  [the longest x2 45.8 us: on_device(): partner - spectrum]
    select_n x2 -> x0, other arithmetic: 50.9 us -> none  [on_device(): spectrum = jnp.where(upper_half, turned, spectrum + partner)]
    all_to_all x0 -> x5, starting transfers between devices: none -> 23.7 us  [the longest x2 9.87 us: on_device(): lax.all_to_all(blocks, 'wave', split_axis=0, concat_axis=0, tiled=True)]
  transfers between devices with their start and end apart: 3 -> 6, of which waited for: 2 -> 4; matrix products, arithmetic and copies ran while one was open for 31% -> 1% of each run, Pallas kernels for 0% -> 24%
where the time goes in v2:
time: 382 us; the launch traced here: 381 us
  waiting for transfers between devices  228 us (60%)
  Pallas kernels  113 us (30%)
  starting transfers between devices  23.7 us (6%)
  between operations  13.4 us (4%)
    all_to_all x2, waiting for transfers between devices, on_device(): lax.all_to_all(depth, ('wave', 'pix'), split_axis=0, concat_axis=0, tiled...  156 us
    all_to_all x2, waiting for transfers between devices, on_device(): lax.all_to_all(blocks, 'wave', split_axis=0, concat_axis=0, tiled=True)  70.8 us
    pallas_call x2, Pallas kernels, refocus(): pl.pallas_call(functools.partial(refocus_kernel, row_count, pix_count), o...  45.2 us
    pallas_call x2, Pallas kernels, coarse_stage(): pl.pallas_call(coarse_kernel, out_shape=(out_shape, out_shape), grid=(ste...  32.1 us
    pallas_call x2, Pallas kernels, fine_stage(): pl.pallas_call(functools.partial(fine_kernel, chunks), out_shape=jax.Shap...  22.1 us
    pallas_call x2, Pallas kernels, pack(): pl.pallas_call(pack_kernel, out_shape=jax.ShapeDtypeStruct((wave_count, 2...  13.9 us
    all_to_all x2, starting transfers between devices, on_device(): lax.all_to_all(blocks, 'wave', split_axis=0, concat_axis=0, tiled=True)  9.87 us
    all_to_all x2, starting transfers between devices, on_device(): lax.all_to_all(depth, ('wave', 'pix'), split_axis=0, concat_axis=0, tiled...  8.64 us
  transfers between devices with their start and end apart: 6, of which 4 were waited for; matrix products, arithmetic and copies ran while one was open for 1% of the time, Pallas kernels for 24%

profile of v2, /device:TPU:0, one launch (start us, length us, event | category | flops | bytes accessed | tf_op | source)
XLA Modules:
  0.0 381.3 jit_solution(3830232578287026900)
XLA Ops:
  6.5 0.0 all-gather.3.cloned.1.call-start
  6.5 0.7 all-gather.3.cloned.1.call-update
  7.3 0.8 cosine_bitcast_fusion
  8.0 0.7 maximum_bitcast_fusion
  8.8 0.7 broadcast_in_dim.8
  9.5 5.2 %all-to-all-start.1 = ((f32[4,3,32,128]{3,2,1,0:T(8,128)}), f32[4,3,32,128]{3,2,1,0:T(8,128)S(1)}, u32[]{:S(2)}, u32[]{:S(2)}) async-start(f32[4,3,32,128]{3,2,1,0:T(8,128)} %broadcast_in_dim.8), calls=%async_computation.1 | async-start | bytes 393216 | tf_op jit(solution)/shard_map/all_to_all | solution.py:248
  14.6 7.0 %shard_map.100 = bf16[4,2,32,64,128]{4,3,2,1,0:T(8,128)(2,1)} custom-call(bf16[2,2,32,128,256]{4,3,2,1,0:T(8,128)(2,1)} %bitcast.13), custom_call_target="tpu_custom_call" | custom-call | bytes 8388608 | tf_op jit(solution)/shard_map/pallas_call | solution.py:40
  21.6 0.0 all-to-all-done.1
  21.6 4.9 %all-to-all-start = ((bf16[4,2,32,64,128]{4,3,2,1,0:T(8,128)(2,1)}), bf16[4,2,32,64,128]{4,3,2,1,0:T(8,128)(2,1)}, u32[]{:S(2)}, u32[]{:S(2)}) async-start(bf16[4,2,32,64,128]{4,3,2,1,0:T(8,128)(2,1)} %shard_map.100), calls=%async_computation | async-start | bytes 8388608 | tf_op jit(solution)/shard_map/all_to_all | solution.py:255
  26.6 6.9 %shard_map.102 = bf16[4,2,32,64,128]{4,3,2,1,0:T(8,128)(2,1)} custom-call(bf16[2,2,32,128,256]{4,3,2,1,0:T(8,128)(2,1)} %bitcast.14), custom_call_target="tpu_custom_call" | custom-call | bytes 8388608 | tf_op jit(solution)/shard_map/pallas_call | solution.py:40
  33.5 40.7 %all-to-all-done.x_ref = bf16[4,2,32,64,128]{4,3,2,1,0:T(8,128)(2,1)} async-done(((bf16[4,2,32,64,128]{4,3,2,1,0:T(8,128)(2,1)}), bf16[4,2,32,64,128]{4,3,2,1,0:T(8,128)(2,1)}, u32[]{:S(2)}, u32[]{:S(2)}) %all-to-all-start) | async-done | bytes 4194336 | tf_op jit(solution)/shard_map/all_to_all | solution.py:255
  74.2 4.9 %all-to-all-start.2 = ((bf16[4,2,32,64,128]{4,3,2,1,0:T(8,128)(2,1)}), bf16[4,2,32,64,128]{4,3,2,1,0:T(8,128)(2,1)}, u32[]{:S(2)}, u32[]{:S(2)}) async-start(bf16[4,2,32,64,128]{4,3,2,1,0:T(8,128)(2,1)} %shard_map.102), calls=%async_computation.2 | async-start | bytes 8388608 | tf_op jit(solution)/shard_map/all_to_all | solution.py:255
  79.2 0.8 copy.15.phase_ref
  80.0 16.0 %shard_map.101 = (bf16[2,128,64,128]{3,2,1,0:T(8,128)(2,1)}, bf16[2,128,64,128]{3,2,1,0:T(8,128)(2,1)}) custom-call(bf16[4,2,32,64,128]{4,3,2,1,0:T(8,128)(2,1)} %all-to-all-done.x_ref, f32[3,128,128]{2,1,0:T(8,128)} %copy.15.phase_ref, f32[2,128,128]{2,1,0:T(8,128)} %constant.6.clone.small_ref, f32[2,8,128,16]{3,2,1,0:T(8,128)} %constant.7.clone.turn_ref), custom_call_target="tpu_custom_call" | custom-call | flops 4294967296 | bytes 12582912 | tf_op jit(solution)/shard_map/pallas_call | solution.py:102
  96.0 30.1 %all-to-all-done.2.x_ref = bf16[4,2,32,64,128]{4,3,2,1,0:T(8,128)(2,1)} async-done(((bf16[4,2,32,64,128]{4,3,2,1,0:T(8,128)(2,1)}), bf16[4,2,32,64,128]{4,3,2,1,0:T(8,128)(2,1)}, u32[]{:S(2)}, u32[]{:S(2)}) %all-to-all-start.2) | async-done | bytes 4194336 | tf_op jit(solution)/shard_map/all_to_all | solution.py:255
  126.1 16.1 %shard_map.103 = (bf16[2,128,64,128]{3,2,1,0:T(8,128)(2,1)}, bf16[2,128,64,128]{3,2,1,0:T(8,128)(2,1)}) custom-call(bf16[4,2,32,64,128]{4,3,2,1,0:T(8,128)(2,1)} %all-to-all-done.2.x_ref, f32[3,128,128]{2,1,0:T(8,128)} %copy.15.phase_ref, f32[2,128,128]{2,1,0:T(8,128)} %constant.6.clone.small_ref, f32[2,8,128,16]{3,2,1,0:T(8,128)} %constant.7.clone.turn_ref), custom_call_target="tpu_custom_call" | custom-call | flops 4294967296 | bytes 12582912 | tf_op jit(solution)/shard_map/pallas_call | solution.py:102
  142.2 11.1 %shard_map.105 = bf16[32,2,4,64,128]{4,3,2,1,0:T(8,128)(2,1)} custom-call(bf16[2,128,64,128]{3,2,1,0:T(8,128)(2,1)} %get-tuple-element.9.refs_0_, bf16[2,128,64,128]{3,2,1,0:T(8,128)(2,1)} %get-tuple-element.10.refs_1_, bf16[2,128,64,128]{3,2,1,0:T(8,128)(2,1)} %get-tuple-element.11.refs_2_, bf16[2,128,64,128]{3,2,1,0:T(8,128)(2,1)} %get-tuple-element.12.refs_3_, ...), custom_call_target="tpu_custom_call" | custom-call | flops 6442450944 | bytes 12582912 | tf_op jit(solution)/shard_map/pallas_call | solution.py:166
  153.2 4.9 %all-to-all-start.4 = ((bf16[32,2,4,64,128]{4,3,2,1,0:T(8,128)(2,1)}), bf16[32,2,4,64,128]{4,3,2,1,0:T(8,128)(2,1)}, u32[]{:S(2)}, u32[]{:S(2)}) async-start(bf16[32,2,4,64,128]{4,3,2,1,0:T(8,128)(2,1)} %shard_map.105), calls=%async_computation.4 | async-start | bytes 8388608 | tf_op jit(solution)/shard_map/all_to_all | solution.py:262
  158.1 11.1 %shard_map.104 = bf16[32,2,4,64,128]{4,3,2,1,0:T(8,128)(2,1)} custom-call(bf16[2,128,64,128]{3,2,1,0:T(8,128)(2,1)} %get-tuple-element.9.refs_0_, bf16[2,128,64,128]{3,2,1,0:T(8,128)(2,1)} %get-tuple-element.10.refs_1_, bf16[2,128,64,128]{3,2,1,0:T(8,128)(2,1)} %get-tuple-element.11.refs_2_, bf16[2,128,64,128]{3,2,1,0:T(8,128)(2,1)} %get-tuple-element.12.refs_3_, ...), custom_call_target="tpu_custom_call" | custom-call | flops 6442450944 | bytes 12582912 | tf_op jit(solution)/shard_map/pallas_call | solution.py:166
  169.2 84.0 %all-to-all-done.4.depth_ref = bf16[32,2,4,64,128]{4,3,2,1,0:T(8,128)(2,1)} async-done(((bf16[32,2,4,64,128]{4,3,2,1,0:T(8,128)(2,1)}), bf16[32,2,4,64,128]{4,3,2,1,0:T(8,128)(2,1)}, u32[]{:S(2)}, u32[]{:S(2)}) %all-to-all-start.4) | async-done | bytes 4194336 | tf_op jit(solution)/shard_map/all_to_all | solution.py:262
  253.2 3.8 all-to-all-start.3
  256.9 0.0 all-gather.3.cloned.1.call-done
  257.0 22.6 %shard_map.106.rest_0_ = f32[2,2,4,128,2048]{4,3,2,1,0:T(8,128)} custom-call(bf16[32,2,4,64,128]{4,3,2,1,0:T(8,128)(2,1)} %all-to-all-done.4.depth_ref, bf16[8,2,2048,256]{3,2,1,0:T(8,128)(2,1)} %bitcast.17), custom_call_target="tpu_custom_call" | custom-call | flops 17179869184 | bytes 29360128 | tf_op jit(solution)/shard_map/pallas_call | solution.py:211
  279.6 72.3 %all-to-all-done.3.depth_ref = bf16[32,2,4,64,128]{4,3,2,1,0:T(8,128)(2,1)} async-done(((bf16[32,2,4,64,128]{4,3,2,1,0:T(8,128)(2,1)}), bf16[32,2,4,64,128]{4,3,2,1,0:T(8,128)(2,1)}, u32[]{:S(2)}, u32[]{:S(2)}) %all-to-all-start.3) | async-done | bytes 4194336 | tf_op jit(solution)/shard_map/all_to_all | solution.py:262
  351.8 22.6 %shard_map.107 = f32[2,2,4,128,2048]{4,3,2,1,0:T(8,128)} custom-call(bf16[32,2,4,64,128]{4,3,2,1,0:T(8,128)(2,1)} %all-to-all-done.3.depth_ref, bf16[8,2,2048,256]{3,2,1,0:T(8,128)(2,1)} %bitcast.18, f32[2,2,4,128,2048]{4,3,2,1,0:T(8,128)} %shard_map.106.rest_0_), custom_call_target="tpu_custom_call", output_to_operand_aliasing={{}: (2, {})} | custom-call | flops 17179869184 | bytes 29360128 | tf_op jit(solution)/shard_map/pallas_call | solution.py:211
  (1 shorter events, 0.0 us)
Async XLA Ops:
  6.5 250.4 %all-gather.3.cloned.1.call-start = ((), (), s32[]{:S(2)}) async-start(), calls=%async_computation.5 | async-start | bytes 18874368 | tf_op jit(solution)/shard_map/all_gather | solution.py:244
  9.5 12.2 %all-to-all-start.1 = ((f32[4,3,32,128]{3,2,1,0:T(8,128)}), f32[4,3,32,128]{3,2,1,0:T(8,128)S(1)}, u32[]{:S(2)}, u32[]{:S(2)}) async-start(f32[4,3,32,128]{3,2,1,0:T(8,128)} %broadcast_in_dim.8), calls=%async_computation.1 | async-start | bytes 393216 | tf_op jit(solution)/shard_map/all_to_all | solution.py:248
  21.6 52.6 %all-to-all-start = ((bf16[4,2,32,64,128]{4,3,2,1,0:T(8,128)(2,1)}), bf16[4,2,32,64,128]{4,3,2,1,0:T(8,128)(2,1)}, u32[]{:S(2)}, u32[]{:S(2)}) async-start(bf16[4,2,32,64,128]{4,3,2,1,0:T(8,128)(2,1)} %shard_map.100), calls=%async_computation | async-start | bytes 8388608 | tf_op jit(solution)/shard_map/all_to_all | solution.py:255
  74.2 51.9 %all-to-all-start.2 = ((bf16[4,2,32,64,128]{4,3,2,1,0:T(8,128)(2,1)}), bf16[4,2,32,64,128]{4,3,2,1,0:T(8,128)(2,1)}, u32[]{:S(2)}, u32[]{:S(2)}) async-start(bf16[4,2,32,64,128]{4,3,2,1,0:T(8,128)(2,1)} %shard_map.102), calls=%async_computation.2 | async-start | bytes 8388608 | tf_op jit(solution)/shard_map/all_to_all | solution.py:255
  153.2 99.9 %all-to-all-start.4 = ((bf16[32,2,4,64,128]{4,3,2,1,0:T(8,128)(2,1)}), bf16[32,2,4,64,128]{4,3,2,1,0:T(8,128)(2,1)}, u32[]{:S(2)}, u32[]{:S(2)}) async-start(bf16[32,2,4,64,128]{4,3,2,1,0:T(8,128)(2,1)} %shard_map.105), calls=%async_computation.4 | async-start | bytes 8388608 | tf_op jit(solution)/shard_map/all_to_all | solution.py:262
  253.2 98.7 %all-to-all-start.3 = ((bf16[32,2,4,64,128]{4,3,2,1,0:T(8,128)(2,1)}), bf16[32,2,4,64,128]{4,3,2,1,0:T(8,128)(2,1)}, u32[]{:S(2)}, u32[]{:S(2)}) async-start(bf16[32,2,4,64,128]{4,3,2,1,0:T(8,128)(2,1)} %shard_map.104), calls=%async_computation.3 | async-start | bytes 8388608 | tf_op jit(solution)/shard_map/all_to_all | solution.py:262
Sparse Core Ops, SparseCore 0:
  9.0 153.8 all-gather.2

commit v3 on v1

v3 whole, which is shorter than its diff:
```python
import functools
import math

import jax
import jax.numpy as jnp
import numpy as np
from jax import lax
from jax.experimental import pallas as pl
from jax.experimental.pallas import tpu as pltpu
from jax.sharding import PartitionSpec as P

CHUNK = 16
VMEM_BYTES = 56 * 1024 * 1024


def unit_roots(rows, columns, modulus):
    product = np.outer(np.arange(rows), np.arange(columns)) % modulus
    angle = -2.0 * np.pi / modulus * product
    return np.cos(angle), np.sin(angle)


def split(value):
    high = value.astype(jnp.bfloat16)
    return high, (value - high.astype(jnp.float32)).astype(jnp.bfloat16)


def swap_halves(value):
    half = value.shape[-1] // 2
    if 2 * half == 128:
        return pltpu.roll(value, half, value.ndim - 1)
    return jnp.concatenate((value[..., half:], value[..., :half]), axis=-1)


def left_half(shape):
    return lax.broadcasted_iota(jnp.int32, shape, len(shape) - 1) < shape[-1] // 2


def pack_kernel(me_ref, raw_ref, *out_refs):
    count = len(out_refs)
    pixels = out_refs[0].shape[2] // 2
    for d in range(count):
        lanes = slice(d * pixels, (d + 1) * pixels)
        piece = jnp.concatenate((raw_ref[0, 0, :, :, lanes], raw_ref[1, 0, :, :, lanes]), axis=2)
        for m in range(count):

            @pl.when((me_ref[0] ^ m) == d)
            def _():
                out_refs[m][...] = piece


def pack(me, raw, wave_count, row):
    _, _, k1_part, k0_count, pix_local = raw.shape
    lanes = 2 * pix_local // wave_count
    span = min(4, k1_part)
    return pl.pallas_call(
        pack_kernel,
        out_shape=[jax.ShapeDtypeStruct((k1_part, k0_count, lanes), raw.dtype)] * wave_count,
        grid=(k1_part // span,),
        in_specs=[
            pl.BlockSpec(memory_space=pltpu.SMEM),
            pl.BlockSpec((2, 1, span, k0_count, pix_local), lambda k: (0, row, k, 0, 0)),
        ],
        out_specs=[pl.BlockSpec((span, k0_count, lanes), lambda k: (k, 0, 0))] * wave_count,
        compiler_params=pltpu.CompilerParams(vmem_limit_bytes=VMEM_BYTES),
        cost_estimate=pl.CostEstimate(
            flops=0, bytes_accessed=8 * k1_part * k0_count * pix_local, transcendentals=0
        ),
    )(me, raw)


def transform_kernel(steps, me_ref, *refs):
    x_refs = refs[:-9]
    phase_ref, small_ref, turn_ref, fine_ref, out_ref, data, high, low, part = refs[-9:]
    step = pl.program_id(0)
    k1_count, lanes = data.shape[1], data.shape[2]
    k1_part = x_refs[0].shape[0]
    sign = jnp.where(left_half((1, lanes)), -1.0, 1.0)

    @pl.when(step < steps)
    def _():
        for m, x_ref in enumerate(x_refs):
            start = pl.multiple_of((me_ref[0] ^ m) * k1_part, k1_part)
            block = jnp.swapaxes(x_ref[...].astype(jnp.float32), 0, 1)
            data[:, pl.ds(start, k1_part), :] = block.astype(jnp.bfloat16)
        for i in range(CHUNK):
            turn_real = turn_ref[0, 0, :, i : i + 1]
            turn_imag = turn_ref[1, 0, :, i : i + 1]
            cosine = phase_ref[0, i : i + 1, :]
            sine = phase_ref[1, i : i + 1, :]
            background = phase_ref[2, i : i + 1, :]
            small_real = small_ref[0] * turn_real - small_ref[1] * turn_imag
            small_imag = small_ref[0] * turn_imag + small_ref[1] * turn_real
            real = small_real * cosine - small_imag * sine
            imag = small_real * sine + small_imag * cosine
            base_real = jnp.sum(real * background, axis=1, keepdims=True)
            base_imag = jnp.sum(imag * background, axis=1, keepdims=True)
            real_high, real_low = split(real)
            imag_high, imag_low = split(imag)
            matrix = jnp.concatenate((real_high, imag_high, real_low, imag_low), axis=0)
            both = jnp.dot(matrix, data[i], preferred_element_type=jnp.float32)
            half = both.shape[0] // 2
            both = both[:half] + both[half:]
            by_real, by_imag = both[: half // 2], both[half // 2 :]
            base = jnp.where(left_half(by_real.shape), base_real, base_imag)
            part[i] = by_real + sign * swap_halves(by_imag) - base
        at = pl.ds(pl.multiple_of(step * CHUNK, CHUNK), CHUNK)
        turned_high, turned_low = split(jnp.swapaxes(part[...], 0, 1))
        high[:, at, :] = turned_high
        low[:, at, :] = turned_low

    @pl.when(step >= steps)
    def _():
        first = (step - steps) * CHUNK
        for i in range(0, CHUNK, 2):
            at = first + i
            columns = jnp.concatenate((high[at], high[at + 1]), axis=1)
            rest = jnp.concatenate((low[at], low[at + 1]), axis=1)
            both = jnp.dot(fine_ref[...], columns, preferred_element_type=jnp.float32)
            half = both.shape[0] // 2
            both = (
                both[:half]
                + both[half:]
                + jnp.dot(fine_ref[:half], rest, preferred_element_type=jnp.float32)
            )
            by_real, by_imag = both[: half // 2], both[half // 2 :]
            for j in range(2):
                own = slice(j * lanes, (j + 1) * lanes)
                part[i + j] = by_real[:, own] + sign * swap_halves(by_imag[:, own])
        turned = jnp.swapaxes(part[...], 0, 1).astype(jnp.bfloat16)
        out_ref[...] = turned.reshape(out_ref.shape)


def depth_transform(me, pieces, phases, devices):
    wave_count = len(pieces)
    k1_part, k0_count, lanes = pieces[0].shape
    k1_count = wave_count * k1_part
    length = k1_count * k0_count
    steps = k0_count // CHUNK
    small = np.stack(unit_roots(k1_count, k1_count, k1_count)).astype(np.float32)
    turn = np.stack(unit_roots(k1_count, k0_count, length)).astype(np.float32)
    turn = turn.reshape(2, k1_count, steps, CHUNK).transpose(0, 2, 1, 3)
    fine = np.concatenate(unit_roots(k0_count, k0_count, k0_count), axis=0) / math.sqrt(length)
    fine_high = fine.astype(jnp.bfloat16)
    fine_low = (fine - fine_high.astype(np.float64)).astype(jnp.bfloat16)
    fine = np.concatenate((fine_high, fine_low), axis=0)
    out_shape = (devices, k0_count // devices, k1_count, lanes)
    return pl.pallas_call(
        functools.partial(transform_kernel, steps),
        out_shape=jax.ShapeDtypeStruct(out_shape, jnp.bfloat16),
        grid=(2 * steps,),
        in_specs=[pl.BlockSpec(memory_space=pltpu.SMEM)]
        + [
            pl.BlockSpec((k1_part, CHUNK, lanes), lambda i: (0, jnp.minimum(i, steps - 1), 0))
        ]
        * wave_count
        + [
            pl.BlockSpec((3, CHUNK, k1_count), lambda i: (0, jnp.minimum(i, steps - 1), 0)),
            pl.BlockSpec(small.shape, lambda i: (0, 0, 0)),
            pl.BlockSpec(
                (2, 1, k1_count, CHUNK), lambda i: (0, jnp.minimum(i, steps - 1), 0, 0)
            ),
            pl.BlockSpec(fine.shape, lambda i: (0, 0)),
        ],
        out_specs=pl.BlockSpec(
            out_shape[:2] + (CHUNK, lanes), lambda i: (0, 0, jnp.maximum(i - steps, 0), 0)
        ),
        scratch_shapes=[
            pltpu.VMEM((CHUNK, k1_count, lanes), jnp.bfloat16),
            pltpu.VMEM((k1_count, k0_count, lanes), jnp.bfloat16),
            pltpu.VMEM((k1_count, k0_count, lanes), jnp.bfloat16),
            pltpu.VMEM((CHUNK, k1_count, lanes), jnp.float32),
        ],
        compiler_params=pltpu.CompilerParams(vmem_limit_bytes=VMEM_BYTES),
        cost_estimate=pl.CostEstimate(
            flops=20 * 128 * length * lanes, bytes_accessed=4 * length * lanes, transcendentals=0
        ),
    )(me, *pieces, phases, jnp.asarray(small), jnp.asarray(turn), jnp.asarray(fine))


def refocus_kernel(depth_ref, prop_ref, *rest):
    out_ref, rows = rest[-2:]
    senders, depths, lanes = depth_ref.shape

    @pl.when(pl.program_id(0) == 0)
    def _():
        sign = jnp.where(left_half((1, lanes)), 1.0, -1.0)
        for sender in range(senders):
            own = slice(sender * lanes, (sender + 1) * lanes)
            value = depth_ref[sender].astype(jnp.float32)
            rows[:depths, own] = (value * sign).astype(jnp.bfloat16)
            rows[depths:, own] = swap_halves(value).astype(jnp.bfloat16)

    columns = prop_ref[...].reshape(senders * lanes, prop_ref.shape[3])
    for c in range(2):
        out_ref[c, 0] = jnp.dot(
            rows[c * depths : (c + 1) * depths], columns, preferred_element_type=jnp.float32
        )


def refocus(depth, propagator, row, row_count, image):
    wave_count, pix_count, span, columns = propagator.shape
    senders, depths, lanes = depth.shape
    earlier = () if image is None else (image,)
    return pl.pallas_call(
        refocus_kernel,
        out_shape=jax.ShapeDtypeStruct(
            (2, row_count, depths, pix_count * columns), jnp.float32
        ),
        grid=(pix_count,),
        in_specs=[
            pl.BlockSpec(depth.shape, lambda q: (0, 0, 0)),
            pl.BlockSpec((wave_count, 1, span, columns), lambda q: (0, q, 0, 0)),
        ]
        + [pl.BlockSpec(memory_space=pl.ANY)] * len(earlier),
        out_specs=pl.BlockSpec((2, 1, depths, columns), lambda q: (0, row, 0, q)),
        input_output_aliases={2: 0} if earlier else {},
        scratch_shapes=[pltpu.VMEM((2 * depths, senders * lanes), jnp.bfloat16)],
        compiler_params=pltpu.CompilerParams(vmem_limit_bytes=VMEM_BYTES),
        cost_estimate=pl.CostEstimate(
            flops=4 * depths * senders * lanes * pix_count * columns,
            bytes_accessed=28 * 1024 * 1024,
            transcendentals=0,
        ),
    )(depth, propagator, *earlier)


def on_device(raw_spectra, background, dispersion, propagator):
    _, row_count, wave_span, pix_local = raw_spectra.shape
    wave_count = lax.axis_size("wave")
    pix_count = lax.axis_size("pix")
    devices = wave_count * pix_count
    pixels = pix_local // wave_count
    k0_count = 128
    k1_part = wave_span // k0_count
    k1_count = k1_part * wave_count
    wave_pos = lax.axis_index("wave")
    me = wave_pos.astype(jnp.int32).reshape(1)

    columns = propagator.reshape(2, pix_count, wave_count, pixels, pix_local)
    columns = lax.dynamic_index_in_dim(columns, wave_pos, axis=2, keepdims=False)
    columns = jnp.swapaxes(columns, 0, 1).reshape(2 * pix_count * pixels, pix_local)
    columns = lax.all_gather(columns, ("wave", "pix"), axis=0, tiled=False)
    columns = columns.reshape(wave_count, pix_count, -1, pix_local)

    phases = jnp.stack((jnp.cos(dispersion), jnp.sin(dispersion), background))
    phases = phases.reshape(1, 3, k1_part, k0_count)
    phases = jnp.broadcast_to(phases, (wave_count,) + phases.shape[1:])
    phases = lax.all_to_all(phases, "wave", split_axis=0, concat_axis=0, tiled=True)
    phases = jnp.transpose(phases, (1, 3, 0, 2)).reshape(3, k0_count, k1_count)

    raw = raw_spectra.reshape(2, row_count, k1_part, k0_count, pix_local)
    image = None
    arrived = ()
    for row in range(row_count):
        pieces = pack(me, raw, wave_count, row)
        if row > 0:
            pieces, arrived = lax.optimization_barrier((pieces, arrived))
        arrived = [pieces[0]] + [
            lax.ppermute(pieces[m], "wave", [(s, s ^ m) for s in range(wave_count)])
            for m in range(1, wave_count)
        ]
        depth = depth_transform(me, arrived, phases, devices)
        depth = depth.reshape(devices, -1, 2 * pixels)
        depth = lax.all_to_all(depth, ("wave", "pix"), split_axis=0, concat_axis=0, tiled=True)
        image = refocus(depth, columns, row, row_count, image)
    return image


def solution(mesh):
    in_specs = (P(None, None, "wave", "pix"), P("wave"), P("wave"), P(None, None, "pix"))
    out_specs = P(None, None, ("wave", "pix"), None)
    return jax.shard_map(
        on_device, mesh=mesh, in_specs=in_specs, out_specs=out_specs, check_vma=False
    )
```

time: 419 us -> 429 us (1.024)
  blocking collectives: 288 us -> 66 us
  waiting for transfers between devices: 0.71 us -> 156 us
  Pallas kernels: 87.7 us -> 169 us
  local copies, waits for them, and re-layouts: 22.6 us -> 5.85 us
  starting transfers between devices: 5.8 us -> 17.7 us
    all_to_all x1, blocking collectives: 190 us -> 66 us  [on_device(): lax.all_to_all(phases, 'wave', split_axis=0, concat_axis=0, tiled=True)]
    all_gather x1 -> x0, blocking collectives: 97.9 us -> none  [on_device(): lax.all_gather(phases.reshape(3, k1_part, k0_count), 'wave', axis=1, tile...]
    ppermute x0 -> x6, waiting for transfers between devices: none -> 85.1 us  [on_device(): lax.ppermute(pieces[m], 'wave', [(s, s ^ m) for s in range(wave_count)])]
    all_to_all x1 -> x2, waiting for transfers between devices: 0.01 us -> 70.7 us  [on_device(): lax.all_to_all(depth, ('wave', 'pix'), split_axis=0, concat_axis=0, tiled...]
    pallas_call x1 -> x2, Pallas kernels: 46.3 us -> 104 us  [depth_transform(): pl.pallas_call(functools.partial(transform_kernel, steps), out_shape=jax....]
    pallas_call x1 -> x4, Pallas kernels: 41.4 us -> 65.2 us  [the longest x2 48.5 us: refocus(): pl.pallas_call(refocus_kernel, out_shape=jax.ShapeDtypeStruct((2, row_cou...]
    reshape x1, local copies, waits for them, and re-layouts: 12.6 us -> 0.82 us  [on_device(): phases = jnp.transpose(phases, (1, 3, 0, 2)).reshape(3, k0_count, k1_count)]
    transpose x1 -> x2, local copies, waits for them, and re-layouts: 9.14 us -> 0.92 us  [on_device(): jnp.swapaxes(columns, 0, 1).reshape(2 * pix_count * pixels, pix_local)]
  transfers between devices with their start and end apart: 2 -> 9, of which waited for: 0 -> 3; matrix products, arithmetic and copies ran while one was open for 5% -> 0% of each run, Pallas kernels for 11% -> 34%
where the time goes in v3:
time: 429 us; the launch traced here: 428 us
  Pallas kernels  169 us (39%)
  waiting for transfers between devices  156 us (36%)
  blocking collectives  66 us (15%)
  starting transfers between devices  17.7 us (4%)
  between operations  13.5 us (3%)
  local copies, waits for them, and re-layouts  5.85 us (1%)
    pallas_call x2, Pallas kernels, depth_transform(): pl.pallas_call(functools.partial(transform_kernel, steps), out_shape=jax....  104 us
    ppermute x6, waiting for transfers between devices, on_device(): lax.ppermute(pieces[m], 'wave', [(s, s ^ m) for s in range(wave_count)])  85.1 us
    all_to_all x2, waiting for transfers between devices, on_device(): lax.all_to_all(depth, ('wave', 'pix'), split_axis=0, concat_axis=0, tiled...  70.7 us
    all_to_all x1, blocking collectives, on_device(): lax.all_to_all(phases, 'wave', split_axis=0, concat_axis=0, tiled=True)  66 us
    pallas_call x2, Pallas kernels, refocus(): pl.pallas_call(refocus_kernel, out_shape=jax.ShapeDtypeStruct((2, row_cou...  48.5 us
    pallas_call x2, Pallas kernels, pack(): pl.pallas_call(pack_kernel, out_shape=[jax.ShapeDtypeStruct((k1_part, k0_...  16.8 us
    all_to_all x2, starting transfers between devices, on_device(): lax.all_to_all(depth, ('wave', 'pix'), split_axis=0, concat_axis=0, tiled...  9.72 us
  transfers between devices with their start and end apart: 9, of which 3 were waited for; matrix products, arithmetic and copies ran while one was open for 0% of the time, Pallas kernels for 34%

profile of v3, /device:TPU:0, one launch (start us, length us, event | category | flops | bytes accessed | tf_op | source)
XLA Modules:
  0.0 427.9 jit_solution(6913529002231323360)
XLA Ops:
  6.5 0.0 copy-start
  6.5 0.0 all-gather.2.cloned.1.call-start
  6.5 1.6 copy-done
  8.2 0.9 copy.19
  9.0 0.0 all-gather.2.cloned.1.call-update
  9.1 0.0 copy-start.2
  9.1 0.0 copy-start.3
  9.1 8.4 %shard_map.101 = (bf16[32,128,128]{2,1,0:T(8,128)(2,1)}, bf16[32,128,128]{2,1,0:T(8,128)(2,1)}, bf16[32,128,128]{2,1,0:T(8,128)(2,1)}, bf16[32,128,128]{2,1,0:T(8,128)(2,1)}) custom-call(s32[1]{0:T(128)} %bitcast.me_ref, bf16[2,2,32,128,256]{4,3,2,1,0:T(8,128)(2,1)} %bitcast.22), custom_call_target="tpu_custom_call" | custom-call | bytes 8388608 | tf_op jit(solution)/shard_map/pallas_call | solution.py:55
  17.5 2.9 collective-permute-start
  20.4 1.5 collective-permute-start.1
  21.9 0.0 collective-permute-start.2
  21.9 0.0 copy-done.2
  21.9 0.1 cosine_bitcast_fusion
  22.0 0.0 copy-done.3
  22.0 66.0 %all_to_all.15 = f32[4,3,32,128]{3,2,1,0:T(8,128)S(1)} all-to-all(f32[4,3,32,128]{3,2,1,0:T(8,128)S(1)} %broadcast_in_dim.8), channel_id=1, replica_groups=mesh['wave'=4,'pix'=8] {'wave'}, dimensions={0} | all-to-all | bytes 393216 | tf_op jit(solution)/shard_map/all_to_all | solution.py:248
  88.1 0.8 copy.18.refs_4_
  88.9 0.0 collective-permute-done.refs_1_
  88.9 0.0 copy-start.4
  88.9 0.0 collective-permute-done.1.refs_2_
  88.9 0.0 copy-start.5
  88.9 0.0 collective-permute-done.2.refs_3_
  88.9 1.0 copy-done.4
  89.9 0.4 copy-done.5
  90.3 51.9 %shard_map.103 = bf16[32,4,128,128]{3,2,1,0:T(8,128)(2,1)} custom-call(s32[1]{0:T(128)} %bitcast.me_ref, bf16[32,128,128]{2,1,0:T(8,128)(2,1)} %get-tuple-element.21.refs_0_, bf16[32,128,128]{2,1,0:T(8,128)(2,1)} %copy-done.4, bf16[32,128,128]{2,1,0:T(8,128)(2,1)} %copy-done.5, bf16[32,128,128]{2,1,0:T(8,128)(2,1)} %collective-permute-done.2.refs_3_, ...), custom_call_target="tpu_custom_call" | custom-call | flops 5368709120 | bytes 8388608 | tf_op jit(solution)/shard_map/pallas_call | solution.py:147
  142.2 5.2 %all-to-all-start.2 = ((bf16[32,512,128]{2,1,0:T(8,128)(2,1)}), bf16[32,512,128]{2,1,0:T(8,128)(2,1)}, u32[]{:S(2)}, u32[]{:S(2)}) async-start(bf16[32,512,128]{2,1,0:T(8,128)(2,1)} %bitcast.24), calls=%async_computation.2 | async-start | bytes 8388608 | tf_op jit(solution)/shard_map/all_to_all | solution.py:264
  147.4 8.4 %shard_map.100 = (bf16[32,128,128]{2,1,0:T(8,128)(2,1)}, bf16[32,128,128]{2,1,0:T(8,128)(2,1)}, bf16[32,128,128]{2,1,0:T(8,128)(2,1)}, bf16[32,128,128]{2,1,0:T(8,128)(2,1)}) custom-call(s32[1]{0:T(128)} %bitcast.me_ref, bf16[2,2,32,128,256]{4,3,2,1,0:T(8,128)(2,1)} %bitcast.23), custom_call_target="tpu_custom_call" | custom-call | bytes 8388608 | tf_op jit(solution)/shard_map/pallas_call | solution.py:55
  155.8 1.7 collective-permute-start.3
  157.5 1.5 collective-permute-start.4
  159.0 0.3 collective-permute-start.5
  159.3 52.6 %collective-permute-done.3.refs_1_ = bf16[32,128,128]{2,1,0:T(8,128)(2,1)S(1)} collective-permute-done((bf16[32,128,128]{2,1,0:T(8,128)(2,1)}, bf16[32,128,128]{2,1,0:T(8,128)(2,1)S(1)}, u32[]{:S(2)}, u32[]{:S(2)}) %collective-permute-start.3) | collective-permute-done | bytes 1048608 | tf_op jit(solution)/shard_map/ppermute | solution.py:259
  211.9 0.0 copy-start.6
  211.9 0.0 collective-permute-done.4.refs_2_
  211.9 0.0 copy-start.7
  211.9 32.5 %collective-permute-done.5.refs_3_ = bf16[32,128,128]{2,1,0:T(8,128)(2,1)S(1)} collective-permute-done((bf16[32,128,128]{2,1,0:T(8,128)(2,1)}, bf16[32,128,128]{2,1,0:T(8,128)(2,1)S(1)}, u32[]{:S(2)}, u32[]{:S(2)}) %collective-permute-start.5) | collective-permute-done | bytes 1048608 | tf_op jit(solution)/shard_map/ppermute | solution.py:259
  244.4 0.0 copy-done.6
  244.4 0.0 copy-done.7
  244.4 0.0 copy-start.8
  244.4 1.0 copy-done.8
  245.4 51.9 %shard_map.102 = bf16[32,4,128,128]{3,2,1,0:T(8,128)(2,1)} custom-call(s32[1]{0:T(128)} %bitcast.me_ref, bf16[32,128,128]{2,1,0:T(8,128)(2,1)} %get-tuple-element.25.refs_0_, bf16[32,128,128]{2,1,0:T(8,128)(2,1)} %copy-done.6, bf16[32,128,128]{2,1,0:T(8,128)(2,1)} %copy-done.7, bf16[32,128,128]{2,1,0:T(8,128)(2,1)} %copy-done.8, ...), custom_call_target="tpu_custom_call" | custom-call | flops 5368709120 | bytes 8388608 | tf_op jit(solution)/shard_map/pallas_call | solution.py:147
  297.4 0.0 all-to-all-done.2.depth_ref
  297.4 4.5 %all-to-all-start.1 = ((bf16[32,512,128]{2,1,0:T(8,128)(2,1)}), bf16[32,512,128]{2,1,0:T(8,128)(2,1)}, u32[]{:S(2)}, u32[]{:S(2)}) async-start(bf16[32,512,128]{2,1,0:T(8,128)(2,1)} %bitcast.25), calls=%async_computation.1 | async-start | bytes 8388608 | tf_op jit(solution)/shard_map/all_to_all | solution.py:264
  301.9 0.0 all-gather.2.cloned.1.call-done
  301.9 24.2 %shard_map.104.rest_0_ = f32[2,2,512,2048]{3,2,1,0:T(8,128)} custom-call(bf16[32,512,128]{2,1,0:T(8,128)(2,1)} %all-to-all-done.2.depth_ref, bf16[4,8,1024,256]{3,2,1,0:T(8,128)(2,1)} %bitcast.29), custom_call_target="tpu_custom_call" | custom-call | flops 17179869184 | bytes 29360128 | tf_op jit(solution)/shard_map/pallas_call | solution.py:204
  326.1 70.7 %all-to-all-done.1.depth_ref = bf16[32,512,128]{2,1,0:T(8,128)(2,1)} async-done(((bf16[32,512,128]{2,1,0:T(8,128)(2,1)}), bf16[32,512,128]{2,1,0:T(8,128)(2,1)}, u32[]{:S(2)}, u32[]{:S(2)}) %all-to-all-start.1) | async-done | bytes 4194336 | tf_op jit(solution)/shard_map/all_to_all | solution.py:264
  396.8 0.0 copy-start.1
  396.8 24.3 %shard_map.105 = f32[2,2,512,2048]{3,2,1,0:T(8,128)} custom-call(bf16[32,512,128]{2,1,0:T(8,128)(2,1)} %all-to-all-done.1.depth_ref, bf16[4,8,1024,256]{3,2,1,0:T(8,128)(2,1)} %bitcast.30, f32[2,2,512,2048]{3,2,1,0:T(8,128)} %shard_map.104.rest_0_), custom_call_target="tpu_custom_call", output_to_operand_aliasing={{}: (2, {})} | custom-call | flops 17179869184 | bytes 29360128 | tf_op jit(solution)/shard_map/pallas_call | solution.py:204
  421.0 0.0 copy-done.1
  (4 shorter events, 0.1 us)
Async XLA Ops:
  6.5 1.6 copy-start
  6.5 295.4 %all-gather.2.cloned.1.call-start = ((), (), s32[]{:S(2)}) async-start(), calls=%async_computation.3 | async-start | bytes 17301504 | tf_op jit(solution)/shard_map/all_gather | solution.py:242
  9.1 12.9 %copy-start.2 = (f32[4096]{0:T(1024)S(1)}, f32[4096]{0:T(1024)}, u32[]{:S(2)}) copy-start(f32[4096]{0:T(1024)} %param.12) | copy-start | bytes 49156
  9.1 12.9 %copy-start.3 = (f32[4096]{0:T(1024)S(1)}, f32[4096]{0:T(1024)}, u32[]{:S(2)}) copy-start(f32[4096]{0:T(1024)} %param.11) | copy-start | bytes 49156
  17.5 71.4 %collective-permute-start = (bf16[32,128,128]{2,1,0:T(8,128)(2,1)}, bf16[32,128,128]{2,1,0:T(8,128)(2,1)S(1)}, u32[]{:S(2)}, u32[]{:S(2)}) collective-permute-start(bf16[32,128,128]{2,1,0:T(8,128)(2,1)} %get-tuple-element.22), channel_id=1, source_target_pairs={{0,8},{8,0},{16,24},{24,16},{1,9},{9,1},{17,25},{25,17},{2,10},{10... | collective-permute-start | bytes 3145736 | tf_op jit(solution)/shard_map/ppermute | solution.py:259
  20.4 68.5 %collective-permute-start.1 = (bf16[32,128,128]{2,1,0:T(8,128)(2,1)}, bf16[32,128,128]{2,1,0:T(8,128)(2,1)S(1)}, u32[]{:S(2)}, u32[]{:S(2)}) collective-permute-start(bf16[32,128,128]{2,1,0:T(8,128)(2,1)} %get-tuple-element.23), channel_id=1, source_target_pairs={{0,16},{8,24},{16,0},{24,8},{1,17},{9,25},{17,1},{25,9},{2,18},{10... | collective-permute-start | bytes 3145736 | tf_op jit(solution)/shard_map/ppermute | solution.py:259
  21.9 67.0 %collective-permute-start.2 = (bf16[32,128,128]{2,1,0:T(8,128)(2,1)}, bf16[32,128,128]{2,1,0:T(8,128)(2,1)}, u32[]{:S(2)}, u32[]{:S(2)}) collective-permute-start(bf16[32,128,128]{2,1,0:T(8,128)(2,1)} %get-tuple-element.24), channel_id=1, source_target_pairs={{0,24},{8,16},{16,8},{24,0},{1,25},{9,17},{17,9},{25,1},{2,26},{10... | collective-permute-start | bytes 3145736 | tf_op jit(solution)/shard_map/ppermute | solution.py:259
  88.9 1.0 copy-start.4
  88.9 1.4 copy-start.5
  142.2 155.1 %all-to-all-start.2 = ((bf16[32,512,128]{2,1,0:T(8,128)(2,1)}), bf16[32,512,128]{2,1,0:T(8,128)(2,1)}, u32[]{:S(2)}, u32[]{:S(2)}) async-start(bf16[32,512,128]{2,1,0:T(8,128)(2,1)} %bitcast.24), calls=%async_computation.2 | async-start | bytes 8388608 | tf_op jit(solution)/shard_map/all_to_all | solution.py:264
  155.8 56.0 %collective-permute-start.3 = (bf16[32,128,128]{2,1,0:T(8,128)(2,1)}, bf16[32,128,128]{2,1,0:T(8,128)(2,1)S(1)}, u32[]{:S(2)}, u32[]{:S(2)}) collective-permute-start(bf16[32,128,128]{2,1,0:T(8,128)(2,1)} %get-tuple-element.26), channel_id=1, source_target_pairs={{0,8},{8,0},{16,24},{24,16},{1,9},{9,1},{17,25},{25,17},{2,10},{10... | collective-permute-start | bytes 3145736 | tf_op jit(solution)/shard_map/ppermute | solution.py:259
  157.5 54.4 %collective-permute-start.4 = (bf16[32,128,128]{2,1,0:T(8,128)(2,1)}, bf16[32,128,128]{2,1,0:T(8,128)(2,1)S(1)}, u32[]{:S(2)}, u32[]{:S(2)}) collective-permute-start(bf16[32,128,128]{2,1,0:T(8,128)(2,1)} %get-tuple-element.27), channel_id=1, source_target_pairs={{0,16},{8,24},{16,0},{24,8},{1,17},{9,25},{17,1},{25,9},{2,18},{10... | collective-permute-start | bytes 3145736 | tf_op jit(solution)/shard_map/ppermute | solution.py:259
  159.0 85.4 %collective-permute-start.5 = (bf16[32,128,128]{2,1,0:T(8,128)(2,1)}, bf16[32,128,128]{2,1,0:T(8,128)(2,1)S(1)}, u32[]{:S(2)}, u32[]{:S(2)}) collective-permute-start(bf16[32,128,128]{2,1,0:T(8,128)(2,1)} %get-tuple-element.28), channel_id=1, source_target_pairs={{0,24},{8,16},{16,8},{24,0},{1,25},{9,17},{17,9},{25,1},{2,26},{10... | collective-permute-start | bytes 3145736 | tf_op jit(solution)/shard_map/ppermute | solution.py:259
  211.9 32.5 %copy-start.6 = (bf16[32,128,128]{2,1,0:T(8,128)(2,1)}, bf16[32,128,128]{2,1,0:T(8,128)(2,1)S(1)}, u32[]{:S(2)}) copy-start(bf16[32,128,128]{2,1,0:T(8,128)(2,1)S(1)} %collective-permute-done.3.refs_1_) | copy-start | bytes 3145732
  211.9 32.5 %copy-start.7 = (bf16[32,128,128]{2,1,0:T(8,128)(2,1)}, bf16[32,128,128]{2,1,0:T(8,128)(2,1)S(1)}, u32[]{:S(2)}) copy-start(bf16[32,128,128]{2,1,0:T(8,128)(2,1)S(1)} %collective-permute-done.4.refs_2_) | copy-start | bytes 3145732
  244.4 1.0 copy-start.8
  297.4 99.4 %all-to-all-start.1 = ((bf16[32,512,128]{2,1,0:T(8,128)(2,1)}), bf16[32,512,128]{2,1,0:T(8,128)(2,1)}, u32[]{:S(2)}, u32[]{:S(2)}) async-start(bf16[32,512,128]{2,1,0:T(8,128)(2,1)} %bitcast.25), calls=%async_computation.1 | async-start | bytes 8388608 | tf_op jit(solution)/shard_map/all_to_all | solution.py:264
  396.8 24.3 %copy-start.1 = (bf16[2,2048,256]{2,1,0:T(8,128)(2,1)S(1)}, bf16[2,2048,256]{2,1,0:T(8,128)(2,1)}, u32[]{:S(2)}) copy-start(bf16[2,2048,256]{2,1,0:T(8,128)(2,1)} %param.13) | copy-start | bytes 6291460
Sparse Core Ops, SparseCore 0:
  10.4 135.7 all-gather.1

commit v4 on v3

--- a/solution.py
+++ b/solution.py
@@ -38,14 +38,14 @@
 def pack_kernel(me_ref, raw_ref, *out_refs):
     count = len(out_refs)
     pixels = out_refs[0].shape[2] // 2
-    for d in range(count):
-        lanes = slice(d * pixels, (d + 1) * pixels)
-        piece = jnp.concatenate((raw_ref[0, 0, :, :, lanes], raw_ref[1, 0, :, :, lanes]), axis=2)
-        for m in range(count):
-
-            @pl.when((me_ref[0] ^ m) == d)
-            def _():
-                out_refs[m][...] = piece
+    for me in range(count):
+
+        @pl.when(me_ref[0] == me)
+        def _():
+            for m in range(count):
+                lanes = slice((me ^ m) * pixels, (me ^ m) * pixels + pixels)
+                parts = (raw_ref[0, 0, :, :, lanes], raw_ref[1, 0, :, :, lanes])
+                out_refs[m][...] = jnp.concatenate(parts, axis=2)
 
 
 def pack(me, raw, wave_count, row):
@@ -68,11 +68,65 @@
     )(me, raw)
 
 
+def matrix_kernel(phase_ref, small_ref, turn_ref, matrix_ref, base_ref):
+    bases = []
+    for i in range(CHUNK):
+        turn_real = turn_ref[0, 0, :, i : i + 1]
+        turn_imag = turn_ref[1, 0, :, i : i + 1]
+        cosine = phase_ref[0, i : i + 1, :]
+        sine = phase_ref[1, i : i + 1, :]
+        background = phase_ref[2, i : i + 1, :]
+        small_real = small_ref[0] * turn_real - small_ref[1] * turn_imag
+        small_imag = small_ref[0] * turn_imag + small_ref[1] * turn_real
+        real = small_real * cosine - small_imag * sine
+        imag = small_real * sine + small_imag * cosine
+        bases.append([jnp.sum(v * background, axis=1, keepdims=True) for v in (real, imag)])
+        real_high, real_low = split(real)
+        imag_high, imag_low = split(imag)
+        count = real.shape[0]
+        matrix_ref[i, :count] = jnp.concatenate((real_high, imag_high), axis=1)
+        matrix_ref[i, count:] = jnp.concatenate((real_low, imag_low), axis=1)
+    for c in range(2):
+        base_ref[c, 0] = jnp.concatenate([base[c] for base in bases], axis=1)
+
+
+def stage_matrices(phases):
+    _, k0_count, k1_count = phases.shape
+    length = k1_count * k0_count
+    steps = k0_count // CHUNK
+    small = np.stack(unit_roots(k1_count, k1_count, k1_count)).astype(np.float32)
+    turn = np.stack(unit_roots(k1_count, k0_count, length)).astype(np.float32)
+    turn = turn.reshape(2, k1_count, steps, CHUNK).transpose(0, 2, 1, 3)
+    column_spec = pl.BlockSpec((2, 1, k1_count, CHUNK), lambda i: (0, i, 0, 0))
+    return pl.pallas_call(
+        matrix_kernel,
+        out_shape=(
+            jax.ShapeDtypeStruct((k0_count, 2 * k1_count, 2 * k1_count), jnp.bfloat16),
+            jax.ShapeDtypeStruct((2, steps, k1_count, CHUNK), jnp.float32),
+        ),
+        grid=(steps,),
+        in_specs=[
+            pl.BlockSpec((3, CHUNK, k1_count), lambda i: (0, i, 0)),
+            pl.BlockSpec(small.shape, lambda i: (0, 0, 0)),
+            column_spec,
+        ],
+        out_specs=(
+            pl.BlockSpec((CHUNK, 2 * k1_count, 2 * k1_count), lambda i: (i, 0, 0)),
+            column_spec,
+        ),
+        compiler_params=pltpu.CompilerParams(vmem_limit_bytes=VMEM_BYTES),
+        cost_estimate=pl.CostEstimate(
+            flops=20 * length * k1_count, bytes_accessed=8 * length * k1_count, transcendentals=0
+        ),
+    )(phases, jnp.asarray(small), jnp.asarray(turn))
+
+
 def transform_kernel(steps, me_ref, *refs):
-    x_refs = refs[:-9]
-    phase_ref, small_ref, turn_ref, fine_ref, out_ref, data, high, low, part = refs[-9:]
+    x_refs = refs[:-7]
+    matrix_ref, base_ref, fine_ref, out_ref, data, middle, part = refs[-7:]
     step = pl.program_id(0)
-    k1_count, lanes = data.shape[1], data.shape[2]
+    k1_count, lanes = data.shape[1] // 2, data.shape[2]
+    k0_count = middle.shape[1] // 2
     k1_part = x_refs[0].shape[0]
     sign = jnp.where(left_half((1, lanes)), -1.0, 1.0)
 
@@ -82,46 +136,30 @@
             start = pl.multiple_of((me_ref[0] ^ m) * k1_part, k1_part)
             block = jnp.swapaxes(x_ref[...].astype(jnp.float32), 0, 1)
             data[:, pl.ds(start, k1_part), :] = block.astype(jnp.bfloat16)
+            other = swap_halves(block) * sign
+            data[:, pl.ds(k1_count + start, k1_part), :] = other.astype(jnp.bfloat16)
         for i in range(CHUNK):
-            turn_real = turn_ref[0, 0, :, i : i + 1]
-            turn_imag = turn_ref[1, 0, :, i : i + 1]
-            cosine = phase_ref[0, i : i + 1, :]
-            sine = phase_ref[1, i : i + 1, :]
-            background = phase_ref[2, i : i + 1, :]
-            small_real = small_ref[0] * turn_real - small_ref[1] * turn_imag
-            small_imag = small_ref[0] * turn_imag + small_ref[1] * turn_real
-            real = small_real * cosine - small_imag * sine
-            imag = small_real * sine + small_imag * cosine
-            base_real = jnp.sum(real * background, axis=1, keepdims=True)
-            base_imag = jnp.sum(imag * background, axis=1, keepdims=True)
-            real_high, real_low = split(real)
-            imag_high, imag_low = split(imag)
-            matrix = jnp.concatenate((real_high, imag_high, real_low, imag_low), axis=0)
-            both = jnp.dot(matrix, data[i], preferred_element_type=jnp.float32)
-            half = both.shape[0] // 2
-            both = both[:half] + both[half:]
-            by_real, by_imag = both[: half // 2], both[half // 2 :]
-            base = jnp.where(left_half(by_real.shape), base_real, base_imag)
-            part[i] = by_real + sign * swap_halves(by_imag) - base
-        at = pl.ds(pl.multiple_of(step * CHUNK, CHUNK), CHUNK)
+            both = jnp.dot(matrix_ref[i], data[i], preferred_element_type=jnp.float32)
+            base = jnp.where(
+                left_half((k1_count, lanes)),
+                base_ref[0, 0, :, i : i + 1],
+                base_ref[1, 0, :, i : i + 1],
+            )
+            part[i] = both[:k1_count] + both[k1_count:] - base
+        at = pl.multiple_of(step * CHUNK, CHUNK)
         turned_high, turned_low = split(jnp.swapaxes(part[...], 0, 1))
-        high[:, at, :] = turned_high
-        low[:, at, :] = turned_low
+        middle[:, pl.ds(at, CHUNK), :] = turned_high
+        middle[:, pl.ds(k0_count + at, CHUNK), :] = turned_low
 
     @pl.when(step >= steps)
     def _():
         first = (step - steps) * CHUNK
         for i in range(0, CHUNK, 2):
             at = first + i
-            columns = jnp.concatenate((high[at], high[at + 1]), axis=1)
-            rest = jnp.concatenate((low[at], low[at + 1]), axis=1)
+            columns = jnp.concatenate((middle[at], middle[at + 1]), axis=1)
             both = jnp.dot(fine_ref[...], columns, preferred_element_type=jnp.float32)
             half = both.shape[0] // 2
-            both = (
-                both[:half]
-                + both[half:]
-                + jnp.dot(fine_ref[:half], rest, preferred_element_type=jnp.float32)
-            )
+            both = both[:half] + both[half:]
             by_real, by_imag = both[: half // 2], both[half // 2 :]
             for j in range(2):
                 own = slice(j * lanes, (j + 1) * lanes)
@@ -130,19 +168,17 @@
         out_ref[...] = turned.reshape(out_ref.shape)
 
 
-def depth_transform(me, pieces, phases, devices):
+def depth_transform(me, pieces, matrices, base, devices):
     wave_count = len(pieces)
     k1_part, k0_count, lanes = pieces[0].shape
     k1_count = wave_count * k1_part
     length = k1_count * k0_count
     steps = k0_count // CHUNK
-    small = np.stack(unit_roots(k1_count, k1_count, k1_count)).astype(np.float32)
-    turn = np.stack(unit_roots(k1_count, k0_count, length)).astype(np.float32)
-    turn = turn.reshape(2, k1_count, steps, CHUNK).transpose(0, 2, 1, 3)
     fine = np.concatenate(unit_roots(k0_count, k0_count, k0_count), axis=0) / math.sqrt(length)
     fine_high = fine.astype(jnp.bfloat16)
     fine_low = (fine - fine_high.astype(np.float64)).astype(jnp.bfloat16)
     fine = np.concatenate((fine_high, fine_low), axis=0)
+    fine = np.concatenate((fine, fine), axis=1)
     out_shape = (devices, k0_count // devices, k1_count, lanes)
     return pl.pallas_call(
         functools.partial(transform_kernel, steps),
@@ -154,8 +190,9 @@
         ]
         * wave_count
         + [
-            pl.BlockSpec((3, CHUNK, k1_count), lambda i: (0, jnp.minimum(i, steps - 1), 0)),
-            pl.BlockSpec(small.shape, lambda i: (0, 0, 0)),
+            pl.BlockSpec(
+                (CHUNK, 2 * k1_count, 2 * k1_count), lambda i: (jnp.minimum(i, steps - 1), 0, 0)
+            ),
             pl.BlockSpec(
                 (2, 1, k1_count, CHUNK), lambda i: (0, jnp.minimum(i, steps - 1), 0, 0)
             ),
@@ -165,16 +202,15 @@
             out_shape[:2] + (CHUNK, lanes), lambda i: (0, 0, jnp.maximum(i - steps, 0), 0)
         ),
         scratch_shapes=[
-            pltpu.VMEM((CHUNK, k1_count, lanes), jnp.bfloat16),
-            pltpu.VMEM((k1_count, k0_count, lanes), jnp.bfloat16),
-            pltpu.VMEM((k1_count, k0_count, lanes), jnp.bfloat16),
+            pltpu.VMEM((CHUNK, 2 * k1_count, lanes), jnp.bfloat16),
+            pltpu.VMEM((k1_count, 2 * k0_count, lanes), jnp.bfloat16),
             pltpu.VMEM((CHUNK, k1_count, lanes), jnp.float32),
         ],
         compiler_params=pltpu.CompilerParams(vmem_limit_bytes=VMEM_BYTES),
         cost_estimate=pl.CostEstimate(
-            flops=20 * 128 * length * lanes, bytes_accessed=4 * length * lanes, transcendentals=0
-        ),
-    )(me, *pieces, phases, jnp.asarray(small), jnp.asarray(turn), jnp.asarray(fine))
+            flops=20 * 128 * length * lanes, bytes_accessed=12 * length * lanes, transcendentals=0
+        ),
+    )(me, *pieces, matrices, base, jnp.asarray(fine))
 
 
 def refocus_kernel(depth_ref, prop_ref, *rest):
@@ -239,8 +275,8 @@
     columns = propagator.reshape(2, pix_count, wave_count, pixels, pix_local)
     columns = lax.dynamic_index_in_dim(columns, wave_pos, axis=2, keepdims=False)
     columns = jnp.swapaxes(columns, 0, 1).reshape(2 * pix_count * pixels, pix_local)
-    columns = lax.all_gather(columns, ("wave", "pix"), axis=0, tiled=False)
-    columns = columns.reshape(wave_count, pix_count, -1, pix_local)
+    columns = lax.all_gather(columns, "pix", axis=0, tiled=False)
+    columns = lax.all_gather(columns, "wave", axis=0, tiled=False)
 
     phases = jnp.stack((jnp.cos(dispersion), jnp.sin(dispersion), background))
     phases = phases.reshape(1, 3, k1_part, k0_count)
@@ -249,17 +285,18 @@
     phases = jnp.transpose(phases, (1, 3, 0, 2)).reshape(3, k0_count, k1_count)
 
     raw = raw_spectra.reshape(2, row_count, k1_part, k0_count, pix_local)
+    packed = [pack(me, raw, wave_count, row) for row in range(row_count)]
+    packed[0], phases = lax.optimization_barrier((packed[0], phases))
+    matrices, base = stage_matrices(phases)
     image = None
-    arrived = ()
     for row in range(row_count):
-        pieces = pack(me, raw, wave_count, row)
-        if row > 0:
-            pieces, arrived = lax.optimization_barrier((pieces, arrived))
-        arrived = [pieces[0]] + [
-            lax.ppermute(pieces[m], "wave", [(s, s ^ m) for s in range(wave_count)])
+        arrived = [packed[row][0]] + [
+            lax.ppermute(packed[row][m], "wave", [(s, s ^ m) for s in range(wave_count)])
             for m in range(1, wave_count)
         ]
-        depth = depth_transform(me, arrived, phases, devices)
+        if row + 1 < row_count:
+            arrived, packed[row + 1] = lax.optimization_barrier((arrived, packed[row + 1]))
+        depth = depth_transform(me, arrived, matrices, base, devices)
         depth = depth.reshape(devices, -1, 2 * pixels)
         depth = lax.all_to_all(depth, ("wave", "pix"), split_axis=0, concat_axis=0, tiled=True)
         image = refocus(depth, columns, row, row_count, image)

time: 429 us -> 499 us (1.16)
  waiting for transfers between devices: 156 us -> 326 us
  blocking collectives: 66 us -> 0 us
  Pallas kernels: 169 us -> 133 us
    ppermute x6, waiting for transfers between devices: 85.1 us -> 206 us  [on_device(): lax.ppermute(packed[row][m], 'wave', [(s, s ^ m) for s in range(wave_coun...]
    all_to_all x1 -> x0, blocking collectives: 66 us -> none  [on_device(): lax.all_to_all(phases, 'wave', split_axis=0, concat_axis=0, tiled=True)]
    pallas_call x2, Pallas kernels: 104 us -> 47.5 us  [depth_transform(): pl.pallas_call(functools.partial(transform_kernel, steps), out_shape=jax....]
    all_gather x1 -> x2, waiting for transfers between devices: 0.02 us -> 50 us  [the longest x1 50 us: on_device(): columns = lax.all_gather(columns, 'pix', axis=0, tiled=False)]
    pallas_call x0 -> x1, Pallas kernels: none -> 22.1 us  [stage_matrices(): pl.pallas_call(matrix_kernel, out_shape=(jax.ShapeDtypeStruct((k0_count,...]
  transfers between devices with their start and end apart: 9 -> 11, of which waited for: 3 -> 7; matrix products, arithmetic and copies ran while one was open for 0% -> 0% of each run, Pallas kernels for 34% -> 22%
where the time goes in v4:
time: 499 us; the launch traced here: 498 us
  waiting for transfers between devices  326 us (65%)
  Pallas kernels  133 us (27%)
  starting transfers between devices  18.9 us (4%)
  between operations  13.5 us (3%)
  local copies, waits for them, and re-layouts  6.03 us (1%)
    ppermute x6, waiting for transfers between devices, on_device(): lax.ppermute(packed[row][m], 'wave', [(s, s ^ m) for s in range(wave_coun...  206 us
    all_to_all x2, waiting for transfers between devices, on_device(): lax.all_to_all(depth, ('wave', 'pix'), split_axis=0, concat_axis=0, tiled...  70.7 us
    all_gather x1, waiting for transfers between devices, on_device(): columns = lax.all_gather(columns, 'pix', axis=0, tiled=False)  50 us
    pallas_call x2, Pallas kernels, refocus(): pl.pallas_call(refocus_kernel, out_shape=jax.ShapeDtypeStruct((2, row_cou...  48.5 us
    pallas_call x2, Pallas kernels, depth_transform(): pl.pallas_call(functools.partial(transform_kernel, steps), out_shape=jax....  47.5 us
    pallas_call x1, Pallas kernels, stage_matrices(): pl.pallas_call(matrix_kernel, out_shape=(jax.ShapeDtypeStruct((k0_count,...  22.1 us
    pallas_call x2, Pallas kernels, pack(): pl.pallas_call(pack_kernel, out_shape=[jax.ShapeDtypeStruct((k1_part, k0_...  15.3 us
  transfers between devices with their start and end apart: 11, of which 7 were waited for; matrix products, arithmetic and copies ran while one was open for 0% of the time, Pallas kernels for 22%

profile of v4, /device:TPU:0, one launch (start us, length us, event | category | flops | bytes accessed | tf_op | source)
XLA Modules:
  0.0 498.1 jit_solution(15408896288538825969)
XLA Ops:
  6.5 0.0 copy-start
  6.5 0.0 copy-start.8
  6.5 0.0 copy-start.9
  6.5 0.0 all-gather.4.cloned.1.call-start
  6.6 1.6 copy-done
  8.2 0.8 copy.15
  9.0 0.0 all-gather.4.cloned.1.call-update
  9.0 0.0 all-gather.6.cloned.1.call-start
  9.1 50.0 %all-gather.4.cloned.1.call-done = bf16[8,1024,256]{2,1,0:T(8,128)(2,1)} async-done(((bf16[1,1024,256]{2,1,0:T(8,128)(2,1)}), bf16[8,1024,256]{2,1,0:T(8,128)(2,1)}) %all-gather.4.cloned.1.call-update) | async-done | bytes 4194320 | tf_op jit(solution)/shard_map/all_gather | solution.py:278
  59.0 0.0 all-gather.6.cloned.1.call-update
  59.0 0.0 copy-done.8
  59.1 0.1 cosine_bitcast_fusion
  59.1 0.0 copy-done.9
  59.2 0.7 broadcast_in_dim.8
  59.9 3.6 all-to-all-start
  63.5 7.7 %shard_map.82 = (bf16[32,128,128]{2,1,0:T(8,128)(2,1)}, bf16[32,128,128]{2,1,0:T(8,128)(2,1)}, bf16[32,128,128]{2,1,0:T(8,128)(2,1)}, bf16[32,128,128]{2,1,0:T(8,128)(2,1)}) custom-call(s32[1]{0:T(128)} %bitcast.me_ref, bf16[2,2,32,128,256]{4,3,2,1,0:T(8,128)(2,1)} %bitcast.22), custom_call_target="tpu_custom_call" | custom-call | bytes 8388608 | tf_op jit(solution)/shard_map/pallas_call | solution.py:55
  71.2 0.0 all-to-all-done
  71.2 2.1 collective-permute-start
  73.3 1.4 collective-permute-start.1
  74.7 0.1 collective-permute-start.2
  74.8 7.6 %shard_map.83 = (bf16[32,128,128]{2,1,0:T(8,128)(2,1)}, bf16[32,128,128]{2,1,0:T(8,128)(2,1)}, bf16[32,128,128]{2,1,0:T(8,128)(2,1)}, bf16[32,128,128]{2,1,0:T(8,128)(2,1)}) custom-call(s32[1]{0:T(128)} %bitcast.me_ref, bf16[2,2,32,128,256]{4,3,2,1,0:T(8,128)(2,1)} %bitcast.23), custom_call_target="tpu_custom_call" | custom-call | bytes 8388608 | tf_op jit(solution)/shard_map/pallas_call | solution.py:55
  82.4 0.8 copy.14.phase_ref
  83.2 22.1 %shard_map.84 = (bf16[128,256,256]{2,1,0:T(8,128)(2,1)}, f32[2,8,128,16]{3,2,1,0:T(8,128)}) custom-call(f32[3,128,128]{2,1,0:T(8,128)} %copy.14.phase_ref, f32[2,128,128]{2,1,0:T(8,128)} %constant.17.clone.small_ref, f32[2,8,128,16]{3,2,1,0:T(8,128)} %constant.18.clone.turn_ref), custom_call_target="tpu_custom_call" | custom-call | flops 41943040 | bytes 16777216 | tf_op jit(solution)/shard_map/pallas_call | solution.py:101
  105.3 14.4 %collective-permute-done.refs_1_ = bf16[32,128,128]{2,1,0:T(8,128)(2,1)S(1)} collective-permute-done((bf16[32,128,128]{2,1,0:T(8,128)(2,1)}, bf16[32,128,128]{2,1,0:T(8,128)(2,1)S(1)}, u32[]{:S(2)}, u32[]{:S(2)}) %collective-permute-start) | collective-permute-done | bytes 1048608 | tf_op jit(solution)/shard_map/ppermute | solution.py:294
  119.6 0.0 copy-start.2
  119.6 2.7 collective-permute-done.1.refs_2_
  122.4 0.0 copy-start.3
  122.4 42.2 %collective-permute-done.2.refs_3_ = bf16[32,128,128]{2,1,0:T(8,128)(2,1)S(1)} collective-permute-done((bf16[32,128,128]{2,1,0:T(8,128)(2,1)}, bf16[32,128,128]{2,1,0:T(8,128)(2,1)S(1)}, u32[]{:S(2)}, u32[]{:S(2)}) %collective-permute-start.2) | collective-permute-done | bytes 1048608 | tf_op jit(solution)/shard_map/ppermute | solution.py:294
  164.6 0.0 copy-start.4
  164.6 0.0 copy-done.2
  164.6 0.0 copy-done.3
  164.6 1.0 copy-done.4
  165.6 24.3 %shard_map.86 = bf16[32,4,128,128]{3,2,1,0:T(8,128)(2,1)} custom-call(s32[1]{0:T(128)} %bitcast.me_ref, bf16[32,128,128]{2,1,0:T(8,128)(2,1)} %get-tuple-element.47.refs_0_, bf16[32,128,128]{2,1,0:T(8,128)(2,1)} %copy-done.2, bf16[32,128,128]{2,1,0:T(8,128)(2,1)} %copy-done.3, bf16[32,128,128]{2,1,0:T(8,128)(2,1)} %copy-done.4, ...), custom_call_target="tpu_custom_call" | custom-call | flops 5368709120 | bytes 25165824 | tf_op jit(solution)/shard_map/pallas_call | solution.py:183
  189.9 0.0 copy-start.12
  189.9 0.0 copy-start.11
  189.9 0.0 copy-start.10
  189.9 3.9 all-to-all-start.2
  193.8 0.0 copy-done.12
  193.8 1.6 collective-permute-start.3
  195.4 0.0 copy-done.11
  195.4 1.5 collective-permute-start.4
  196.9 0.0 copy-done.10
  196.9 0.4 collective-permute-start.5
  197.4 100.6 %collective-permute-done.3.refs_1_ = bf16[32,128,128]{2,1,0:T(8,128)(2,1)S(1)} collective-permute-done((bf16[32,128,128]{2,1,0:T(8,128)(2,1)S(1)}, bf16[32,128,128]{2,1,0:T(8,128)(2,1)S(1)}, u32[]{:S(2)}, u32[]{:S(2)}) %collective-permute-start.3) | collective-permute-done | bytes 1048608 | tf_op jit(solution)/shard_map/ppermute | solution.py:294
  298.0 0.0 copy-start.5
  298.0 0.0 collective-permute-done.4.refs_2_
  298.0 0.0 copy-start.6
  298.0 45.7 %collective-permute-done.5.refs_3_ = bf16[32,128,128]{2,1,0:T(8,128)(2,1)S(1)} collective-permute-done((bf16[32,128,128]{2,1,0:T(8,128)(2,1)S(1)}, bf16[32,128,128]{2,1,0:T(8,128)(2,1)S(1)}, u32[]{:S(2)}, u32[]{:S(2)}) %collective-permute-start.5) | collective-permute-done | bytes 1048608 | tf_op jit(solution)/shard_map/ppermute | solution.py:294
  343.7 0.0 copy-done.5
  343.7 0.0 copy-done.6
  343.7 0.0 copy-start.7
  343.7 1.0 copy-done.7
  344.7 23.2 %shard_map.85 = bf16[32,4,128,128]{3,2,1,0:T(8,128)(2,1)} custom-call(s32[1]{0:T(128)} %bitcast.me_ref, bf16[32,128,128]{2,1,0:T(8,128)(2,1)} %get-tuple-element.40.refs_0_, bf16[32,128,128]{2,1,0:T(8,128)(2,1)} %copy-done.5, bf16[32,128,128]{2,1,0:T(8,128)(2,1)} %copy-done.6, bf16[32,128,128]{2,1,0:T(8,128)(2,1)} %copy-done.7, ...), custom_call_target="tpu_custom_call" | custom-call | flops 5368709120 | bytes 25165824 | tf_op jit(solution)/shard_map/pallas_call | solution.py:183
  367.9 0.0 all-to-all-done.2.depth_ref
  367.9 4.2 all-to-all-start.1
  372.1 0.0 all-gather.6.cloned.1.call-done
  372.1 24.2 %shard_map.87.rest_0_ = f32[2,2,512,2048]{3,2,1,0:T(8,128)} custom-call(bf16[32,512,128]{2,1,0:T(8,128)(2,1)} %all-to-all-done.2.depth_ref, bf16[4,8,1024,256]{3,2,1,0:T(8,128)(2,1)} %bitcast.29), custom_call_target="tpu_custom_call" | custom-call | flops 17179869184 | bytes 29360128 | tf_op jit(solution)/shard_map/pallas_call | solution.py:240
  396.3 70.7 %all-to-all-done.1.depth_ref = bf16[32,512,128]{2,1,0:T(8,128)(2,1)} async-done(((bf16[32,512,128]{2,1,0:T(8,128)(2,1)}), bf16[32,512,128]{2,1,0:T(8,128)(2,1)}, u32[]{:S(2)}, u32[]{:S(2)}) %all-to-all-start.1) | async-done | bytes 4194336 | tf_op jit(solution)/shard_map/all_to_all | solution.py:301
  467.0 0.0 copy-start.1
  467.0 24.3 %shard_map.88 = f32[2,2,512,2048]{3,2,1,0:T(8,128)} custom-call(bf16[32,512,128]{2,1,0:T(8,128)(2,1)} %all-to-all-done.1.depth_ref, bf16[4,8,1024,256]{3,2,1,0:T(8,128)(2,1)} %bitcast.30, f32[2,2,512,2048]{3,2,1,0:T(8,128)} %shard_map.87.rest_0_), custom_call_target="tpu_custom_call", output_to_operand_aliasing={{}: (2, {})} | custom-call | flops 17179869184 | bytes 29360128 | tf_op jit(solution)/shard_map/pallas_call | solution.py:240
  491.3 0.0 copy-done.1
  (3 shorter events, 0.1 us)
Async XLA Ops:
  6.5 1.6 copy-start
  6.5 52.5 %copy-start.8 = (f32[4096]{0:T(1024)S(1)}, f32[4096]{0:T(1024)}, u32[]{:S(2)}) copy-start(f32[4096]{0:T(1024)} %param.10) | copy-start | bytes 49156
  6.5 52.6 %copy-start.9 = (f32[4096]{0:T(1024)S(1)}, f32[4096]{0:T(1024)}, u32[]{:S(2)}) copy-start(f32[4096]{0:T(1024)} %param.9) | copy-start | bytes 49156
  6.5 52.5 %all-gather.4.cloned.1.call-start = ((), (), s32[]{:S(2)}) async-start(), calls=%async_computation.3 | async-start | bytes 4718592 | tf_op jit(solution)/shard_map/all_gather | solution.py:278
  9.0 363.1 %all-gather.6.cloned.1.call-start = ((), (), s32[]{:S(2)}) async-start(), calls=%async_computation.4 | async-start | bytes 20971520 | tf_op jit(solution)/shard_map/all_gather | solution.py:279
  59.9 11.4 %all-to-all-start = ((f32[4,3,32,128]{3,2,1,0:T(8,128)}), f32[4,3,32,128]{3,2,1,0:T(8,128)S(1)}, u32[]{:S(2)}, u32[]{:S(2)}) async-start(f32[4,3,32,128]{3,2,1,0:T(8,128)} %broadcast_in_dim.8), calls=%async_computation | async-start | bytes 393216 | tf_op jit(solution)/shard_map/all_to_all | solution.py:284
  71.2 48.4 %collective-permute-start = (bf16[32,128,128]{2,1,0:T(8,128)(2,1)}, bf16[32,128,128]{2,1,0:T(8,128)(2,1)S(1)}, u32[]{:S(2)}, u32[]{:S(2)}) collective-permute-start(bf16[32,128,128]{2,1,0:T(8,128)(2,1)} %get-tuple-element.33), channel_id=1, source_target_pairs={{0,8},{8,0},{16,24},{24,16},{1,9},{9,1},{17,25},{25,17},{2,10},{10... | collective-permute-start | bytes 3145736 | tf_op jit(solution)/shard_map/ppermute | solution.py:294
  73.3 49.1 %collective-permute-start.1 = (bf16[32,128,128]{2,1,0:T(8,128)(2,1)}, bf16[32,128,128]{2,1,0:T(8,128)(2,1)S(1)}, u32[]{:S(2)}, u32[]{:S(2)}) collective-permute-start(bf16[32,128,128]{2,1,0:T(8,128)(2,1)} %get-tuple-element.34), channel_id=1, source_target_pairs={{0,16},{8,24},{16,0},{24,8},{1,17},{9,25},{17,1},{25,9},{2,18},{10... | collective-permute-start | bytes 3145736 | tf_op jit(solution)/shard_map/ppermute | solution.py:294
  74.7 89.9 %collective-permute-start.2 = (bf16[32,128,128]{2,1,0:T(8,128)(2,1)}, bf16[32,128,128]{2,1,0:T(8,128)(2,1)S(1)}, u32[]{:S(2)}, u32[]{:S(2)}) collective-permute-start(bf16[32,128,128]{2,1,0:T(8,128)(2,1)} %get-tuple-element.35), channel_id=1, source_target_pairs={{0,24},{8,16},{16,8},{24,0},{1,25},{9,17},{17,9},{25,1},{2,26},{10... | collective-permute-start | bytes 3145736 | tf_op jit(solution)/shard_map/ppermute | solution.py:294
  119.6 45.0 %copy-start.2 = (bf16[32,128,128]{2,1,0:T(8,128)(2,1)}, bf16[32,128,128]{2,1,0:T(8,128)(2,1)S(1)}, u32[]{:S(2)}) copy-start(bf16[32,128,128]{2,1,0:T(8,128)(2,1)S(1)} %collective-permute-done.refs_1_) | copy-start | bytes 3145732
  122.4 42.2 %copy-start.3 = (bf16[32,128,128]{2,1,0:T(8,128)(2,1)}, bf16[32,128,128]{2,1,0:T(8,128)(2,1)S(1)}, u32[]{:S(2)}) copy-start(bf16[32,128,128]{2,1,0:T(8,128)(2,1)S(1)} %collective-permute-done.1.refs_2_) | copy-start | bytes 3145732
  164.6 1.0 copy-start.4
  189.9 3.9 copy-start.12
  189.9 5.5 %copy-start.11 = (bf16[32,128,128]{2,1,0:T(8,128)(2,1)S(1)}, bf16[32,128,128]{2,1,0:T(8,128)(2,1)}, u32[]{:S(2)}) copy-start(bf16[32,128,128]{2,1,0:T(8,128)(2,1)} %get-tuple-element.42) | copy-start | bytes 3145732
  189.9 7.0 %copy-start.10 = (bf16[32,128,128]{2,1,0:T(8,128)(2,1)S(1)}, bf16[32,128,128]{2,1,0:T(8,128)(2,1)}, u32[]{:S(2)}) copy-start(bf16[32,128,128]{2,1,0:T(8,128)(2,1)} %get-tuple-element.43) | copy-start | bytes 3145732
  189.9 178.0 %all-to-all-start.2 = ((bf16[32,512,128]{2,1,0:T(8,128)(2,1)}), bf16[32,512,128]{2,1,0:T(8,128)(2,1)}, u32[]{:S(2)}, u32[]{:S(2)}) async-start(bf16[32,512,128]{2,1,0:T(8,128)(2,1)} %bitcast.24), calls=%async_computation.2 | async-start | bytes 8388608 | tf_op jit(solution)/shard_map/all_to_all | solution.py:301
  193.8 104.2 %collective-permute-start.3 = (bf16[32,128,128]{2,1,0:T(8,128)(2,1)S(1)}, bf16[32,128,128]{2,1,0:T(8,128)(2,1)S(1)}, u32[]{:S(2)}, u32[]{:S(2)}) collective-permute-start(bf16[32,128,128]{2,1,0:T(8,128)(2,1)S(1)} %copy-done.12), channel_id=1, source_target_pairs={{0,8},{8,0},{16,24},{24,16},{1,9},{9,1},{17,25},{25,17},{2,10},{10... | collective-permute-start | bytes 3145736 | tf_op jit(solution)/shard_map/ppermute | solution.py:294
  195.4 102.6 %collective-permute-start.4 = (bf16[32,128,128]{2,1,0:T(8,128)(2,1)S(1)}, bf16[32,128,128]{2,1,0:T(8,128)(2,1)S(1)}, u32[]{:S(2)}, u32[]{:S(2)}) collective-permute-start(bf16[32,128,128]{2,1,0:T(8,128)(2,1)S(1)} %copy-done.11), channel_id=1, source_target_pairs={{0,16},{8,24},{16,0},{24,8},{1,17},{9,25},{17,1},{25,9},{2,18},{10... | collective-permute-start | bytes 3145736 | tf_op jit(solution)/shard_map/ppermute | solution.py:294
  196.9 146.8 %collective-permute-start.5 = (bf16[32,128,128]{2,1,0:T(8,128)(2,1)S(1)}, bf16[32,128,128]{2,1,0:T(8,128)(2,1)S(1)}, u32[]{:S(2)}, u32[]{:S(2)}) collective-permute-start(bf16[32,128,128]{2,1,0:T(8,128)(2,1)S(1)} %copy-done.10), channel_id=1, source_target_pairs={{0,24},{8,16},{16,8},{24,0},{1,25},{9,17},{17,9},{25,1},{2,26},{10... | collective-permute-start | bytes 3145736 | tf_op jit(solution)/shard_map/ppermute | solution.py:294
  298.0 45.7 %copy-start.5 = (bf16[32,128,128]{2,1,0:T(8,128)(2,1)}, bf16[32,128,128]{2,1,0:T(8,128)(2,1)S(1)}, u32[]{:S(2)}) copy-start(bf16[32,128,128]{2,1,0:T(8,128)(2,1)S(1)} %collective-permute-done.3.refs_1_) | copy-start | bytes 3145732
  298.0 45.7 %copy-start.6 = (bf16[32,128,128]{2,1,0:T(8,128)(2,1)}, bf16[32,128,128]{2,1,0:T(8,128)(2,1)S(1)}, u32[]{:S(2)}) copy-start(bf16[32,128,128]{2,1,0:T(8,128)(2,1)S(1)} %collective-permute-done.4.refs_2_) | copy-start | bytes 3145732
  343.7 1.0 copy-start.7
  367.9 99.1 %all-to-all-start.1 = ((bf16[32,512,128]{2,1,0:T(8,128)(2,1)}), bf16[32,512,128]{2,1,0:T(8,128)(2,1)}, u32[]{:S(2)}, u32[]{:S(2)}) async-start(bf16[32,512,128]{2,1,0:T(8,128)(2,1)} %bitcast.25), calls=%async_computation.1 | async-start | bytes 8388608 | tf_op jit(solution)/shard_map/all_to_all | solution.py:301
  467.0 24.3 %copy-start.1 = (bf16[2,2048,256]{2,1,0:T(8,128)(2,1)S(1)}, bf16[2,2048,256]{2,1,0:T(8,128)(2,1)}, u32[]{:S(2)}) copy-start(bf16[2,2048,256]{2,1,0:T(8,128)(2,1)} %param.11) | copy-start | bytes 6291460
Sparse Core Ops, SparseCore 0:
  9.1 49.8 all-gather.3
  60.9 289.8 all-gather.5

commit v5 on v4

--- a/solution.py
+++ b/solution.py
@@ -213,43 +213,68 @@
     )(me, *pieces, matrices, base, jnp.asarray(fine))
 
 
-def refocus_kernel(depth_ref, prop_ref, *rest):
-    out_ref, rows = rest[-2:]
-    senders, depths, lanes = depth_ref.shape
+def even_mask(mask):
+    return bin(mask).count("1") % 2 == 0
+
+
+def refocus_kernel(wave_count, pix_count, me_ref, depth_ref, *refs):
+    prop_refs = refs[: 2 * wave_count]
+    out_ref, rows = refs[-2:]
+    _, depths, lanes = depth_ref.shape
+    half = pix_count // 2
+    core = me_ref[1]
 
     @pl.when(pl.program_id(0) == 0)
     def _():
         sign = jnp.where(left_half((1, lanes)), 1.0, -1.0)
-        for sender in range(senders):
-            own = slice(sender * lanes, (sender + 1) * lanes)
-            value = depth_ref[sender].astype(jnp.float32)
-            rows[:depths, own] = (value * sign).astype(jnp.bfloat16)
-            rows[depths:, own] = swap_halves(value).astype(jnp.bfloat16)
-
-    columns = prop_ref[...].reshape(senders * lanes, prop_ref.shape[3])
+        for m in range(wave_count):
+            first = (me_ref[0] ^ m) * pix_count
+            for h in range(2):
+                start = first + (h if even_mask(m) else core ^ h) * half
+                for p in range(half):
+                    at = (m * pix_count + h * half + p) * lanes
+                    own = slice(at, at + lanes)
+                    value = depth_ref[start + p].astype(jnp.float32)
+                    rows[:depths, own] = (value * sign).astype(jnp.bfloat16)
+                    rows[depths:, own] = swap_halves(value).astype(jnp.bfloat16)
+
+    columns = jnp.concatenate([ref[0] for ref in prop_refs], axis=0)
     for c in range(2):
         out_ref[c, 0] = jnp.dot(
             rows[c * depths : (c + 1) * depths], columns, preferred_element_type=jnp.float32
         )
 
 
-def refocus(depth, propagator, row, row_count, image):
-    wave_count, pix_count, span, columns = propagator.shape
+def refocus(me, depth, slices, row, row_count, image):
+    wave_count = len(slices)
     senders, depths, lanes = depth.shape
+    pix_count = senders // wave_count
+    span = pix_count // 2 * lanes
+    columns = slices[0][0].shape[2]
+    operands, specs = [], []
+    for mask in range(wave_count):
+        for h in range(2):
+            if even_mask(mask):
+                operands.append(slices[mask][0])
+                specs.append(pl.BlockSpec((1, span, columns), lambda q, h=h: (q, h, 0)))
+            else:
+                operands.append(slices[mask][h])
+                specs.append(pl.BlockSpec((1, span, columns), lambda q: (q, 0, 0)))
     earlier = () if image is None else (image,)
     return pl.pallas_call(
-        refocus_kernel,
+        functools.partial(refocus_kernel, wave_count, pix_count),
         out_shape=jax.ShapeDtypeStruct(
             (2, row_count, depths, pix_count * columns), jnp.float32
         ),
         grid=(pix_count,),
         in_specs=[
+            pl.BlockSpec(memory_space=pltpu.SMEM),
             pl.BlockSpec(depth.shape, lambda q: (0, 0, 0)),
-            pl.BlockSpec((wave_count, 1, span, columns), lambda q: (0, q, 0, 0)),
         ]
+        + specs
         + [pl.BlockSpec(memory_space=pl.ANY)] * len(earlier),
         out_specs=pl.BlockSpec((2, 1, depths, columns), lambda q: (0, row, 0, q)),
-        input_output_aliases={2: 0} if earlier else {},
+        input_output_aliases={2 + len(operands): 0} if earlier else {},
         scratch_shapes=[pltpu.VMEM((2 * depths, senders * lanes), jnp.bfloat16)],
         compiler_params=pltpu.CompilerParams(vmem_limit_bytes=VMEM_BYTES),
         cost_estimate=pl.CostEstimate(
@@ -257,7 +282,35 @@
             bytes_accessed=28 * 1024 * 1024,
             transcendentals=0,
         ),
-    )(depth, propagator, *earlier)
+    )(me, depth, *operands, *earlier)
+
+
+def gather_slices(propagator, wave_pos, wave_count):
+    _, span, pix_local = propagator.shape
+    pix_count = lax.axis_size("pix")
+    rows = propagator.reshape(2, pix_count, wave_count, -1, pix_local)
+    slices = {}
+    for mask in range(wave_count):
+        if even_mask(mask):
+            own = lax.dynamic_index_in_dim(rows, wave_pos ^ mask, axis=2, keepdims=False)
+            own = jnp.swapaxes(own, 0, 1).reshape(2 * span // wave_count, pix_local)
+            slices[mask] = [lax.all_gather(own, "pix", axis=0, tiled=False)]
+    return slices
+
+
+def exchange_slices(slices, wave_count, core):
+    pix_count = lax.axis_size("pix")
+    result = dict(slices)
+    for mask in range(wave_count):
+        if not even_mask(mask):
+            bit = mask & -mask
+            source = slices[mask ^ bit][0]
+            half = source.shape[1] // 2
+            own = lax.dynamic_slice_in_dim(source, core * half, half, axis=1)
+            own = lax.ppermute(own, "wave", [(s, s ^ bit) for s in range(wave_count)])
+            mate = lax.ppermute(own, "pix", [(s, s ^ 1) for s in range(pix_count)])
+            result[mask] = [own, mate]
+    return result
 
 
 def on_device(raw_spectra, background, dispersion, propagator):
@@ -270,13 +323,9 @@
     k1_part = wave_span // k0_count
     k1_count = k1_part * wave_count
     wave_pos = lax.axis_index("wave")
-    me = wave_pos.astype(jnp.int32).reshape(1)
-
-    columns = propagator.reshape(2, pix_count, wave_count, pixels, pix_local)
-    columns = lax.dynamic_index_in_dim(columns, wave_pos, axis=2, keepdims=False)
-    columns = jnp.swapaxes(columns, 0, 1).reshape(2 * pix_count * pixels, pix_local)
-    columns = lax.all_gather(columns, "pix", axis=0, tiled=False)
-    columns = lax.all_gather(columns, "wave", axis=0, tiled=False)
+    core = lax.axis_index("pix") % 2
+    me = jnp.stack((wave_pos, core)).astype(jnp.int32)
+    slices = gather_slices(propagator, wave_pos, wave_count)
 
     phases = jnp.stack((jnp.cos(dispersion), jnp.sin(dispersion), background))
     phases = phases.reshape(1, 3, k1_part, k0_count)
@@ -296,10 +345,13 @@
         ]
         if row + 1 < row_count:
             arrived, packed[row + 1] = lax.optimization_barrier((arrived, packed[row + 1]))
+        if row == 0:
+            slices[0], _ = lax.optimization_barrier((slices[0], arrived[1]))
+            slices = exchange_slices(slices, wave_count, core)
         depth = depth_transform(me, arrived, matrices, base, devices)
         depth = depth.reshape(devices, -1, 2 * pixels)
         depth = lax.all_to_all(depth, ("wave", "pix"), split_axis=0, concat_axis=0, tiled=True)
-        image = refocus(depth, columns, row, row_count, image)
+        image = refocus(me, depth, slices, row, row_count, image)
     return image
 
 

time: 499 us -> 389 us (0.78)
  waiting for transfers between devices: 326 us -> 208 us
  starting transfers between devices: 18.9 us -> 24.1 us
    ppermute x6, waiting for transfers between devices: 206 us -> 94 us  [on_device(): lax.ppermute(packed[row][m], 'wave', [(s, s ^ m) for s in range(wave_coun...]
    ppermute x0 -> x4, waiting for transfers between devices: none -> 94.4 us  [the longest x2 89.9 us: exchange_slices(): own = lax.ppermute(own, 'wave', [(s, s ^ bit) for s in range(wave_count)])]
    all_to_all x2, waiting for transfers between devices: 70.7 us -> 19.6 us  [on_device(): lax.all_to_all(depth, ('wave', 'pix'), split_axis=0, concat_axis=0, tiled...]
    all_gather x2, waiting for transfers between devices: 50 us -> 0.02 us  [gather_slices(): slices[mask] = [lax.all_gather(own, 'pix', axis=0, tiled=False)]]
  transfers between devices with their start and end apart: 11 -> 15, of which waited for: 7 -> 7; matrix products, arithmetic and copies ran while one was open for 0% -> 2% of each run, Pallas kernels for 22% -> 28%
where the time goes in v5:
time: 389 us; the launch traced here: 388 us
  waiting for transfers between devices  208 us (53%)
  Pallas kernels  133 us (34%)
  starting transfers between devices  24.1 us (6%)
  between operations  13.5 us (3%)
  local copies, waits for them, and re-layouts  8 us (2%)
    ppermute x6, waiting for transfers between devices, on_device(): lax.ppermute(packed[row][m], 'wave', [(s, s ^ m) for s in range(wave_coun...  94 us
    ppermute x2, waiting for transfers between devices, exchange_slices(): own = lax.ppermute(own, 'wave', [(s, s ^ bit) for s in range(wave_count)])  89.9 us
    pallas_call x2, Pallas kernels, refocus(): pl.pallas_call(functools.partial(refocus_kernel, wave_count, pix_count),...  49.6 us
    pallas_call x2, Pallas kernels, depth_transform(): pl.pallas_call(functools.partial(transform_kernel, steps), out_shape=jax....  46.8 us
    pallas_call x1, Pallas kernels, stage_matrices(): pl.pallas_call(matrix_kernel, out_shape=(jax.ShapeDtypeStruct((k0_count,...  22.1 us
    all_to_all x2, waiting for transfers between devices, on_device(): lax.all_to_all(depth, ('wave', 'pix'), split_axis=0, concat_axis=0, tiled...  19.6 us
    pallas_call x2, Pallas kernels, pack(): pl.pallas_call(pack_kernel, out_shape=[jax.ShapeDtypeStruct((k1_part, k0_...  14.8 us
    all_to_all x2, starting transfers between devices, on_device(): lax.all_to_all(depth, ('wave', 'pix'), split_axis=0, concat_axis=0, tiled...  8.72 us
  transfers between devices with their start and end apart: 15, of which 7 were waited for; matrix products, arithmetic and copies ran while one was open for 2% of the time, Pallas kernels for 28%

profile of v5, /device:TPU:0, one launch (start us, length us, event | category | flops | bytes accessed | tf_op | source)
XLA Modules:
  0.0 388.1 jit_solution(2519033988630697474)
XLA Ops:
  6.5 0.8 cosine_bitcast_fusion
  7.3 0.7 maximum_bitcast_fusion
  8.0 0.7 broadcast_in_dim.8
  8.7 5.2 %all-to-all-start = ((f32[4,3,32,128]{3,2,1,0:T(8,128)}), f32[4,3,32,128]{3,2,1,0:T(8,128)S(1)}, u32[]{:S(2)}, u32[]{:S(2)}) async-start(f32[4,3,32,128]{3,2,1,0:T(8,128)} %broadcast_in_dim.8), calls=%async_computation | async-start | bytes 393216 | tf_op jit(solution)/shard_map/all_to_all | solution.py:333
  13.9 0.0 all-gather.3.cloned.1.call-start
  13.9 0.6 pad_add_fusion.me_ref
  14.5 7.4 %shard_map.82 = (bf16[32,128,128]{2,1,0:T(8,128)(2,1)}, bf16[32,128,128]{2,1,0:T(8,128)(2,1)}, bf16[32,128,128]{2,1,0:T(8,128)(2,1)}, bf16[32,128,128]{2,1,0:T(8,128)(2,1)}) custom-call(s32[2]{0:T(128)} %pad_add_fusion.me_ref, bf16[2,2,32,128,256]{4,3,2,1,0:T(8,128)(2,1)} %bitcast.26), custom_call_target="tpu_custom_call" | custom-call | bytes 8388608 | tf_op jit(solution)/shard_map/pallas_call | solution.py:55
  21.9 0.0 all-to-all-done
  21.9 2.1 collective-permute-start
  24.0 1.5 collective-permute-start.1
  25.5 0.1 collective-permute-start.2
  25.6 1.3 constant_dynamic-slice_fusion
  26.8 0.8 copy.17
  27.6 0.0 all-gather.3.cloned.1.call-update
  27.7 7.4 %shard_map.83 = (bf16[32,128,128]{2,1,0:T(8,128)(2,1)}, bf16[32,128,128]{2,1,0:T(8,128)(2,1)}, bf16[32,128,128]{2,1,0:T(8,128)(2,1)}, bf16[32,128,128]{2,1,0:T(8,128)(2,1)}) custom-call(s32[2]{0:T(128)} %pad_add_fusion.me_ref, bf16[2,2,32,128,256]{4,3,2,1,0:T(8,128)(2,1)} %bitcast.27), custom_call_target="tpu_custom_call" | custom-call | bytes 8388608 | tf_op jit(solution)/shard_map/pallas_call | solution.py:55
  35.0 0.8 copy.16.phase_ref
  35.9 22.1 %shard_map.84 = (bf16[128,256,256]{2,1,0:T(8,128)(2,1)}, f32[2,8,128,16]{3,2,1,0:T(8,128)}) custom-call(f32[3,128,128]{2,1,0:T(8,128)} %copy.16.phase_ref, f32[2,128,128]{2,1,0:T(8,128)} %constant.41.clone.small_ref, f32[2,8,128,16]{3,2,1,0:T(8,128)} %constant.42.clone.turn_ref), custom_call_target="tpu_custom_call" | custom-call | flops 41943040 | bytes 16777216 | tf_op jit(solution)/shard_map/pallas_call | solution.py:101
  58.0 0.0 collective-permute-done.refs_1_
  58.0 0.0 copy-start
  58.0 12.8 %collective-permute-done.1.refs_2_ = bf16[32,128,128]{2,1,0:T(8,128)(2,1)S(1)} collective-permute-done((bf16[32,128,128]{2,1,0:T(8,128)(2,1)}, bf16[32,128,128]{2,1,0:T(8,128)(2,1)S(1)}, u32[]{:S(2)}, u32[]{:S(2)}) %collective-permute-start.1) | collective-permute-done | bytes 1048608 | tf_op jit(solution)/shard_map/ppermute | solution.py:343
  70.8 0.0 copy-start.1
  70.8 0.0 collective-permute-done.2.refs_3_
  70.8 0.0 copy-done
  70.8 1.0 copy-done.1
  71.7 23.4 %shard_map.86 = bf16[32,4,128,128]{3,2,1,0:T(8,128)(2,1)} custom-call(s32[2]{0:T(128)} %pad_add_fusion.me_ref, bf16[32,128,128]{2,1,0:T(8,128)(2,1)} %get-tuple-element.50.refs_0_, bf16[32,128,128]{2,1,0:T(8,128)(2,1)} %copy-done, bf16[32,128,128]{2,1,0:T(8,128)(2,1)} %copy-done.1, bf16[32,128,128]{2,1,0:T(8,128)(2,1)} %collective-permute-done.2.refs_3_, ...), custom_call_target="tpu_custom_call" | custom-call | flops 5368709120 | bytes 25165824 | tf_op jit(solution)/shard_map/pallas_call | solution.py:183
  95.1 5.0 %all-to-all-start.2 = ((bf16[32,512,128]{2,1,0:T(8,128)(2,1)}), bf16[32,512,128]{2,1,0:T(8,128)(2,1)}, u32[]{:S(2)}, u32[]{:S(2)}) async-start(bf16[32,512,128]{2,1,0:T(8,128)(2,1)} %bitcast.29), calls=%async_computation.2 | async-start | bytes 8388608 | tf_op jit(solution)/shard_map/all_to_all | solution.py:353
  100.1 0.0 all-gather.5.cloned.1.call-start
  100.1 1.8 collective-permute-start.3
  101.9 1.5 collective-permute-start.4
  103.4 0.3 collective-permute-start.5
  103.7 0.9 copy.18
  104.6 0.0 all-gather.5.cloned.1.call-update
  104.6 49.9 %collective-permute-done.3.refs_1_ = bf16[32,128,128]{2,1,0:T(8,128)(2,1)S(1)} collective-permute-done((bf16[32,128,128]{2,1,0:T(8,128)(2,1)}, bf16[32,128,128]{2,1,0:T(8,128)(2,1)S(1)}, u32[]{:S(2)}, u32[]{:S(2)}) %collective-permute-start.3) | collective-permute-done | bytes 1048608 | tf_op jit(solution)/shard_map/ppermute | solution.py:343
  154.5 0.0 copy-start.2
  154.5 0.0 collective-permute-done.4.refs_2_
  154.5 0.0 copy-start.3
  154.5 31.3 %collective-permute-done.5.refs_3_ = bf16[32,128,128]{2,1,0:T(8,128)(2,1)} collective-permute-done((bf16[32,128,128]{2,1,0:T(8,128)(2,1)}, bf16[32,128,128]{2,1,0:T(8,128)(2,1)}, u32[]{:S(2)}, u32[]{:S(2)}) %collective-permute-start.5) | collective-permute-done | bytes 1048608 | tf_op jit(solution)/shard_map/ppermute | solution.py:343
  185.8 0.0 copy-done.2
  185.8 0.0 copy-done.3
  185.8 23.4 %shard_map.85 = bf16[32,4,128,128]{3,2,1,0:T(8,128)(2,1)} custom-call(s32[2]{0:T(128)} %pad_add_fusion.me_ref, bf16[32,128,128]{2,1,0:T(8,128)(2,1)} %get-tuple-element.41.refs_0_, bf16[32,128,128]{2,1,0:T(8,128)(2,1)} %copy-done.2, bf16[32,128,128]{2,1,0:T(8,128)(2,1)} %copy-done.3, bf16[32,128,128]{2,1,0:T(8,128)(2,1)} %collective-permute-done.5.refs_3_, ...), custom_call_target="tpu_custom_call" | custom-call | flops 5368709120 | bytes 25165824 | tf_op jit(solution)/shard_map/pallas_call | solution.py:183
  209.2 19.6 %all-to-all-done.2.depth_ref = bf16[32,512,128]{2,1,0:T(8,128)(2,1)} async-done(((bf16[32,512,128]{2,1,0:T(8,128)(2,1)}), bf16[32,512,128]{2,1,0:T(8,128)(2,1)}, u32[]{:S(2)}, u32[]{:S(2)}) %all-to-all-start.2) | async-done | bytes 4194336 | tf_op jit(solution)/shard_map/all_to_all | solution.py:353
  228.8 3.8 all-to-all-start.1
  232.6 0.0 all-gather.3.cloned.1.call-done.refs_0_.refs_1_
  232.6 1.7 constant_dynamic-slice_fusion.1
  234.4 1.5 collective-permute-start.8
  235.8 1.5 collective-permute-start.6
  237.3 84.9 %collective-permute-done.8.refs_4_ = bf16[8,512,256]{2,1,0:T(8,128)(2,1)S(1)} collective-permute-done((bf16[8,512,256]{2,1,0:T(8,128)(2,1)S(1)}, bf16[8,512,256]{2,1,0:T(8,128)(2,1)S(1)}, u32[]{:S(2)}, u32[]{:S(2)}) %collective-permute-start.8) | collective-permute-done | bytes 2097184 | tf_op jit(solution)/shard_map/ppermute | solution.py:310
  322.2 0.0 copy-start.4
  322.2 0.0 collective-permute-start.9
  322.2 5.0 %collective-permute-done.6.refs_2_ = bf16[8,512,256]{2,1,0:T(8,128)(2,1)} collective-permute-done((bf16[8,512,256]{2,1,0:T(8,128)(2,1)S(1)}, bf16[8,512,256]{2,1,0:T(8,128)(2,1)}, u32[]{:S(2)}, u32[]{:S(2)}) %collective-permute-start.6) | collective-permute-done | bytes 2097184 | tf_op jit(solution)/shard_map/ppermute | solution.py:310
  327.2 0.0 collective-permute-start.7
  327.2 0.0 all-gather.5.cloned.1.call-done.refs_6_.refs_7_
  327.2 0.0 collective-permute-done.9.refs_5_
  327.2 4.5 %collective-permute-done.7.refs_3_ = bf16[8,512,256]{2,1,0:T(8,128)(2,1)} collective-permute-done((bf16[8,512,256]{2,1,0:T(8,128)(2,1)}, bf16[8,512,256]{2,1,0:T(8,128)(2,1)}, u32[]{:S(2)}, u32[]{:S(2)}) %collective-permute-start.7) | collective-permute-done | bytes 2097184 | tf_op jit(solution)/shard_map/ppermute | solution.py:311
  331.7 0.0 copy-done.4
  331.7 24.8 %shard_map.87.refs_8_ = f32[2,2,512,2048]{3,2,1,0:T(8,128)} custom-call(s32[2]{0:T(128)} %pad_add_fusion.me_ref, bf16[32,512,128]{2,1,0:T(8,128)(2,1)} %all-to-all-done.2.depth_ref, bf16[8,1024,256]{2,1,0:T(8,128)(2,1)} %all-gather.3.cloned.1.call-done.refs_0_.refs_1_, bf16[8,1024,256]{2,1,0:T(8,128)(2,1)} %all-gather.3.cloned.1.call-done.refs_0_.refs_1_, ...), custom_call_target="tpu_custom_call" | custom-call | flops 17179869184 | bytes 29360128 | tf_op jit(solution)/shard_map/pallas_call | solution.py:264
  356.5 0.0 all-to-all-done.1.depth_ref
  356.5 24.8 %shard_map.88 = f32[2,2,512,2048]{3,2,1,0:T(8,128)} custom-call(s32[2]{0:T(128)} %pad_add_fusion.me_ref, bf16[32,512,128]{2,1,0:T(8,128)(2,1)} %all-to-all-done.1.depth_ref, bf16[8,1024,256]{2,1,0:T(8,128)(2,1)} %all-gather.3.cloned.1.call-done.refs_0_.refs_1_, ...), custom_call_target="tpu_custom_call", output_to_operand_aliasing={{}: (10, {})} | custom-call | flops 17179869184 | bytes 29360128 | tf_op jit(solution)/shard_map/pallas_call | solution.py:264
  (1 shorter events, 0.0 us)
Async XLA Ops:
  8.7 13.2 %all-to-all-start = ((f32[4,3,32,128]{3,2,1,0:T(8,128)}), f32[4,3,32,128]{3,2,1,0:T(8,128)S(1)}, u32[]{:S(2)}, u32[]{:S(2)}) async-start(f32[4,3,32,128]{3,2,1,0:T(8,128)} %broadcast_in_dim.8), calls=%async_computation | async-start | bytes 393216 | tf_op jit(solution)/shard_map/all_to_all | solution.py:333
  13.9 218.7 %all-gather.3.cloned.1.call-start = ((), (), s32[]{:S(2)}) async-start(), calls=%async_computation.3 | async-start | bytes 4718592 | tf_op jit(solution)/shard_map/all_gather | solution.py:297
  21.9 36.1 %collective-permute-start = (bf16[32,128,128]{2,1,0:T(8,128)(2,1)}, bf16[32,128,128]{2,1,0:T(8,128)(2,1)S(1)}, u32[]{:S(2)}, u32[]{:S(2)}) collective-permute-start(bf16[32,128,128]{2,1,0:T(8,128)(2,1)} %get-tuple-element.34), channel_id=1, source_target_pairs={{0,8},{8,0},{16,24},{24,16},{1,9},{9,1},{17,25},{25,17},{2,10},{10... | collective-permute-start | bytes 3145736 | tf_op jit(solution)/shard_map/ppermute | solution.py:343
  24.0 46.7 %collective-permute-start.1 = (bf16[32,128,128]{2,1,0:T(8,128)(2,1)}, bf16[32,128,128]{2,1,0:T(8,128)(2,1)S(1)}, u32[]{:S(2)}, u32[]{:S(2)}) collective-permute-start(bf16[32,128,128]{2,1,0:T(8,128)(2,1)} %get-tuple-element.35), channel_id=1, source_target_pairs={{0,16},{8,24},{16,0},{24,8},{1,17},{9,25},{17,1},{25,9},{2,18},{10... | collective-permute-start | bytes 3145736 | tf_op jit(solution)/shard_map/ppermute | solution.py:343
  25.5 45.3 %collective-permute-start.2 = (bf16[32,128,128]{2,1,0:T(8,128)(2,1)}, bf16[32,128,128]{2,1,0:T(8,128)(2,1)}, u32[]{:S(2)}, u32[]{:S(2)}) collective-permute-start(bf16[32,128,128]{2,1,0:T(8,128)(2,1)} %get-tuple-element.36), channel_id=1, source_target_pairs={{0,24},{8,16},{16,8},{24,0},{1,25},{9,17},{17,9},{25,1},{2,26},{10... | collective-permute-start | bytes 3145736 | tf_op jit(solution)/shard_map/ppermute | solution.py:343
  58.0 12.8 %copy-start = (bf16[32,128,128]{2,1,0:T(8,128)(2,1)}, bf16[32,128,128]{2,1,0:T(8,128)(2,1)S(1)}, u32[]{:S(2)}) copy-start(bf16[32,128,128]{2,1,0:T(8,128)(2,1)S(1)} %collective-permute-done.refs_1_) | copy-start | bytes 3145732
  70.8 1.0 copy-start.1
  95.1 133.7 %all-to-all-start.2 = ((bf16[32,512,128]{2,1,0:T(8,128)(2,1)}), bf16[32,512,128]{2,1,0:T(8,128)(2,1)}, u32[]{:S(2)}, u32[]{:S(2)}) async-start(bf16[32,512,128]{2,1,0:T(8,128)(2,1)} %bitcast.29), calls=%async_computation.2 | async-start | bytes 8388608 | tf_op jit(solution)/shard_map/all_to_all | solution.py:353
  100.1 227.2 %all-gather.5.cloned.1.call-start = ((), (), s32[]{:S(2)}) async-start(), calls=%async_computation.4 | async-start | bytes 4718592 | tf_op jit(solution)/shard_map/all_gather | solution.py:297
  100.1 54.4 %collective-permute-start.3 = (bf16[32,128,128]{2,1,0:T(8,128)(2,1)}, bf16[32,128,128]{2,1,0:T(8,128)(2,1)S(1)}, u32[]{:S(2)}, u32[]{:S(2)}) collective-permute-start(bf16[32,128,128]{2,1,0:T(8,128)(2,1)} %get-tuple-element.42), channel_id=1, source_target_pairs={{0,8},{8,0},{16,24},{24,16},{1,9},{9,1},{17,25},{25,17},{2,10},{10... | collective-permute-start | bytes 3145736 | tf_op jit(solution)/shard_map/ppermute | solution.py:343
  101.9 52.6 %collective-permute-start.4 = (bf16[32,128,128]{2,1,0:T(8,128)(2,1)}, bf16[32,128,128]{2,1,0:T(8,128)(2,1)S(1)}, u32[]{:S(2)}, u32[]{:S(2)}) collective-permute-start(bf16[32,128,128]{2,1,0:T(8,128)(2,1)} %get-tuple-element.43), channel_id=1, source_target_pairs={{0,16},{8,24},{16,0},{24,8},{1,17},{9,25},{17,1},{25,9},{2,18},{10... | collective-permute-start | bytes 3145736 | tf_op jit(solution)/shard_map/ppermute | solution.py:343
  103.4 82.5 %collective-permute-start.5 = (bf16[32,128,128]{2,1,0:T(8,128)(2,1)}, bf16[32,128,128]{2,1,0:T(8,128)(2,1)}, u32[]{:S(2)}, u32[]{:S(2)}) collective-permute-start(bf16[32,128,128]{2,1,0:T(8,128)(2,1)} %get-tuple-element.44), channel_id=1, source_target_pairs={{0,24},{8,16},{16,8},{24,0},{1,25},{9,17},{17,9},{25,1},{2,26},{10... | collective-permute-start | bytes 3145736 | tf_op jit(solution)/shard_map/ppermute | solution.py:343
  154.5 31.3 %copy-start.2 = (bf16[32,128,128]{2,1,0:T(8,128)(2,1)}, bf16[32,128,128]{2,1,0:T(8,128)(2,1)S(1)}, u32[]{:S(2)}) copy-start(bf16[32,128,128]{2,1,0:T(8,128)(2,1)S(1)} %collective-permute-done.3.refs_1_) | copy-start | bytes 3145732
  154.5 31.3 %copy-start.3 = (bf16[32,128,128]{2,1,0:T(8,128)(2,1)}, bf16[32,128,128]{2,1,0:T(8,128)(2,1)S(1)}, u32[]{:S(2)}) copy-start(bf16[32,128,128]{2,1,0:T(8,128)(2,1)S(1)} %collective-permute-done.4.refs_2_) | copy-start | bytes 3145732
  228.8 127.7 %all-to-all-start.1 = ((bf16[32,512,128]{2,1,0:T(8,128)(2,1)}), bf16[32,512,128]{2,1,0:T(8,128)(2,1)}, u32[]{:S(2)}, u32[]{:S(2)}) async-start(bf16[32,512,128]{2,1,0:T(8,128)(2,1)} %bitcast.28), calls=%async_computation.1 | async-start | bytes 8388608 | tf_op jit(solution)/shard_map/all_to_all | solution.py:353
  234.4 87.8 %collective-permute-start.8 = (bf16[8,512,256]{2,1,0:T(8,128)(2,1)S(1)}, bf16[8,512,256]{2,1,0:T(8,128)(2,1)S(1)}, u32[]{:S(2)}, u32[]{:S(2)}) collective-permute-start(bf16[8,512,256]{2,1,0:T(8,128)(2,1)S(1)} %constant_dynamic-slice_fusion.1), channel_id=1, source_target_pairs={{0,16},{8,24},{16,0},{24,8},{1,17},{9,25},{17,1},{25,9},{2,18},{10... | collective-permute-start | bytes 6291464 | tf_op jit(solution)/shard_map/ppermute | solution.py:310
  235.8 91.4 %collective-permute-start.6 = (bf16[8,512,256]{2,1,0:T(8,128)(2,1)S(1)}, bf16[8,512,256]{2,1,0:T(8,128)(2,1)}, u32[]{:S(2)}, u32[]{:S(2)}) collective-permute-start(bf16[8,512,256]{2,1,0:T(8,128)(2,1)S(1)} %constant_dynamic-slice_fusion.1), channel_id=1, source_target_pairs={{0,8},{8,0},{16,24},{24,16},{1,9},{9,1},{17,25},{25,17},{2,10},{10... | collective-permute-start | bytes 6291464 | tf_op jit(solution)/shard_map/ppermute | solution.py:310
  322.2 9.6 %copy-start.4 = (bf16[8,512,256]{2,1,0:T(8,128)(2,1)}, bf16[8,512,256]{2,1,0:T(8,128)(2,1)S(1)}, u32[]{:S(2)}) copy-start(bf16[8,512,256]{2,1,0:T(8,128)(2,1)S(1)} %collective-permute-done.8.refs_4_) | copy-start | bytes 6291460
  322.2 5.1 %collective-permute-start.9 = (bf16[8,512,256]{2,1,0:T(8,128)(2,1)S(1)}, bf16[8,512,256]{2,1,0:T(8,128)(2,1)}, u32[]{:S(2)}, u32[]{:S(2)}) collective-permute-start(bf16[8,512,256]{2,1,0:T(8,128)(2,1)S(1)} %collective-permute-done.8.refs_4_), channel_id=1, source_target_pairs={{0,1},{1,0},{2,3},{3,2},{4,5},{5,4},{6,7},{7,6},{8,9},{9,8},{10,11... | collective-permute-start | bytes 6291464 | tf_op jit(solution)/shard_map/ppermute | solution.py:311
  327.2 4.5 %collective-permute-start.7 = (bf16[8,512,256]{2,1,0:T(8,128)(2,1)}, bf16[8,512,256]{2,1,0:T(8,128)(2,1)}, u32[]{:S(2)}, u32[]{:S(2)}) collective-permute-start(bf16[8,512,256]{2,1,0:T(8,128)(2,1)} %collective-permute-done.6.refs_2_), channel_id=1, source_target_pairs={{0,1},{1,0},{2,3},{3,2},{4,5},{5,4},{6,7},{7,6},{8,9},{9,8},{10,11... | collective-permute-start | bytes 6291464 | tf_op jit(solution)/shard_map/ppermute | solution.py:311
Sparse Core Ops, SparseCore 0:
  27.8 48.7 all-gather.2
  104.7 97.8 all-gather.4

commit v6 on v5

--- a/solution.py
+++ b/solution.py
@@ -10,6 +10,7 @@
 from jax.sharding import PartitionSpec as P
 
 CHUNK = 16
+MATRIX_COST = 120 * 10**9
 VMEM_BYTES = 56 * 1024 * 1024
 
 
@@ -208,13 +209,13 @@
         ],
         compiler_params=pltpu.CompilerParams(vmem_limit_bytes=VMEM_BYTES),
         cost_estimate=pl.CostEstimate(
-            flops=20 * 128 * length * lanes, bytes_accessed=12 * length * lanes, transcendentals=0
+            flops=MATRIX_COST, bytes_accessed=12 * length * lanes, transcendentals=0
         ),
     )(me, *pieces, matrices, base, jnp.asarray(fine))
 
 
-def even_mask(mask):
-    return bin(mask).count("1") % 2 == 0
+def even_masks(count):
+    return [mask for mask in range(count) if bin(mask).count("1") % 2 == 0]
 
 
 def refocus_kernel(wave_count, pix_count, me_ref, depth_ref, *refs):
@@ -230,7 +231,7 @@
         for m in range(wave_count):
             first = (me_ref[0] ^ m) * pix_count
             for h in range(2):
-                start = first + (h if even_mask(m) else core ^ h) * half
+                start = first + (h if m in even_masks(wave_count) else core ^ h) * half
                 for p in range(half):
                     at = (m * pix_count + h * half + p) * lanes
                     own = slice(at, at + lanes)
@@ -238,27 +239,33 @@
                     rows[:depths, own] = (value * sign).astype(jnp.bfloat16)
                     rows[depths:, own] = swap_halves(value).astype(jnp.bfloat16)
 
-    columns = jnp.concatenate([ref[0] for ref in prop_refs], axis=0)
+    columns = jnp.concatenate(
+        [ref[...].reshape(half * lanes, ref.shape[-1]) for ref in prop_refs], axis=0
+    )
     for c in range(2):
         out_ref[c, 0] = jnp.dot(
             rows[c * depths : (c + 1) * depths], columns, preferred_element_type=jnp.float32
         )
 
 
-def refocus(me, depth, slices, row, row_count, image):
-    wave_count = len(slices)
+def refocus(me, depth, gathered, fetched, row, row_count, image):
+    wave_count = 2 * gathered.shape[1]
     senders, depths, lanes = depth.shape
     pix_count = senders // wave_count
     span = pix_count // 2 * lanes
-    columns = slices[0][0].shape[2]
+    columns = gathered.shape[3]
+    even = even_masks(wave_count)
     operands, specs = [], []
     for mask in range(wave_count):
         for h in range(2):
-            if even_mask(mask):
-                operands.append(slices[mask][0])
-                specs.append(pl.BlockSpec((1, span, columns), lambda q, h=h: (q, h, 0)))
+            if mask in even:
+                at = even.index(mask)
+                operands.append(gathered)
+                specs.append(
+                    pl.BlockSpec((1, 1, span, columns), lambda q, at=at, h=h: (q, at, h, 0))
+                )
             else:
-                operands.append(slices[mask][h])
+                operands.append(fetched[mask][h])
                 specs.append(pl.BlockSpec((1, span, columns), lambda q: (q, 0, 0)))
     earlier = () if image is None else (image,)
     return pl.pallas_call(
@@ -278,38 +285,37 @@
         scratch_shapes=[pltpu.VMEM((2 * depths, senders * lanes), jnp.bfloat16)],
         compiler_params=pltpu.CompilerParams(vmem_limit_bytes=VMEM_BYTES),
         cost_estimate=pl.CostEstimate(
-            flops=4 * depths * senders * lanes * pix_count * columns,
+            flops=MATRIX_COST,
             bytes_accessed=28 * 1024 * 1024,
             transcendentals=0,
         ),
     )(me, depth, *operands, *earlier)
 
 
-def gather_slices(propagator, wave_pos, wave_count):
+def own_slices(propagator, wave_pos, wave_count):
     _, span, pix_local = propagator.shape
-    pix_count = lax.axis_size("pix")
-    rows = propagator.reshape(2, pix_count, wave_count, -1, pix_local)
-    slices = {}
+    rows = propagator.reshape(2, lax.axis_size("pix"), wave_count, -1, pix_local)
+    slices = []
+    for mask in even_masks(wave_count):
+        own = lax.dynamic_index_in_dim(rows, wave_pos ^ mask, axis=2, keepdims=False)
+        slices.append(jnp.swapaxes(own, 0, 1).reshape(2 * span // wave_count, pix_local))
+    return jnp.stack(slices)
+
+
+def exchange_slices(gathered, wave_count, core):
+    pix_count, _, span, columns = gathered.shape
+    half = span // 2
+    result = {}
     for mask in range(wave_count):
-        if even_mask(mask):
-            own = lax.dynamic_index_in_dim(rows, wave_pos ^ mask, axis=2, keepdims=False)
-            own = jnp.swapaxes(own, 0, 1).reshape(2 * span // wave_count, pix_local)
-            slices[mask] = [lax.all_gather(own, "pix", axis=0, tiled=False)]
-    return slices
-
-
-def exchange_slices(slices, wave_count, core):
-    pix_count = lax.axis_size("pix")
-    result = dict(slices)
-    for mask in range(wave_count):
-        if not even_mask(mask):
+        if mask not in even_masks(wave_count):
             bit = mask & -mask
-            source = slices[mask ^ bit][0]
-            half = source.shape[1] // 2
-            own = lax.dynamic_slice_in_dim(source, core * half, half, axis=1)
+            at = even_masks(wave_count).index(mask ^ bit)
+            own = lax.dynamic_slice(
+                gathered, (0, at, core * half, 0), (pix_count, 1, half, columns)
+            ).reshape(pix_count, half, columns)
             own = lax.ppermute(own, "wave", [(s, s ^ bit) for s in range(wave_count)])
             mate = lax.ppermute(own, "pix", [(s, s ^ 1) for s in range(pix_count)])
-            result[mask] = [own, mate]
+            result[mask] = (own, mate)
     return result
 
 
@@ -325,7 +331,9 @@
     wave_pos = lax.axis_index("wave")
     core = lax.axis_index("pix") % 2
     me = jnp.stack((wave_pos, core)).astype(jnp.int32)
-    slices = gather_slices(propagator, wave_pos, wave_count)
+    own = own_slices(propagator, wave_pos, wave_count)
+    own, me = lax.optimization_barrier((own, me))
+    gathered = lax.all_gather(own, "pix", axis=0, tiled=False)
 
     phases = jnp.stack((jnp.cos(dispersion), jnp.sin(dispersion), background))
     phases = phases.reshape(1, 3, k1_part, k0_count)
@@ -346,12 +354,11 @@
         if row + 1 < row_count:
             arrived, packed[row + 1] = lax.optimization_barrier((arrived, packed[row + 1]))
         if row == 0:
-            slices[0], _ = lax.optimization_barrier((slices[0], arrived[1]))
-            slices = exchange_slices(slices, wave_count, core)
+            fetched = exchange_slices(gathered, wave_count, core)
         depth = depth_transform(me, arrived, matrices, base, devices)
         depth = depth.reshape(devices, -1, 2 * pixels)
         depth = lax.all_to_all(depth, ("wave", "pix"), split_axis=0, concat_axis=0, tiled=True)
-        image = refocus(me, depth, slices, row, row_count, image)
+        image = refocus(me, depth, gathered, fetched, row, row_count, image)
     return image
 
 

time: 389 us -> 353 us (0.907)
  waiting for transfers between devices: 208 us -> 174 us
    ppermute x6, waiting for transfers between devices: 94 us -> 14.9 us  [on_device(): lax.ppermute(packed[row][m], 'wave', [(s, s ^ m) for s in range(wave_coun...]
    all_to_all x2, waiting for transfers between devices: 19.6 us -> 72.4 us  [on_device(): lax.all_to_all(depth, ('wave', 'pix'), split_axis=0, concat_axis=0, tiled...]
    ppermute x2, waiting for transfers between devices: 89.9 us -> 67.4 us  [exchange_slices(): own = lax.ppermute(own, 'wave', [(s, s ^ bit) for s in range(wave_count)])]
    all_gather x2 -> x1, waiting for transfers between devices: 0.02 us -> 19 us  [on_device(): gathered = lax.all_gather(own, 'pix', axis=0, tiled=False)]
    dynamic_slice x4 -> x0, local copies, waits for them, and re-layouts: 4.72 us -> none  [the longest x3 2.98 us: gather_slices(): lax.dynamic_index_in_dim(rows, wave_pos ^ mask, axis=2, keepdims=False)]
    ppermute x2, waiting for transfers between devices: 4.49 us -> 0.01 us  [exchange_slices(): mate = lax.ppermute(own, 'pix', [(s, s ^ 1) for s in range(pix_count)])]
  transfers between devices with their start and end apart: 15 -> 14, of which waited for: 7 -> 5; matrix products, arithmetic and copies ran while one was open for 2% -> 1% of each run, Pallas kernels for 28% -> 31%
where the time goes in v6:
time: 353 us; the launch traced here: 352 us
  waiting for transfers between devices  174 us (49%)
  Pallas kernels  133 us (38%)
  starting transfers between devices  23.9 us (7%)
  between operations  13.5 us (4%)
  local copies, waits for them, and re-layouts  6.05 us (2%)
    all_to_all x2, waiting for transfers between devices, on_device(): lax.all_to_all(depth, ('wave', 'pix'), split_axis=0, concat_axis=0, tiled...  72.4 us
    ppermute x2, waiting for transfers between devices, exchange_slices(): own = lax.ppermute(own, 'wave', [(s, s ^ bit) for s in range(wave_count)])  67.4 us
    pallas_call x2, Pallas kernels, refocus(): pl.pallas_call(functools.partial(refocus_kernel, wave_count, pix_count),...  49.6 us
    pallas_call x2, Pallas kernels, depth_transform(): pl.pallas_call(functools.partial(transform_kernel, steps), out_shape=jax....  46.8 us
    pallas_call x1, Pallas kernels, stage_matrices(): pl.pallas_call(matrix_kernel, out_shape=(jax.ShapeDtypeStruct((k0_count,...  22.1 us
    all_gather x1, waiting for transfers between devices, on_device(): gathered = lax.all_gather(own, 'pix', axis=0, tiled=False)  19 us
    pallas_call x2, Pallas kernels, pack(): pl.pallas_call(pack_kernel, out_shape=[jax.ShapeDtypeStruct((k1_part, k0_...  15 us
    ppermute x6, waiting for transfers between devices, on_device(): lax.ppermute(packed[row][m], 'wave', [(s, s ^ m) for s in range(wave_coun...  14.9 us
  transfers between devices with their start and end apart: 14, of which 5 were waited for; matrix products, arithmetic and copies ran while one was open for 1% of the time, Pallas kernels for 31%

profile of v6, /device:TPU:0, one launch (start us, length us, event | category | flops | bytes accessed | tf_op | source)
XLA Modules:
  0.0 352.4 jit_solution(15007128056794245594)
XLA Ops:
  6.5 0.0 copy-start
  6.5 0.0 copy-start.1
  6.5 0.0 all-gather.3.cloned.1.call-start
  6.5 1.3 dynamic-slice_bitcast_fusion.2
  7.9 0.7 pad_add_fusion.me_ref
  8.6 1.1 pad_maximum_fusion
  9.7 0.0 all-gather.3.cloned.1.call-update
  9.7 0.0 copy-done
  9.7 0.1 cosine_bitcast_fusion
  9.8 0.0 copy-done.1
  9.8 0.7 broadcast_in_dim.8
  10.5 5.2 %all-to-all-start = ((f32[4,3,32,128]{3,2,1,0:T(8,128)}), f32[4,3,32,128]{3,2,1,0:T(8,128)S(1)}, u32[]{:S(2)}, u32[]{:S(2)}) async-start(f32[4,3,32,128]{3,2,1,0:T(8,128)} %broadcast_in_dim.8), calls=%async_computation | async-start | bytes 393216 | tf_op jit(solution)/shard_map/all_to_all | solution.py:341
  15.7 7.5 %shard_map.82 = (bf16[32,128,128]{2,1,0:T(8,128)(2,1)}, bf16[32,128,128]{2,1,0:T(8,128)(2,1)}, bf16[32,128,128]{2,1,0:T(8,128)(2,1)}, bf16[32,128,128]{2,1,0:T(8,128)(2,1)}) custom-call(s32[2]{0:T(128)} %pad_add_fusion.me_ref, bf16[2,2,32,128,256]{4,3,2,1,0:T(8,128)(2,1)} %bitcast.29), custom_call_target="tpu_custom_call" | custom-call | bytes 8388608 | tf_op jit(solution)/shard_map/pallas_call | solution.py:56
  23.2 0.0 all-to-all-done
  23.2 2.1 collective-permute-start
  25.4 1.5 collective-permute-start.1
  26.8 0.1 collective-permute-start.2
  26.9 7.4 %shard_map.83 = (bf16[32,128,128]{2,1,0:T(8,128)(2,1)}, bf16[32,128,128]{2,1,0:T(8,128)(2,1)}, bf16[32,128,128]{2,1,0:T(8,128)(2,1)}, bf16[32,128,128]{2,1,0:T(8,128)(2,1)}) custom-call(s32[2]{0:T(128)} %pad_add_fusion.me_ref, bf16[2,2,32,128,256]{4,3,2,1,0:T(8,128)(2,1)} %bitcast.30), custom_call_target="tpu_custom_call" | custom-call | bytes 8388608 | tf_op jit(solution)/shard_map/pallas_call | solution.py:56
  34.3 0.8 copy.17.phase_ref
  35.1 22.1 %shard_map.84 = (bf16[128,256,256]{2,1,0:T(8,128)(2,1)}, f32[2,8,128,16]{3,2,1,0:T(8,128)}) custom-call(f32[3,128,128]{2,1,0:T(8,128)} %copy.17.phase_ref, f32[2,128,128]{2,1,0:T(8,128)} %constant.41.clone.small_ref, f32[2,8,128,16]{3,2,1,0:T(8,128)} %constant.42.clone.turn_ref), custom_call_target="tpu_custom_call" | custom-call | flops 41943040 | bytes 16777216 | tf_op jit(solution)/shard_map/pallas_call | solution.py:102
  57.2 0.0 collective-permute-done.refs_1_
  57.2 0.0 copy-start.3
  57.2 14.9 %collective-permute-done.1.refs_2_ = bf16[32,128,128]{2,1,0:T(8,128)(2,1)S(1)} collective-permute-done((bf16[32,128,128]{2,1,0:T(8,128)(2,1)}, bf16[32,128,128]{2,1,0:T(8,128)(2,1)S(1)}, u32[]{:S(2)}, u32[]{:S(2)}) %collective-permute-start.1) | collective-permute-done | bytes 1048608 | tf_op jit(solution)/shard_map/ppermute | solution.py:351
  72.1 0.0 copy-start.4
  72.1 0.0 collective-permute-done.2.refs_3_
  72.1 1.3 collective-permute-start.3
  73.4 0.7 collective-permute-start.4
  74.1 1.5 collective-permute-start.5
  75.6 19.0 %all-gather.3.cloned.1.call-done = bf16[16,1024,256]{2,1,0:T(8,128)(2,1)} async-done(((bf16[2,1024,256]{2,1,0:T(8,128)(2,1)}), bf16[16,1024,256]{2,1,0:T(8,128)(2,1)}) %all-gather.3.cloned.1.call-update) | async-done | bytes 8388624 | tf_op jit(solution)/shard_map/all_gather | solution.py:336
  94.6 0.0 copy-done.4
  94.6 1.7 dynamic-slice_bitcast_fusion
  96.3 1.6 collective-permute-start.8
  97.9 1.5 collective-permute-start.6
  99.4 0.0 copy-done.3
  99.4 23.4 %shard_map.86 = bf16[32,4,128,128]{3,2,1,0:T(8,128)(2,1)} custom-call(s32[2]{0:T(128)} %pad_add_fusion.me_ref, bf16[32,128,128]{2,1,0:T(8,128)(2,1)} %get-tuple-element.51.refs_0_, bf16[32,128,128]{2,1,0:T(8,128)(2,1)} %copy-done.3, bf16[32,128,128]{2,1,0:T(8,128)(2,1)} %copy-done.4, bf16[32,128,128]{2,1,0:T(8,128)(2,1)} %collective-permute-done.2.refs_3_, ...), custom_call_target="tpu_custom_call" | custom-call | flops 120000004096 | bytes 25165824 | tf_op jit(solution)/shard_map/pallas_call | solution.py:184
  122.8 3.6 %all-to-all-start.2 = ((bf16[32,512,128]{2,1,0:T(8,128)(2,1)}), bf16[32,512,128]{2,1,0:T(8,128)(2,1)}, u32[]{:S(2)}, u32[]{:S(2)}) async-start(bf16[32,512,128]{2,1,0:T(8,128)(2,1)} %bitcast.31), calls=%async_computation.2 | async-start | bytes 8388608 | tf_op jit(solution)/shard_map/all_to_all | solution.py:360
  126.4 67.4 %collective-permute-done.8.refs_4_ = bf16[8,512,256]{2,1,0:T(8,128)(2,1)} collective-permute-done((bf16[8,512,256]{2,1,0:T(8,128)(2,1)S(1)}, bf16[8,512,256]{2,1,0:T(8,128)(2,1)}, u32[]{:S(2)}, u32[]{:S(2)}) %collective-permute-start.8) | collective-permute-done | bytes 2097184 | tf_op jit(solution)/shard_map/ppermute | solution.py:316
  193.7 0.0 collective-permute-start.9
  193.7 0.0 collective-permute-done.6.refs_2_
  193.8 0.5 collective-permute-start.7
  194.3 0.0 collective-permute-done.3.refs_1_
  194.3 0.0 collective-permute-done.4.refs_2_
  194.3 0.0 collective-permute-done.5.refs_3_
  194.3 23.4 %shard_map.85 = bf16[32,4,128,128]{3,2,1,0:T(8,128)(2,1)} custom-call(s32[2]{0:T(128)} %pad_add_fusion.me_ref, bf16[32,128,128]{2,1,0:T(8,128)(2,1)} %get-tuple-element.43.refs_0_, bf16[32,128,128]{2,1,0:T(8,128)(2,1)} %collective-permute-done.3.refs_1_, bf16[32,128,128]{2,1,0:T(8,128)(2,1)} %collective-permute-done.4.refs_2_, ...), custom_call_target="tpu_custom_call" | custom-call | flops 120000004096 | bytes 25165824 | tf_op jit(solution)/shard_map/pallas_call | solution.py:184
  217.7 3.7 %all-to-all-done.2.depth_ref = bf16[32,512,128]{2,1,0:T(8,128)(2,1)} async-done(((bf16[32,512,128]{2,1,0:T(8,128)(2,1)}), bf16[32,512,128]{2,1,0:T(8,128)(2,1)}, u32[]{:S(2)}, u32[]{:S(2)}) %all-to-all-start.2) | async-done | bytes 4194336 | tf_op jit(solution)/shard_map/all_to_all | solution.py:360
  221.4 4.5 %all-to-all-start.1 = ((bf16[32,512,128]{2,1,0:T(8,128)(2,1)}), bf16[32,512,128]{2,1,0:T(8,128)(2,1)}, u32[]{:S(2)}, u32[]{:S(2)}) async-start(bf16[32,512,128]{2,1,0:T(8,128)(2,1)} %bitcast.32), calls=%async_computation.1 | async-start | bytes 8388608 | tf_op jit(solution)/shard_map/all_to_all | solution.py:360
  225.8 0.0 collective-permute-done.9.refs_5_
  225.9 0.0 collective-permute-done.7.refs_3_
  225.9 0.0 copy-start.2
  225.9 1.3 copy-done.2
  227.2 24.8 %shard_map.87.refs_8_ = f32[2,2,512,2048]{3,2,1,0:T(8,128)} custom-call(s32[2]{0:T(128)} %pad_add_fusion.me_ref, bf16[32,512,128]{2,1,0:T(8,128)(2,1)} %all-to-all-done.2.depth_ref, bf16[8,2,1024,256]{3,2,1,0:T(8,128)(2,1)} %bitcast.37, bf16[8,2,1024,256]{3,2,1,0:T(8,128)(2,1)} %bitcast.38, bf16[8,512,256]{2,1,0:T(8,128)(2,1)} %collective-permute-done.6.refs_2_, ...), custom_call_target="tpu_custom_call" | custom-call | flops 120000004096 | bytes 29360128 | tf_op jit(solution)/shard_map/pallas_call | solution.py:271
  252.0 68.7 %all-to-all-done.1.depth_ref = bf16[32,512,128]{2,1,0:T(8,128)(2,1)} async-done(((bf16[32,512,128]{2,1,0:T(8,128)(2,1)}), bf16[32,512,128]{2,1,0:T(8,128)(2,1)}, u32[]{:S(2)}, u32[]{:S(2)}) %all-to-all-start.1) | async-done | bytes 4194336 | tf_op jit(solution)/shard_map/all_to_all | solution.py:360
  320.7 24.8 %shard_map.88 = f32[2,2,512,2048]{3,2,1,0:T(8,128)} custom-call(s32[2]{0:T(128)} %pad_add_fusion.me_ref, bf16[32,512,128]{2,1,0:T(8,128)(2,1)} %all-to-all-done.1.depth_ref, bf16[8,2,1024,256]{3,2,1,0:T(8,128)(2,1)} %bitcast.41, bf16[8,2,1024,256]{3,2,1,0:T(8,128)(2,1)} %bitcast.42, ...), custom_call_target="tpu_custom_call", output_to_operand_aliasing={{}: (10, {})} | custom-call | flops 120000004096 | bytes 29360128 | tf_op jit(solution)/shard_map/pallas_call | solution.py:271
  (4 shorter events, 0.1 us)
Async XLA Ops:
  6.5 3.2 copy-start
  6.5 3.2 copy-start.1
  6.5 88.1 %all-gather.3.cloned.1.call-start = ((), (), s32[]{:S(2)}) async-start(), calls=%async_computation.3 | async-start | bytes 9437184 | tf_op jit(solution)/shard_map/all_gather | solution.py:336
  10.5 12.7 %all-to-all-start = ((f32[4,3,32,128]{3,2,1,0:T(8,128)}), f32[4,3,32,128]{3,2,1,0:T(8,128)S(1)}, u32[]{:S(2)}, u32[]{:S(2)}) async-start(f32[4,3,32,128]{3,2,1,0:T(8,128)} %broadcast_in_dim.8), calls=%async_computation | async-start | bytes 393216 | tf_op jit(solution)/shard_map/all_to_all | solution.py:341
  23.2 34.0 %collective-permute-start = (bf16[32,128,128]{2,1,0:T(8,128)(2,1)}, bf16[32,128,128]{2,1,0:T(8,128)(2,1)S(1)}, u32[]{:S(2)}, u32[]{:S(2)}) collective-permute-start(bf16[32,128,128]{2,1,0:T(8,128)(2,1)} %get-tuple-element.36), channel_id=1, source_target_pairs={{0,8},{8,0},{16,24},{24,16},{1,9},{9,1},{17,25},{25,17},{2,10},{10... | collective-permute-start | bytes 3145736 | tf_op jit(solution)/shard_map/ppermute | solution.py:351
  25.4 46.7 %collective-permute-start.1 = (bf16[32,128,128]{2,1,0:T(8,128)(2,1)}, bf16[32,128,128]{2,1,0:T(8,128)(2,1)S(1)}, u32[]{:S(2)}, u32[]{:S(2)}) collective-permute-start(bf16[32,128,128]{2,1,0:T(8,128)(2,1)} %get-tuple-element.37), channel_id=1, source_target_pairs={{0,16},{8,24},{16,0},{24,8},{1,17},{9,25},{17,1},{25,9},{2,18},{10... | collective-permute-start | bytes 3145736 | tf_op jit(solution)/shard_map/ppermute | solution.py:351
  26.8 45.3 %collective-permute-start.2 = (bf16[32,128,128]{2,1,0:T(8,128)(2,1)}, bf16[32,128,128]{2,1,0:T(8,128)(2,1)}, u32[]{:S(2)}, u32[]{:S(2)}) collective-permute-start(bf16[32,128,128]{2,1,0:T(8,128)(2,1)} %get-tuple-element.38), channel_id=1, source_target_pairs={{0,24},{8,16},{16,8},{24,0},{1,25},{9,17},{17,9},{25,1},{2,26},{10... | collective-permute-start | bytes 3145736 | tf_op jit(solution)/shard_map/ppermute | solution.py:351
  57.2 42.2 %copy-start.3 = (bf16[32,128,128]{2,1,0:T(8,128)(2,1)}, bf16[32,128,128]{2,1,0:T(8,128)(2,1)S(1)}, u32[]{:S(2)}) copy-start(bf16[32,128,128]{2,1,0:T(8,128)(2,1)S(1)} %collective-permute-done.refs_1_) | copy-start | bytes 3145732
  72.1 22.5 %copy-start.4 = (bf16[32,128,128]{2,1,0:T(8,128)(2,1)}, bf16[32,128,128]{2,1,0:T(8,128)(2,1)S(1)}, u32[]{:S(2)}) copy-start(bf16[32,128,128]{2,1,0:T(8,128)(2,1)S(1)} %collective-permute-done.1.refs_2_) | copy-start | bytes 3145732
  72.1 122.2 %collective-permute-start.3 = (bf16[32,128,128]{2,1,0:T(8,128)(2,1)}, bf16[32,128,128]{2,1,0:T(8,128)(2,1)}, u32[]{:S(2)}, u32[]{:S(2)}) collective-permute-start(bf16[32,128,128]{2,1,0:T(8,128)(2,1)} %get-tuple-element.44), channel_id=1, source_target_pairs={{0,8},{8,0},{16,24},{24,16},{1,9},{9,1},{17,25},{25,17},{2,10},{10... | collective-permute-start | bytes 3145736 | tf_op jit(solution)/shard_map/ppermute | solution.py:351
  73.4 120.9 %collective-permute-start.4 = (bf16[32,128,128]{2,1,0:T(8,128)(2,1)}, bf16[32,128,128]{2,1,0:T(8,128)(2,1)}, u32[]{:S(2)}, u32[]{:S(2)}) collective-permute-start(bf16[32,128,128]{2,1,0:T(8,128)(2,1)} %get-tuple-element.45), channel_id=1, source_target_pairs={{0,16},{8,24},{16,0},{24,8},{1,17},{9,25},{17,1},{25,9},{2,18},{10... | collective-permute-start | bytes 3145736 | tf_op jit(solution)/shard_map/ppermute | solution.py:351
  74.1 120.2 %collective-permute-start.5 = (bf16[32,128,128]{2,1,0:T(8,128)(2,1)}, bf16[32,128,128]{2,1,0:T(8,128)(2,1)}, u32[]{:S(2)}, u32[]{:S(2)}) collective-permute-start(bf16[32,128,128]{2,1,0:T(8,128)(2,1)} %get-tuple-element.46), channel_id=1, source_target_pairs={{0,24},{8,16},{16,8},{24,0},{1,25},{9,17},{17,9},{25,1},{2,26},{10... | collective-permute-start | bytes 3145736 | tf_op jit(solution)/shard_map/ppermute | solution.py:351
  96.3 97.4 %collective-permute-start.8 = (bf16[8,512,256]{2,1,0:T(8,128)(2,1)S(1)}, bf16[8,512,256]{2,1,0:T(8,128)(2,1)}, u32[]{:S(2)}, u32[]{:S(2)}) collective-permute-start(bf16[8,512,256]{2,1,0:T(8,128)(2,1)S(1)} %dynamic-slice_bitcast_fusion), channel_id=1, source_target_pairs={{0,16},{8,24},{16,0},{24,8},{1,17},{9,25},{17,1},{25,9},{2,18},{10... | collective-permute-start | bytes 6291464 | tf_op jit(solution)/shard_map/ppermute | solution.py:316
  97.9 95.8 %collective-permute-start.6 = (bf16[8,512,256]{2,1,0:T(8,128)(2,1)S(1)}, bf16[8,512,256]{2,1,0:T(8,128)(2,1)}, u32[]{:S(2)}, u32[]{:S(2)}) collective-permute-start(bf16[8,512,256]{2,1,0:T(8,128)(2,1)S(1)} %dynamic-slice_bitcast_fusion), channel_id=1, source_target_pairs={{0,8},{8,0},{16,24},{24,16},{1,9},{9,1},{17,25},{25,17},{2,10},{10... | collective-permute-start | bytes 6291464 | tf_op jit(solution)/shard_map/ppermute | solution.py:316
  122.8 98.6 %all-to-all-start.2 = ((bf16[32,512,128]{2,1,0:T(8,128)(2,1)}), bf16[32,512,128]{2,1,0:T(8,128)(2,1)}, u32[]{:S(2)}, u32[]{:S(2)}) async-start(bf16[32,512,128]{2,1,0:T(8,128)(2,1)} %bitcast.31), calls=%async_computation.2 | async-start | bytes 8388608 | tf_op jit(solution)/shard_map/all_to_all | solution.py:360
  193.7 32.1 %collective-permute-start.9 = (bf16[8,512,256]{2,1,0:T(8,128)(2,1)}, bf16[8,512,256]{2,1,0:T(8,128)(2,1)}, u32[]{:S(2)}, u32[]{:S(2)}) collective-permute-start(bf16[8,512,256]{2,1,0:T(8,128)(2,1)} %collective-permute-done.8.refs_4_), channel_id=1, source_target_pairs={{0,1},{1,0},{2,3},{3,2},{4,5},{5,4},{6,7},{7,6},{8,9},{9,8},{10,11... | collective-permute-start | bytes 6291464 | tf_op jit(solution)/shard_map/ppermute | solution.py:317
  193.8 32.1 %collective-permute-start.7 = (bf16[8,512,256]{2,1,0:T(8,128)(2,1)}, bf16[8,512,256]{2,1,0:T(8,128)(2,1)S(1)}, u32[]{:S(2)}, u32[]{:S(2)}) collective-permute-start(bf16[8,512,256]{2,1,0:T(8,128)(2,1)} %collective-permute-done.6.refs_2_), channel_id=1, source_target_pairs={{0,1},{1,0},{2,3},{3,2},{4,5},{5,4},{6,7},{7,6},{8,9},{9,8},{10,11... | collective-permute-start | bytes 6291464 | tf_op jit(solution)/shard_map/ppermute | solution.py:317
  221.4 99.3 %all-to-all-start.1 = ((bf16[32,512,128]{2,1,0:T(8,128)(2,1)}), bf16[32,512,128]{2,1,0:T(8,128)(2,1)}, u32[]{:S(2)}, u32[]{:S(2)}) async-start(bf16[32,512,128]{2,1,0:T(8,128)(2,1)} %bitcast.32), calls=%async_computation.1 | async-start | bytes 8388608 | tf_op jit(solution)/shard_map/all_to_all | solution.py:360
  225.9 1.4 copy-start.2
Sparse Core Ops, SparseCore 0:
  9.8 84.7 all-gather.2

commit v7 on v6

--- a/solution.py
+++ b/solution.py
@@ -302,10 +302,10 @@
     return jnp.stack(slices)
 
 
-def exchange_slices(gathered, wave_count, core):
+def fetch_slices(gathered, wave_count, core):
     pix_count, _, span, columns = gathered.shape
     half = span // 2
-    result = {}
+    fetched = {}
     for mask in range(wave_count):
         if mask not in even_masks(wave_count):
             bit = mask & -mask
@@ -313,10 +313,15 @@
             own = lax.dynamic_slice(
                 gathered, (0, at, core * half, 0), (pix_count, 1, half, columns)
             ).reshape(pix_count, half, columns)
-            own = lax.ppermute(own, "wave", [(s, s ^ bit) for s in range(wave_count)])
-            mate = lax.ppermute(own, "pix", [(s, s ^ 1) for s in range(pix_count)])
-            result[mask] = (own, mate)
-    return result
+            fetched[mask] = lax.ppermute(
+                own, "wave", [(s, s ^ bit) for s in range(wave_count)]
+            )
+    return fetched
+
+
+def swap_cores(fetched):
+    pairs = [(s, s ^ 1) for s in range(lax.axis_size("pix"))]
+    return {mask: (own, lax.ppermute(own, "pix", pairs)) for mask, own in fetched.items()}
 
 
 def on_device(raw_spectra, background, dispersion, propagator):
@@ -345,7 +350,7 @@
     packed = [pack(me, raw, wave_count, row) for row in range(row_count)]
     packed[0], phases = lax.optimization_barrier((packed[0], phases))
     matrices, base = stage_matrices(phases)
-    image = None
+    depths = []
     for row in range(row_count):
         arrived = [packed[row][0]] + [
             lax.ppermute(packed[row][m], "wave", [(s, s ^ m) for s in range(wave_count)])
@@ -353,11 +358,18 @@
         ]
         if row + 1 < row_count:
             arrived, packed[row + 1] = lax.optimization_barrier((arrived, packed[row + 1]))
+        depth = depth_transform(me, arrived, matrices, base, devices)
         if row == 0:
-            fetched = exchange_slices(gathered, wave_count, core)
-        depth = depth_transform(me, arrived, matrices, base, devices)
+            source, _ = lax.optimization_barrier((gathered, depth))
+            fetched = fetch_slices(source, wave_count, core)
+        if row == row_count - 1:
+            fetched, _ = lax.optimization_barrier((fetched, depth))
+            fetched = swap_cores(fetched)
         depth = depth.reshape(devices, -1, 2 * pixels)
         depth = lax.all_to_all(depth, ("wave", "pix"), split_axis=0, concat_axis=0, tiled=True)
+        depths.append(depth)
+    image = None
+    for row, depth in enumerate(depths):
         image = refocus(me, depth, gathered, fetched, row, row_count, image)
     return image
 

time: 353 us -> 346 us (0.980)
  waiting for transfers between devices: 174 us -> 165 us
    ppermute x6, waiting for transfers between devices: 14.9 us -> 45.8 us  [on_device(): lax.ppermute(packed[row][m], 'wave', [(s, s ^ m) for s in range(wave_coun...]
    all_gather x1, waiting for transfers between devices: 19 us -> 0.02 us  [on_device(): gathered = lax.all_gather(own, 'pix', axis=0, tiled=False)]
    ppermute x4, waiting for transfers between devices: 67.4 us -> 50.2 us  [the longest x2 49 us: fetch_slices(): lax.ppermute(own, 'wave', [(s, s ^ bit) for s in range(wave_count)])]
  transfers between devices with their start and end apart: 14 -> 14, of which waited for: 5 -> 7; matrix products, arithmetic and copies ran while one was open for 1% -> 1% of each run, Pallas kernels for 31% -> 31%
where the time goes in v7:
time: 346 us; the launch traced here: 345 us
  waiting for transfers between devices  165 us (48%)
  Pallas kernels  133 us (38%)
  starting transfers between devices  27.1 us (8%)
  between operations  13.5 us (4%)
  local copies, waits for them, and re-layouts  4.74 us (1%)
    all_to_all x2, waiting for transfers between devices, on_device(): lax.all_to_all(depth, ('wave', 'pix'), split_axis=0, concat_axis=0, tiled...  69 us
    pallas_call x2, Pallas kernels, refocus(): pl.pallas_call(functools.partial(refocus_kernel, wave_count, pix_count),...  49.6 us
    ppermute x2, waiting for transfers between devices, fetch_slices(): lax.ppermute(own, 'wave', [(s, s ^ bit) for s in range(wave_count)])  49 us
    pallas_call x2, Pallas kernels, depth_transform(): pl.pallas_call(functools.partial(transform_kernel, steps), out_shape=jax....  46.7 us
    ppermute x6, waiting for transfers between devices, on_device(): lax.ppermute(packed[row][m], 'wave', [(s, s ^ m) for s in range(wave_coun...  45.8 us
    pallas_call x1, Pallas kernels, stage_matrices(): pl.pallas_call(matrix_kernel, out_shape=(jax.ShapeDtypeStruct((k0_count,...  22.1 us
    pallas_call x2, Pallas kernels, pack(): pl.pallas_call(pack_kernel, out_shape=[jax.ShapeDtypeStruct((k1_part, k0_...  14.9 us
    all_to_all x2, starting transfers between devices, on_device(): lax.all_to_all(depth, ('wave', 'pix'), split_axis=0, concat_axis=0, tiled...  11 us
  transfers between devices with their start and end apart: 14, of which 7 were waited for; matrix products, arithmetic and copies ran while one was open for 1% of the time, Pallas kernels for 31%

profile of v7, /device:TPU:0, one launch (start us, length us, event | category | flops | bytes accessed | tf_op | source)
XLA Modules:
  0.0 345.3 jit_solution(2618971146494781)
XLA Ops:
  6.5 0.0 copy-start
  6.5 0.0 copy-start.1
  6.5 0.0 all-gather.3.cloned.1.call-start
  6.5 1.3 dynamic-slice_bitcast_fusion.2
  7.9 0.6 pad_add_fusion.me_ref
  8.6 1.1 pad_maximum_fusion
  9.7 0.0 all-gather.3.cloned.1.call-update
  9.7 0.0 copy-done
  9.7 0.1 cosine_bitcast_fusion
  9.8 0.0 copy-done.1
  9.8 0.7 broadcast_in_dim.8
  10.5 5.2 %all-to-all-start = ((f32[4,3,32,128]{3,2,1,0:T(8,128)}), f32[4,3,32,128]{3,2,1,0:T(8,128)S(1)}, u32[]{:S(2)}, u32[]{:S(2)}) async-start(f32[4,3,32,128]{3,2,1,0:T(8,128)} %broadcast_in_dim.8), calls=%async_computation | async-start | bytes 393216 | tf_op jit(solution)/shard_map/all_to_all | solution.py:346
  15.7 7.6 %shard_map.82 = (bf16[32,128,128]{2,1,0:T(8,128)(2,1)}, bf16[32,128,128]{2,1,0:T(8,128)(2,1)}, bf16[32,128,128]{2,1,0:T(8,128)(2,1)}, bf16[32,128,128]{2,1,0:T(8,128)(2,1)}) custom-call(s32[2]{0:T(128)} %pad_add_fusion.me_ref, bf16[2,2,32,128,256]{4,3,2,1,0:T(8,128)(2,1)} %bitcast.29), custom_call_target="tpu_custom_call" | custom-call | bytes 8388608 | tf_op jit(solution)/shard_map/pallas_call | solution.py:56
  23.2 0.0 all-to-all-done
  23.3 2.1 collective-permute-start
  25.4 1.5 collective-permute-start.1
  26.9 0.1 collective-permute-start.2
  26.9 7.4 %shard_map.83 = (bf16[32,128,128]{2,1,0:T(8,128)(2,1)}, bf16[32,128,128]{2,1,0:T(8,128)(2,1)}, bf16[32,128,128]{2,1,0:T(8,128)(2,1)}, bf16[32,128,128]{2,1,0:T(8,128)(2,1)}) custom-call(s32[2]{0:T(128)} %pad_add_fusion.me_ref, bf16[2,2,32,128,256]{4,3,2,1,0:T(8,128)(2,1)} %bitcast.30), custom_call_target="tpu_custom_call" | custom-call | bytes 8388608 | tf_op jit(solution)/shard_map/pallas_call | solution.py:56
  34.3 0.8 copy.17.phase_ref
  35.1 22.1 %shard_map.84 = (bf16[128,256,256]{2,1,0:T(8,128)(2,1)}, f32[2,8,128,16]{3,2,1,0:T(8,128)}) custom-call(f32[3,128,128]{2,1,0:T(8,128)} %copy.17.phase_ref, f32[2,128,128]{2,1,0:T(8,128)} %constant.41.clone.small_ref, f32[2,8,128,16]{3,2,1,0:T(8,128)} %constant.42.clone.turn_ref), custom_call_target="tpu_custom_call" | custom-call | flops 41943040 | bytes 16777216 | tf_op jit(solution)/shard_map/pallas_call | solution.py:102
  57.2 0.0 collective-permute-done.refs_1_
  57.2 0.0 copy-start.3
  57.2 14.9 %collective-permute-done.1.refs_2_ = bf16[32,128,128]{2,1,0:T(8,128)(2,1)S(1)} collective-permute-done((bf16[32,128,128]{2,1,0:T(8,128)(2,1)}, bf16[32,128,128]{2,1,0:T(8,128)(2,1)S(1)}, u32[]{:S(2)}, u32[]{:S(2)}) %collective-permute-start.1) | collective-permute-done | bytes 1048608 | tf_op jit(solution)/shard_map/ppermute | solution.py:356
  72.1 0.0 copy-start.4
  72.1 0.0 collective-permute-done.2.refs_3_
  72.1 0.0 copy-start.5
  72.1 1.2 collective-permute-start.3
  73.3 0.9 collective-permute-start.4
  74.2 1.5 collective-permute-start.5
  75.7 0.0 copy-done.3
  75.7 0.0 copy-done.4
  75.7 0.0 copy-done.5
  75.7 23.4 %shard_map.86 = bf16[32,4,128,128]{3,2,1,0:T(8,128)(2,1)} custom-call(s32[2]{0:T(128)} %pad_add_fusion.me_ref, bf16[32,128,128]{2,1,0:T(8,128)(2,1)} %get-tuple-element.54.refs_0_, bf16[32,128,128]{2,1,0:T(8,128)(2,1)} %copy-done.3, bf16[32,128,128]{2,1,0:T(8,128)(2,1)} %copy-done.4, bf16[32,128,128]{2,1,0:T(8,128)(2,1)} %copy-done.5, ...), custom_call_target="tpu_custom_call" | custom-call | flops 120000004096 | bytes 25165824 | tf_op jit(solution)/shard_map/pallas_call | solution.py:184
  99.0 5.2 %all-to-all-start.2 = ((bf16[32,512,128]{2,1,0:T(8,128)(2,1)}), bf16[32,512,128]{2,1,0:T(8,128)(2,1)}, u32[]{:S(2)}, u32[]{:S(2)}) async-start(bf16[32,512,128]{2,1,0:T(8,128)(2,1)} %bitcast.31), calls=%async_computation.2 | async-start | bytes 8388608 | tf_op jit(solution)/shard_map/all_to_all | solution.py:369
  104.2 0.0 all-gather.3.cloned.1.call-done
  104.2 1.7 dynamic-slice_bitcast_fusion
  106.0 1.8 collective-permute-start.7
  107.7 1.5 collective-permute-start.6
  109.2 0.0 collective-permute-done.3.refs_1_
  109.2 18.1 %collective-permute-done.4.refs_2_ = bf16[32,128,128]{2,1,0:T(8,128)(2,1)} collective-permute-done((bf16[32,128,128]{2,1,0:T(8,128)(2,1)}, bf16[32,128,128]{2,1,0:T(8,128)(2,1)}, u32[]{:S(2)}, u32[]{:S(2)}) %collective-permute-start.4) | collective-permute-done | bytes 1048608 | tf_op jit(solution)/shard_map/ppermute | solution.py:356
  127.3 12.8 %collective-permute-done.5.refs_3_ = bf16[32,128,128]{2,1,0:T(8,128)(2,1)} collective-permute-done((bf16[32,128,128]{2,1,0:T(8,128)(2,1)}, bf16[32,128,128]{2,1,0:T(8,128)(2,1)}, u32[]{:S(2)}, u32[]{:S(2)}) %collective-permute-start.5) | collective-permute-done | bytes 1048608 | tf_op jit(solution)/shard_map/ppermute | solution.py:356
  140.1 23.3 %shard_map.85 = bf16[32,4,128,128]{3,2,1,0:T(8,128)(2,1)} custom-call(s32[2]{0:T(128)} %pad_add_fusion.me_ref, bf16[32,128,128]{2,1,0:T(8,128)(2,1)} %get-tuple-element.46.refs_0_, bf16[32,128,128]{2,1,0:T(8,128)(2,1)} %collective-permute-done.3.refs_1_, bf16[32,128,128]{2,1,0:T(8,128)(2,1)} %collective-permute-done.4.refs_2_, ...), custom_call_target="tpu_custom_call" | custom-call | flops 120000004096 | bytes 25165824 | tf_op jit(solution)/shard_map/pallas_call | solution.py:184
  163.4 45.7 %collective-permute-done.7.refs_4_ = bf16[8,512,256]{2,1,0:T(8,128)(2,1)S(1)} collective-permute-done((bf16[8,512,256]{2,1,0:T(8,128)(2,1)S(1)}, bf16[8,512,256]{2,1,0:T(8,128)(2,1)S(1)}, u32[]{:S(2)}, u32[]{:S(2)}) %collective-permute-start.7) | collective-permute-done | bytes 2097184 | tf_op jit(solution)/shard_map/ppermute | solution.py:316
  209.1 0.0 copy-start.2
  209.1 3.4 collective-permute-done.6.refs_2_
  212.5 0.0 collective-permute-start.8
  212.5 0.5 collective-permute-start.9
  213.0 0.0 all-to-all-done.2.depth_ref
  213.0 0.0 copy-done.2
  213.0 5.8 %all-to-all-start.1 = ((bf16[32,512,128]{2,1,0:T(8,128)(2,1)}), bf16[32,512,128]{2,1,0:T(8,128)(2,1)}, u32[]{:S(2)}, u32[]{:S(2)}) async-start(bf16[32,512,128]{2,1,0:T(8,128)(2,1)} %bitcast.32), calls=%async_computation.1 | async-start | bytes 8388608 | tf_op jit(solution)/shard_map/all_to_all | solution.py:369
  218.8 1.1 collective-permute-done.8.refs_3_
  219.9 0.0 collective-permute-done.9.refs_5_
  219.9 24.8 %shard_map.87.refs_8_ = f32[2,2,512,2048]{3,2,1,0:T(8,128)} custom-call(s32[2]{0:T(128)} %pad_add_fusion.me_ref, bf16[32,512,128]{2,1,0:T(8,128)(2,1)} %all-to-all-done.2.depth_ref, bf16[8,2,1024,256]{3,2,1,0:T(8,128)(2,1)} %bitcast.37, bf16[8,2,1024,256]{3,2,1,0:T(8,128)(2,1)} %bitcast.38, bf16[8,512,256]{2,1,0:T(8,128)(2,1)} %collective-permute-done.6.refs_2_, ...), custom_call_target="tpu_custom_call" | custom-call | flops 120000004096 | bytes 29360128 | tf_op jit(solution)/shard_map/pallas_call | solution.py:271
  244.7 69.0 %all-to-all-done.1.depth_ref = bf16[32,512,128]{2,1,0:T(8,128)(2,1)} async-done(((bf16[32,512,128]{2,1,0:T(8,128)(2,1)}), bf16[32,512,128]{2,1,0:T(8,128)(2,1)}, u32[]{:S(2)}, u32[]{:S(2)}) %all-to-all-start.1) | async-done | bytes 4194336 | tf_op jit(solution)/shard_map/all_to_all | solution.py:369
  313.7 24.8 %shard_map.88 = f32[2,2,512,2048]{3,2,1,0:T(8,128)} custom-call(s32[2]{0:T(128)} %pad_add_fusion.me_ref, bf16[32,512,128]{2,1,0:T(8,128)(2,1)} %all-to-all-done.1.depth_ref, bf16[8,2,1024,256]{3,2,1,0:T(8,128)(2,1)} %bitcast.41, bf16[8,2,1024,256]{3,2,1,0:T(8,128)(2,1)} %bitcast.42, ...), custom_call_target="tpu_custom_call", output_to_operand_aliasing={{}: (10, {})} | custom-call | flops 120000004096 | bytes 29360128 | tf_op jit(solution)/shard_map/pallas_call | solution.py:271
  (4 shorter events, 0.1 us)
Async XLA Ops:
  6.5 3.2 copy-start
  6.5 3.2 copy-start.1
  6.5 97.7 %all-gather.3.cloned.1.call-start = ((), (), s32[]{:S(2)}) async-start(), calls=%async_computation.3 | async-start | bytes 9437184 | tf_op jit(solution)/shard_map/all_gather | solution.py:341
  10.5 12.7 %all-to-all-start = ((f32[4,3,32,128]{3,2,1,0:T(8,128)}), f32[4,3,32,128]{3,2,1,0:T(8,128)S(1)}, u32[]{:S(2)}, u32[]{:S(2)}) async-start(f32[4,3,32,128]{3,2,1,0:T(8,128)} %broadcast_in_dim.8), calls=%async_computation | async-start | bytes 393216 | tf_op jit(solution)/shard_map/all_to_all | solution.py:346
  23.3 33.9 %collective-permute-start = (bf16[32,128,128]{2,1,0:T(8,128)(2,1)}, bf16[32,128,128]{2,1,0:T(8,128)(2,1)S(1)}, u32[]{:S(2)}, u32[]{:S(2)}) collective-permute-start(bf16[32,128,128]{2,1,0:T(8,128)(2,1)} %get-tuple-element.39), channel_id=1, source_target_pairs={{0,8},{8,0},{16,24},{24,16},{1,9},{9,1},{17,25},{25,17},{2,10},{10... | collective-permute-start | bytes 3145736 | tf_op jit(solution)/shard_map/ppermute | solution.py:356
  25.4 46.7 %collective-permute-start.1 = (bf16[32,128,128]{2,1,0:T(8,128)(2,1)}, bf16[32,128,128]{2,1,0:T(8,128)(2,1)S(1)}, u32[]{:S(2)}, u32[]{:S(2)}) collective-permute-start(bf16[32,128,128]{2,1,0:T(8,128)(2,1)} %get-tuple-element.40), channel_id=1, source_target_pairs={{0,16},{8,24},{16,0},{24,8},{1,17},{9,25},{17,1},{25,9},{2,18},{10... | collective-permute-start | bytes 3145736 | tf_op jit(solution)/shard_map/ppermute | solution.py:356
  26.9 45.3 %collective-permute-start.2 = (bf16[32,128,128]{2,1,0:T(8,128)(2,1)}, bf16[32,128,128]{2,1,0:T(8,128)(2,1)S(1)}, u32[]{:S(2)}, u32[]{:S(2)}) collective-permute-start(bf16[32,128,128]{2,1,0:T(8,128)(2,1)} %get-tuple-element.41), channel_id=1, source_target_pairs={{0,24},{8,16},{16,8},{24,0},{1,25},{9,17},{17,9},{25,1},{2,26},{10... | collective-permute-start | bytes 3145736 | tf_op jit(solution)/shard_map/ppermute | solution.py:356
  57.2 18.5 %copy-start.3 = (bf16[32,128,128]{2,1,0:T(8,128)(2,1)}, bf16[32,128,128]{2,1,0:T(8,128)(2,1)S(1)}, u32[]{:S(2)}) copy-start(bf16[32,128,128]{2,1,0:T(8,128)(2,1)S(1)} %collective-permute-done.refs_1_) | copy-start | bytes 3145732
  72.1 3.6 %copy-start.4 = (bf16[32,128,128]{2,1,0:T(8,128)(2,1)}, bf16[32,128,128]{2,1,0:T(8,128)(2,1)S(1)}, u32[]{:S(2)}) copy-start(bf16[32,128,128]{2,1,0:T(8,128)(2,1)S(1)} %collective-permute-done.1.refs_2_) | copy-start | bytes 3145732
  72.1 3.6 %copy-start.5 = (bf16[32,128,128]{2,1,0:T(8,128)(2,1)}, bf16[32,128,128]{2,1,0:T(8,128)(2,1)S(1)}, u32[]{:S(2)}) copy-start(bf16[32,128,128]{2,1,0:T(8,128)(2,1)S(1)} %collective-permute-done.2.refs_3_) | copy-start | bytes 3145732
  72.1 37.1 %collective-permute-start.3 = (bf16[32,128,128]{2,1,0:T(8,128)(2,1)}, bf16[32,128,128]{2,1,0:T(8,128)(2,1)}, u32[]{:S(2)}, u32[]{:S(2)}) collective-permute-start(bf16[32,128,128]{2,1,0:T(8,128)(2,1)} %get-tuple-element.47), channel_id=1, source_target_pairs={{0,8},{8,0},{16,24},{24,16},{1,9},{9,1},{17,25},{25,17},{2,10},{10... | collective-permute-start | bytes 3145736 | tf_op jit(solution)/shard_map/ppermute | solution.py:356
  73.3 54.0 %collective-permute-start.4 = (bf16[32,128,128]{2,1,0:T(8,128)(2,1)}, bf16[32,128,128]{2,1,0:T(8,128)(2,1)}, u32[]{:S(2)}, u32[]{:S(2)}) collective-permute-start(bf16[32,128,128]{2,1,0:T(8,128)(2,1)} %get-tuple-element.48), channel_id=1, source_target_pairs={{0,16},{8,24},{16,0},{24,8},{1,17},{9,25},{17,1},{25,9},{2,18},{10... | collective-permute-start | bytes 3145736 | tf_op jit(solution)/shard_map/ppermute | solution.py:356
  74.2 65.9 %collective-permute-start.5 = (bf16[32,128,128]{2,1,0:T(8,128)(2,1)}, bf16[32,128,128]{2,1,0:T(8,128)(2,1)}, u32[]{:S(2)}, u32[]{:S(2)}) collective-permute-start(bf16[32,128,128]{2,1,0:T(8,128)(2,1)} %get-tuple-element.49), channel_id=1, source_target_pairs={{0,24},{8,16},{16,8},{24,0},{1,25},{9,17},{17,9},{25,1},{2,26},{10... | collective-permute-start | bytes 3145736 | tf_op jit(solution)/shard_map/ppermute | solution.py:356
  99.0 114.0 %all-to-all-start.2 = ((bf16[32,512,128]{2,1,0:T(8,128)(2,1)}), bf16[32,512,128]{2,1,0:T(8,128)(2,1)}, u32[]{:S(2)}, u32[]{:S(2)}) async-start(bf16[32,512,128]{2,1,0:T(8,128)(2,1)} %bitcast.31), calls=%async_computation.2 | async-start | bytes 8388608 | tf_op jit(solution)/shard_map/all_to_all | solution.py:369
  106.0 103.1 %collective-permute-start.7 = (bf16[8,512,256]{2,1,0:T(8,128)(2,1)S(1)}, bf16[8,512,256]{2,1,0:T(8,128)(2,1)S(1)}, u32[]{:S(2)}, u32[]{:S(2)}) collective-permute-start(bf16[8,512,256]{2,1,0:T(8,128)(2,1)S(1)} %dynamic-slice_bitcast_fusion), channel_id=1, source_target_pairs={{0,16},{8,24},{16,0},{24,8},{1,17},{9,25},{17,1},{25,9},{2,18},{10... | collective-permute-start | bytes 6291464 | tf_op jit(solution)/shard_map/ppermute | solution.py:316
  107.7 104.8 %collective-permute-start.6 = (bf16[8,512,256]{2,1,0:T(8,128)(2,1)S(1)}, bf16[8,512,256]{2,1,0:T(8,128)(2,1)}, u32[]{:S(2)}, u32[]{:S(2)}) collective-permute-start(bf16[8,512,256]{2,1,0:T(8,128)(2,1)S(1)} %dynamic-slice_bitcast_fusion), channel_id=1, source_target_pairs={{0,8},{8,0},{16,24},{24,16},{1,9},{9,1},{17,25},{25,17},{2,10},{10... | collective-permute-start | bytes 6291464 | tf_op jit(solution)/shard_map/ppermute | solution.py:316
  209.1 3.9 %copy-start.2 = (bf16[8,512,256]{2,1,0:T(8,128)(2,1)}, bf16[8,512,256]{2,1,0:T(8,128)(2,1)S(1)}, u32[]{:S(2)}) copy-start(bf16[8,512,256]{2,1,0:T(8,128)(2,1)S(1)} %collective-permute-done.7.refs_4_) | copy-start | bytes 6291460
  212.5 7.5 %collective-permute-start.8 = (bf16[8,512,256]{2,1,0:T(8,128)(2,1)}, bf16[8,512,256]{2,1,0:T(8,128)(2,1)}, u32[]{:S(2)}, u32[]{:S(2)}) collective-permute-start(bf16[8,512,256]{2,1,0:T(8,128)(2,1)} %collective-permute-done.6.refs_2_), channel_id=1, source_target_pairs={{0,1},{1,0},{2,3},{3,2},{4,5},{5,4},{6,7},{7,6},{8,9},{9,8},{10,11... | collective-permute-start | bytes 6291464 | tf_op jit(solution)/shard_map/ppermute | solution.py:324
  212.5 7.5 %collective-permute-start.9 = (bf16[8,512,256]{2,1,0:T(8,128)(2,1)S(1)}, bf16[8,512,256]{2,1,0:T(8,128)(2,1)}, u32[]{:S(2)}, u32[]{:S(2)}) collective-permute-start(bf16[8,512,256]{2,1,0:T(8,128)(2,1)S(1)} %collective-permute-done.7.refs_4_), channel_id=1, source_target_pairs={{0,1},{1,0},{2,3},{3,2},{4,5},{5,4},{6,7},{7,6},{8,9},{9,8},{10,11... | collective-permute-start | bytes 6291464 | tf_op jit(solution)/shard_map/ppermute | solution.py:324
  213.0 100.7 %all-to-all-start.1 = ((bf16[32,512,128]{2,1,0:T(8,128)(2,1)}), bf16[32,512,128]{2,1,0:T(8,128)(2,1)}, u32[]{:S(2)}, u32[]{:S(2)}) async-start(bf16[32,512,128]{2,1,0:T(8,128)(2,1)} %bitcast.32), calls=%async_computation.1 | async-start | bytes 8388608 | tf_op jit(solution)/shard_map/all_to_all | solution.py:369
Sparse Core Ops, SparseCore 0:
  9.8 84.7 all-gather.2

commit v8 on v7

--- a/solution.py
+++ b/solution.py
@@ -218,11 +218,11 @@
     return [mask for mask in range(count) if bin(mask).count("1") % 2 == 0]
 
 
-def refocus_kernel(wave_count, pix_count, me_ref, depth_ref, *refs):
-    prop_refs = refs[: 2 * wave_count]
+def refocus_kernel(wave_count, pix_count, blocks, me_ref, depth_ref, *refs):
+    prop_refs = refs[:blocks]
     out_ref, rows = refs[-2:]
     _, depths, lanes = depth_ref.shape
-    half = pix_count // 2
+    half, quarter = pix_count // 2, pix_count // 4
     core = me_ref[1]
 
     @pl.when(pl.program_id(0) == 0)
@@ -230,17 +230,18 @@
         sign = jnp.where(left_half((1, lanes)), 1.0, -1.0)
         for m in range(wave_count):
             first = (me_ref[0] ^ m) * pix_count
-            for h in range(2):
-                start = first + (h if m in even_masks(wave_count) else core ^ h) * half
-                for p in range(half):
-                    at = (m * pix_count + h * half + p) * lanes
-                    own = slice(at, at + lanes)
-                    value = depth_ref[start + p].astype(jnp.float32)
-                    rows[:depths, own] = (value * sign).astype(jnp.bfloat16)
-                    rows[depths:, own] = swap_halves(value).astype(jnp.bfloat16)
+            for p in range(pix_count):
+                source = first + p
+                if m not in even_masks(wave_count) and p < half:
+                    source = first + (core ^ (p // quarter)) * quarter + p % quarter
+                at = (m * pix_count + p) * lanes
+                own = slice(at, at + lanes)
+                value = depth_ref[source].astype(jnp.float32)
+                rows[:depths, own] = (value * sign).astype(jnp.bfloat16)
+                rows[depths:, own] = swap_halves(value).astype(jnp.bfloat16)
 
     columns = jnp.concatenate(
-        [ref[...].reshape(half * lanes, ref.shape[-1]) for ref in prop_refs], axis=0
+        [ref[...].reshape(ref.shape[-2:]) for ref in prop_refs], axis=0
     )
     for c in range(2):
         out_ref[c, 0] = jnp.dot(
@@ -257,19 +258,19 @@
     even = even_masks(wave_count)
     operands, specs = [], []
     for mask in range(wave_count):
-        for h in range(2):
-            if mask in even:
-                at = even.index(mask)
-                operands.append(gathered)
-                specs.append(
-                    pl.BlockSpec((1, 1, span, columns), lambda q, at=at, h=h: (q, at, h, 0))
-                )
-            else:
-                operands.append(fetched[mask][h])
-                specs.append(pl.BlockSpec((1, span, columns), lambda q: (q, 0, 0)))
+        if mask in even:
+            at = even.index(mask)
+            operands.append(gathered)
+            specs.append(
+                pl.BlockSpec((1, 1, 2 * span, columns), lambda q, at=at: (q, at, 0, 0))
+            )
+        else:
+            for piece in fetched[mask]:
+                operands.append(piece)
+                specs.append(pl.BlockSpec((1,) + piece.shape[1:], lambda q: (q, 0, 0)))
     earlier = () if image is None else (image,)
     return pl.pallas_call(
-        functools.partial(refocus_kernel, wave_count, pix_count),
+        functools.partial(refocus_kernel, wave_count, pix_count, len(operands)),
         out_shape=jax.ShapeDtypeStruct(
             (2, row_count, depths, pix_count * columns), jnp.float32
         ),
@@ -302,26 +303,24 @@
     return jnp.stack(slices)
 
 
-def fetch_slices(gathered, wave_count, core):
-    pix_count, _, span, columns = gathered.shape
-    half = span // 2
+def fetch_slices(gathered, wave_count, start, rows):
+    pix_count, _, _, columns = gathered.shape
     fetched = {}
     for mask in range(wave_count):
         if mask not in even_masks(wave_count):
             bit = mask & -mask
             at = even_masks(wave_count).index(mask ^ bit)
             own = lax.dynamic_slice(
-                gathered, (0, at, core * half, 0), (pix_count, 1, half, columns)
-            ).reshape(pix_count, half, columns)
+                gathered, (0, at, start, 0), (pix_count, 1, rows, columns)
+            ).reshape(pix_count, rows, columns)
             fetched[mask] = lax.ppermute(
                 own, "wave", [(s, s ^ bit) for s in range(wave_count)]
             )
     return fetched
 
 
-def swap_cores(fetched):
-    pairs = [(s, s ^ 1) for s in range(lax.axis_size("pix"))]
-    return {mask: (own, lax.ppermute(own, "pix", pairs)) for mask, own in fetched.items()}
+def swap_cores(value):
+    return lax.ppermute(value, "pix", [(s, s ^ 1) for s in range(lax.axis_size("pix"))])
 
 
 def on_device(raw_spectra, background, dispersion, propagator):
@@ -361,10 +360,12 @@
         depth = depth_transform(me, arrived, matrices, base, devices)
         if row == 0:
             source, _ = lax.optimization_barrier((gathered, depth))
-            fetched = fetch_slices(source, wave_count, core)
+            quarter = source.shape[2] // 4
+            shared = fetch_slices(source, wave_count, core * quarter, quarter)
         if row == row_count - 1:
-            fetched, _ = lax.optimization_barrier((fetched, depth))
-            fetched = swap_cores(fetched)
+            source, shared, _ = lax.optimization_barrier((source, shared, depth))
+            whole = fetch_slices(source, wave_count, 2 * quarter, 2 * quarter)
+            fetched = {m: (own, swap_cores(own), whole[m]) for m, own in shared.items()}
         depth = depth.reshape(devices, -1, 2 * pixels)
         depth = lax.all_to_all(depth, ("wave", "pix"), split_axis=0, concat_axis=0, tiled=True)
         depths.append(depth)

time: 346 us -> 331 us (0.957)
  waiting for transfers between devices: 165 us -> 148 us
    all_to_all x2, waiting for transfers between devices: 69 us -> 17.9 us  [on_device(): lax.all_to_all(depth, ('wave', 'pix'), split_axis=0, concat_axis=0, tiled...]
    ppermute x2 -> x4, waiting for transfers between devices: 49 us -> 84.3 us  [fetch_slices(): lax.ppermute(own, 'wave', [(s, s ^ bit) for s in range(wave_count)])]
  transfers between devices with their start and end apart: 14 -> 16, of which waited for: 7 -> 8; matrix products, arithmetic and copies ran while one was open for 1% -> 1% of each run, Pallas kernels for 31% -> 33%
where the time goes in v8:
time: 331 us; the launch traced here: 330 us
  waiting for transfers between devices  148 us (45%)
  Pallas kernels  133 us (40%)
  starting transfers between devices  27.2 us (8%)
  between operations  13.5 us (4%)
  local copies, waits for them, and re-layouts  6.03 us (2%)
    ppermute x4, waiting for transfers between devices, fetch_slices(): lax.ppermute(own, 'wave', [(s, s ^ bit) for s in range(wave_count)])  84.3 us
    pallas_call x2, Pallas kernels, refocus(): pl.pallas_call(functools.partial(refocus_kernel, wave_count, pix_count, l...  49.4 us
    pallas_call x2, Pallas kernels, depth_transform(): pl.pallas_call(functools.partial(transform_kernel, steps), out_shape=jax....  46.7 us
    ppermute x6, waiting for transfers between devices, on_device(): lax.ppermute(packed[row][m], 'wave', [(s, s ^ m) for s in range(wave_coun...  46.2 us
    pallas_call x1, Pallas kernels, stage_matrices(): pl.pallas_call(matrix_kernel, out_shape=(jax.ShapeDtypeStruct((k0_count,...  22.1 us
    all_to_all x2, waiting for transfers between devices, on_device(): lax.all_to_all(depth, ('wave', 'pix'), split_axis=0, concat_axis=0, tiled...  17.9 us
    pallas_call x2, Pallas kernels, pack(): pl.pallas_call(pack_kernel, out_shape=[jax.ShapeDtypeStruct((k1_part, k0_...  14.9 us
    all_to_all x2, starting transfers between devices, on_device(): lax.all_to_all(depth, ('wave', 'pix'), split_axis=0, concat_axis=0, tiled...  8.92 us
  transfers between devices with their start and end apart: 16, of which 8 were waited for; matrix products, arithmetic and copies ran while one was open for 1% of the time, Pallas kernels for 33%

profile of v8, /device:TPU:0, one launch (start us, length us, event | category | flops | bytes accessed | tf_op | source)
XLA Modules:
  0.0 329.8 jit_solution(3906891217127986191)
XLA Ops:
  6.5 0.0 copy-start
  6.5 0.0 copy-start.1
  6.5 0.0 all-gather.3.cloned.1.call-start
  6.5 1.3 dynamic-slice_bitcast_fusion.2
  7.9 0.6 pad_add_fusion.me_ref
  8.5 1.1 pad_maximum_fusion
  9.6 0.0 all-gather.3.cloned.1.call-update
  9.6 0.0 copy-done
  9.6 0.1 cosine_bitcast_fusion
  9.7 0.0 copy-done.1
  9.7 0.7 broadcast_in_dim.8
  10.4 5.2 %all-to-all-start = ((f32[4,3,32,128]{3,2,1,0:T(8,128)}), f32[4,3,32,128]{3,2,1,0:T(8,128)S(1)}, u32[]{:S(2)}, u32[]{:S(2)}) async-start(f32[4,3,32,128]{3,2,1,0:T(8,128)} %broadcast_in_dim.8), calls=%async_computation | async-start | bytes 393216 | tf_op jit(solution)/shard_map/all_to_all | solution.py:345
  15.6 7.5 %shard_map.82 = (bf16[32,128,128]{2,1,0:T(8,128)(2,1)}, bf16[32,128,128]{2,1,0:T(8,128)(2,1)}, bf16[32,128,128]{2,1,0:T(8,128)(2,1)}, bf16[32,128,128]{2,1,0:T(8,128)(2,1)}) custom-call(s32[2]{0:T(128)} %pad_add_fusion.me_ref, bf16[2,2,32,128,256]{4,3,2,1,0:T(8,128)(2,1)} %bitcast.31), custom_call_target="tpu_custom_call" | custom-call | bytes 8388608 | tf_op jit(solution)/shard_map/pallas_call | solution.py:56
  23.1 0.0 all-to-all-done
  23.2 2.1 collective-permute-start
  25.3 1.5 collective-permute-start.1
  26.7 0.1 collective-permute-start.2
  26.8 7.4 %shard_map.83 = (bf16[32,128,128]{2,1,0:T(8,128)(2,1)}, bf16[32,128,128]{2,1,0:T(8,128)(2,1)}, bf16[32,128,128]{2,1,0:T(8,128)(2,1)}, bf16[32,128,128]{2,1,0:T(8,128)(2,1)}) custom-call(s32[2]{0:T(128)} %pad_add_fusion.me_ref, bf16[2,2,32,128,256]{4,3,2,1,0:T(8,128)(2,1)} %bitcast.32), custom_call_target="tpu_custom_call" | custom-call | bytes 8388608 | tf_op jit(solution)/shard_map/pallas_call | solution.py:56
  34.2 0.8 copy.17.phase_ref
  35.0 22.1 %shard_map.84 = (bf16[128,256,256]{2,1,0:T(8,128)(2,1)}, f32[2,8,128,16]{3,2,1,0:T(8,128)}) custom-call(f32[3,128,128]{2,1,0:T(8,128)} %copy.17.phase_ref, f32[2,128,128]{2,1,0:T(8,128)} %constant.41.clone.small_ref, f32[2,8,128,16]{3,2,1,0:T(8,128)} %constant.42.clone.turn_ref), custom_call_target="tpu_custom_call" | custom-call | flops 41943040 | bytes 16777216 | tf_op jit(solution)/shard_map/pallas_call | solution.py:102
  57.1 0.0 collective-permute-done.refs_1_
  57.1 0.0 copy-start.3
  57.1 14.9 %collective-permute-done.1.refs_2_ = bf16[32,128,128]{2,1,0:T(8,128)(2,1)S(1)} collective-permute-done((bf16[32,128,128]{2,1,0:T(8,128)(2,1)}, bf16[32,128,128]{2,1,0:T(8,128)(2,1)S(1)}, u32[]{:S(2)}, u32[]{:S(2)}) %collective-permute-start.1) | collective-permute-done | bytes 1048608 | tf_op jit(solution)/shard_map/ppermute | solution.py:355
  72.0 0.0 copy-start.4
  72.0 0.0 collective-permute-done.2.refs_3_
  72.0 0.0 copy-start.5
  72.0 1.2 collective-permute-start.3
  73.2 0.9 collective-permute-start.4
  74.1 1.5 collective-permute-start.5
  75.6 0.0 copy-done.3
  75.6 0.0 copy-done.4
  75.6 0.0 copy-done.5
  75.6 23.4 %shard_map.86 = bf16[32,4,128,128]{3,2,1,0:T(8,128)(2,1)} custom-call(s32[2]{0:T(128)} %pad_add_fusion.me_ref, bf16[32,128,128]{2,1,0:T(8,128)(2,1)} %get-tuple-element.55.refs_0_, bf16[32,128,128]{2,1,0:T(8,128)(2,1)} %copy-done.3, bf16[32,128,128]{2,1,0:T(8,128)(2,1)} %copy-done.4, bf16[32,128,128]{2,1,0:T(8,128)(2,1)} %copy-done.5, ...), custom_call_target="tpu_custom_call" | custom-call | flops 120000004096 | bytes 25165824 | tf_op jit(solution)/shard_map/pallas_call | solution.py:184
  98.9 5.2 %all-to-all-start.2 = ((bf16[32,512,128]{2,1,0:T(8,128)(2,1)}), bf16[32,512,128]{2,1,0:T(8,128)(2,1)}, u32[]{:S(2)}, u32[]{:S(2)}) async-start(bf16[32,512,128]{2,1,0:T(8,128)(2,1)} %bitcast.33), calls=%async_computation.2 | async-start | bytes 8388608 | tf_op jit(solution)/shard_map/all_to_all | solution.py:370
  104.1 0.0 all-gather.3.cloned.1.call-done
  104.1 1.3 dynamic-slice_bitcast_fusion
  105.4 1.8 collective-permute-start.7
  107.2 1.5 collective-permute-start.6
  108.6 0.0 collective-permute-done.3.refs_1_
  108.6 18.5 %collective-permute-done.4.refs_2_ = bf16[32,128,128]{2,1,0:T(8,128)(2,1)} collective-permute-done((bf16[32,128,128]{2,1,0:T(8,128)(2,1)}, bf16[32,128,128]{2,1,0:T(8,128)(2,1)}, u32[]{:S(2)}, u32[]{:S(2)}) %collective-permute-start.4) | collective-permute-done | bytes 1048608 | tf_op jit(solution)/shard_map/ppermute | solution.py:355
  127.2 12.8 %collective-permute-done.5.refs_3_ = bf16[32,128,128]{2,1,0:T(8,128)(2,1)} collective-permute-done((bf16[32,128,128]{2,1,0:T(8,128)(2,1)}, bf16[32,128,128]{2,1,0:T(8,128)(2,1)}, u32[]{:S(2)}, u32[]{:S(2)}) %collective-permute-start.5) | collective-permute-done | bytes 1048608 | tf_op jit(solution)/shard_map/ppermute | solution.py:355
  140.0 23.3 %shard_map.85 = bf16[32,4,128,128]{3,2,1,0:T(8,128)(2,1)} custom-call(s32[2]{0:T(128)} %pad_add_fusion.me_ref, bf16[32,128,128]{2,1,0:T(8,128)(2,1)} %get-tuple-element.47.refs_0_, bf16[32,128,128]{2,1,0:T(8,128)(2,1)} %collective-permute-done.3.refs_1_, bf16[32,128,128]{2,1,0:T(8,128)(2,1)} %collective-permute-done.4.refs_2_, ...), custom_call_target="tpu_custom_call" | custom-call | flops 120000004096 | bytes 25165824 | tf_op jit(solution)/shard_map/pallas_call | solution.py:184
  163.3 19.0 %collective-permute-done.7.refs_4_ = bf16[8,256,256]{2,1,0:T(8,128)(2,1)S(1)} collective-permute-done((bf16[8,256,256]{2,1,0:T(8,128)(2,1)S(1)}, bf16[8,256,256]{2,1,0:T(8,128)(2,1)S(1)}, u32[]{:S(2)}, u32[]{:S(2)}) %collective-permute-start.7) | collective-permute-done | bytes 1048608 | tf_op jit(solution)/shard_map/ppermute | solution.py:316
  182.3 0.0 copy-start.2
  182.3 3.4 %collective-permute-done.6.refs_1_ = bf16[8,256,256]{2,1,0:T(8,128)(2,1)} collective-permute-done((bf16[8,256,256]{2,1,0:T(8,128)(2,1)S(1)}, bf16[8,256,256]{2,1,0:T(8,128)(2,1)}, u32[]{:S(2)}, u32[]{:S(2)}) %collective-permute-start.6) | collective-permute-done | bytes 1048608 | tf_op jit(solution)/shard_map/ppermute | solution.py:316
  185.7 1.7 slice_bitcast_fusion
  187.4 0.1 collective-permute-start.11
  187.5 2.1 collective-permute-start.9
  189.6 0.0 collective-permute-start.8
  189.6 0.5 collective-permute-start.10
  190.1 9.6 %all-to-all-done.2.depth_ref = bf16[32,512,128]{2,1,0:T(8,128)(2,1)} async-done(((bf16[32,512,128]{2,1,0:T(8,128)(2,1)}), bf16[32,512,128]{2,1,0:T(8,128)(2,1)}, u32[]{:S(2)}, u32[]{:S(2)}) %all-to-all-start.2) | async-done | bytes 4194336 | tf_op jit(solution)/shard_map/all_to_all | solution.py:370
  199.7 0.0 copy-done.2
  199.7 3.8 %all-to-all-start.1 = ((bf16[32,512,128]{2,1,0:T(8,128)(2,1)}), bf16[32,512,128]{2,1,0:T(8,128)(2,1)}, u32[]{:S(2)}, u32[]{:S(2)}) async-start(bf16[32,512,128]{2,1,0:T(8,128)(2,1)} %bitcast.34), calls=%async_computation.1 | async-start | bytes 8388608 | tf_op jit(solution)/shard_map/all_to_all | solution.py:370
  203.5 0.0 collective-permute-done.8.refs_2_
  203.5 0.0 collective-permute-done.10.refs_5_
  203.5 61.9 %collective-permute-done.11.refs_6_ = bf16[8,512,256]{2,1,0:T(8,128)(2,1)} collective-permute-done((bf16[8,512,256]{2,1,0:T(8,128)(2,1)S(1)}, bf16[8,512,256]{2,1,0:T(8,128)(2,1)}, u32[]{:S(2)}, u32[]{:S(2)}) %collective-permute-start.11) | collective-permute-done | bytes 2097184 | tf_op jit(solution)/shard_map/ppermute | solution.py:316
  265.4 0.0 collective-permute-done.9.refs_3_
  265.4 24.7 %shard_map.87.refs_8_ = f32[2,2,512,2048]{3,2,1,0:T(8,128)} custom-call(s32[2]{0:T(128)} %pad_add_fusion.me_ref, bf16[32,512,128]{2,1,0:T(8,128)(2,1)} %all-to-all-done.2.depth_ref, bf16[8,2,1024,256]{3,2,1,0:T(8,128)(2,1)} %bitcast.39, bf16[8,256,256]{2,1,0:T(8,128)(2,1)} %collective-permute-done.6.refs_1_, ...), custom_call_target="tpu_custom_call" | custom-call | flops 120000004096 | bytes 29360128 | tf_op jit(solution)/shard_map/pallas_call | solution.py:272
  290.1 8.2 %all-to-all-done.1.depth_ref = bf16[32,512,128]{2,1,0:T(8,128)(2,1)} async-done(((bf16[32,512,128]{2,1,0:T(8,128)(2,1)}), bf16[32,512,128]{2,1,0:T(8,128)(2,1)}, u32[]{:S(2)}, u32[]{:S(2)}) %all-to-all-start.1) | async-done | bytes 4194336 | tf_op jit(solution)/shard_map/all_to_all | solution.py:370
  298.3 24.7 %shard_map.88 = f32[2,2,512,2048]{3,2,1,0:T(8,128)} custom-call(s32[2]{0:T(128)} %pad_add_fusion.me_ref, bf16[32,512,128]{2,1,0:T(8,128)(2,1)} %all-to-all-done.1.depth_ref, bf16[8,2,1024,256]{3,2,1,0:T(8,128)(2,1)} %bitcast.41, bf16[8,256,256]{2,1,0:T(8,128)(2,1)} %collective-permute-done.6.refs_1_, ...), custom_call_target="tpu_custom_call", output_to_operand_aliasing={{}: (10, {})} | custom-call | flops 120000004096 | bytes 29360128 | tf_op jit(solution)/shard_map/pallas_call | solution.py:272
  (4 shorter events, 0.1 us)
Async XLA Ops:
  6.5 3.1 copy-start
  6.5 3.2 copy-start.1
  6.5 97.6 %all-gather.3.cloned.1.call-start = ((), (), s32[]{:S(2)}) async-start(), calls=%async_computation.3 | async-start | bytes 9437184 | tf_op jit(solution)/shard_map/all_gather | solution.py:340
  10.4 12.7 %all-to-all-start = ((f32[4,3,32,128]{3,2,1,0:T(8,128)}), f32[4,3,32,128]{3,2,1,0:T(8,128)S(1)}, u32[]{:S(2)}, u32[]{:S(2)}) async-start(f32[4,3,32,128]{3,2,1,0:T(8,128)} %broadcast_in_dim.8), calls=%async_computation | async-start | bytes 393216 | tf_op jit(solution)/shard_map/all_to_all | solution.py:345
  23.2 34.0 %collective-permute-start = (bf16[32,128,128]{2,1,0:T(8,128)(2,1)}, bf16[32,128,128]{2,1,0:T(8,128)(2,1)S(1)}, u32[]{:S(2)}, u32[]{:S(2)}) collective-permute-start(bf16[32,128,128]{2,1,0:T(8,128)(2,1)} %get-tuple-element.40), channel_id=1, source_target_pairs={{0,8},{8,0},{16,24},{24,16},{1,9},{9,1},{17,25},{25,17},{2,10},{10... | collective-permute-start | bytes 3145736 | tf_op jit(solution)/shard_map/ppermute | solution.py:355
  25.3 46.7 %collective-permute-start.1 = (bf16[32,128,128]{2,1,0:T(8,128)(2,1)}, bf16[32,128,128]{2,1,0:T(8,128)(2,1)S(1)}, u32[]{:S(2)}, u32[]{:S(2)}) collective-permute-start(bf16[32,128,128]{2,1,0:T(8,128)(2,1)} %get-tuple-element.41), channel_id=1, source_target_pairs={{0,16},{8,24},{16,0},{24,8},{1,17},{9,25},{17,1},{25,9},{2,18},{10... | collective-permute-start | bytes 3145736 | tf_op jit(solution)/shard_map/ppermute | solution.py:355
  26.7 45.3 %collective-permute-start.2 = (bf16[32,128,128]{2,1,0:T(8,128)(2,1)}, bf16[32,128,128]{2,1,0:T(8,128)(2,1)S(1)}, u32[]{:S(2)}, u32[]{:S(2)}) collective-permute-start(bf16[32,128,128]{2,1,0:T(8,128)(2,1)} %get-tuple-element.42), channel_id=1, source_target_pairs={{0,24},{8,16},{16,8},{24,0},{1,25},{9,17},{17,9},{25,1},{2,26},{10... | collective-permute-start | bytes 3145736 | tf_op jit(solution)/shard_map/ppermute | solution.py:355
  57.1 18.4 %copy-start.3 = (bf16[32,128,128]{2,1,0:T(8,128)(2,1)}, bf16[32,128,128]{2,1,0:T(8,128)(2,1)S(1)}, u32[]{:S(2)}) copy-start(bf16[32,128,128]{2,1,0:T(8,128)(2,1)S(1)} %collective-permute-done.refs_1_) | copy-start | bytes 3145732
  72.0 3.6 %copy-start.4 = (bf16[32,128,128]{2,1,0:T(8,128)(2,1)}, bf16[32,128,128]{2,1,0:T(8,128)(2,1)S(1)}, u32[]{:S(2)}) copy-start(bf16[32,128,128]{2,1,0:T(8,128)(2,1)S(1)} %collective-permute-done.1.refs_2_) | copy-start | bytes 3145732
  72.0 3.6 %copy-start.5 = (bf16[32,128,128]{2,1,0:T(8,128)(2,1)}, bf16[32,128,128]{2,1,0:T(8,128)(2,1)S(1)}, u32[]{:S(2)}) copy-start(bf16[32,128,128]{2,1,0:T(8,128)(2,1)S(1)} %collective-permute-done.2.refs_3_) | copy-start | bytes 3145732
  72.0 36.6 %collective-permute-start.3 = (bf16[32,128,128]{2,1,0:T(8,128)(2,1)}, bf16[32,128,128]{2,1,0:T(8,128)(2,1)}, u32[]{:S(2)}, u32[]{:S(2)}) collective-permute-start(bf16[32,128,128]{2,1,0:T(8,128)(2,1)} %get-tuple-element.48), channel_id=1, source_target_pairs={{0,8},{8,0},{16,24},{24,16},{1,9},{9,1},{17,25},{25,17},{2,10},{10... | collective-permute-start | bytes 3145736 | tf_op jit(solution)/shard_map/ppermute | solution.py:355
  73.2 54.0 %collective-permute-start.4 = (bf16[32,128,128]{2,1,0:T(8,128)(2,1)}, bf16[32,128,128]{2,1,0:T(8,128)(2,1)}, u32[]{:S(2)}, u32[]{:S(2)}) collective-permute-start(bf16[32,128,128]{2,1,0:T(8,128)(2,1)} %get-tuple-element.49), channel_id=1, source_target_pairs={{0,16},{8,24},{16,0},{24,8},{1,17},{9,25},{17,1},{25,9},{2,18},{10... | collective-permute-start | bytes 3145736 | tf_op jit(solution)/shard_map/ppermute | solution.py:355
  74.1 65.9 %collective-permute-start.5 = (bf16[32,128,128]{2,1,0:T(8,128)(2,1)}, bf16[32,128,128]{2,1,0:T(8,128)(2,1)}, u32[]{:S(2)}, u32[]{:S(2)}) collective-permute-start(bf16[32,128,128]{2,1,0:T(8,128)(2,1)} %get-tuple-element.50), channel_id=1, source_target_pairs={{0,24},{8,16},{16,8},{24,0},{1,25},{9,17},{17,9},{25,1},{2,26},{10... | collective-permute-start | bytes 3145736 | tf_op jit(solution)/shard_map/ppermute | solution.py:355
  98.9 100.8 %all-to-all-start.2 = ((bf16[32,512,128]{2,1,0:T(8,128)(2,1)}), bf16[32,512,128]{2,1,0:T(8,128)(2,1)}, u32[]{:S(2)}, u32[]{:S(2)}) async-start(bf16[32,512,128]{2,1,0:T(8,128)(2,1)} %bitcast.33), calls=%async_computation.2 | async-start | bytes 8388608 | tf_op jit(solution)/shard_map/all_to_all | solution.py:370
  105.4 76.9 %collective-permute-start.7 = (bf16[8,256,256]{2,1,0:T(8,128)(2,1)S(1)}, bf16[8,256,256]{2,1,0:T(8,128)(2,1)S(1)}, u32[]{:S(2)}, u32[]{:S(2)}) collective-permute-start(bf16[8,256,256]{2,1,0:T(8,128)(2,1)S(1)} %dynamic-slice_bitcast_fusion), channel_id=1, source_target_pairs={{0,16},{8,24},{16,0},{24,8},{1,17},{9,25},{17,1},{25,9},{2,18},{10... | collective-permute-start | bytes 3145736 | tf_op jit(solution)/shard_map/ppermute | solution.py:316
  107.2 78.5 %collective-permute-start.6 = (bf16[8,256,256]{2,1,0:T(8,128)(2,1)S(1)}, bf16[8,256,256]{2,1,0:T(8,128)(2,1)}, u32[]{:S(2)}, u32[]{:S(2)}) collective-permute-start(bf16[8,256,256]{2,1,0:T(8,128)(2,1)S(1)} %dynamic-slice_bitcast_fusion), channel_id=1, source_target_pairs={{0,8},{8,0},{16,24},{24,16},{1,9},{9,1},{17,25},{25,17},{2,10},{10... | collective-permute-start | bytes 3145736 | tf_op jit(solution)/shard_map/ppermute | solution.py:316
  182.3 17.4 %copy-start.2 = (bf16[8,256,256]{2,1,0:T(8,128)(2,1)}, bf16[8,256,256]{2,1,0:T(8,128)(2,1)S(1)}, u32[]{:S(2)}) copy-start(bf16[8,256,256]{2,1,0:T(8,128)(2,1)S(1)} %collective-permute-done.7.refs_4_) | copy-start | bytes 3145732
  187.4 78.0 %collective-permute-start.11 = (bf16[8,512,256]{2,1,0:T(8,128)(2,1)S(1)}, bf16[8,512,256]{2,1,0:T(8,128)(2,1)}, u32[]{:S(2)}, u32[]{:S(2)}) collective-permute-start(bf16[8,512,256]{2,1,0:T(8,128)(2,1)S(1)} %slice_bitcast_fusion), channel_id=1, source_target_pairs={{0,16},{8,24},{16,0},{24,8},{1,17},{9,25},{17,1},{25,9},{2,18},{10... | collective-permute-start | bytes 6291464 | tf_op jit(solution)/shard_map/ppermute | solution.py:316
  187.5 77.9 %collective-permute-start.9 = (bf16[8,512,256]{2,1,0:T(8,128)(2,1)S(1)}, bf16[8,512,256]{2,1,0:T(8,128)(2,1)}, u32[]{:S(2)}, u32[]{:S(2)}) collective-permute-start(bf16[8,512,256]{2,1,0:T(8,128)(2,1)S(1)} %slice_bitcast_fusion), channel_id=1, source_target_pairs={{0,8},{8,0},{16,24},{24,16},{1,9},{9,1},{17,25},{25,17},{2,10},{10... | collective-permute-start | bytes 6291464 | tf_op jit(solution)/shard_map/ppermute | solution.py:316
  189.6 13.9 %collective-permute-start.8 = (bf16[8,256,256]{2,1,0:T(8,128)(2,1)}, bf16[8,256,256]{2,1,0:T(8,128)(2,1)}, u32[]{:S(2)}, u32[]{:S(2)}) collective-permute-start(bf16[8,256,256]{2,1,0:T(8,128)(2,1)} %collective-permute-done.6.refs_1_), channel_id=1, source_target_pairs={{0,1},{1,0},{2,3},{3,2},{4,5},{5,4},{6,7},{7,6},{8,9},{9,8},{10,11... | collective-permute-start | bytes 3145736 | tf_op jit(solution)/shard_map/ppermute | solution.py:323
  189.6 13.9 %collective-permute-start.10 = (bf16[8,256,256]{2,1,0:T(8,128)(2,1)S(1)}, bf16[8,256,256]{2,1,0:T(8,128)(2,1)}, u32[]{:S(2)}, u32[]{:S(2)}) collective-permute-start(bf16[8,256,256]{2,1,0:T(8,128)(2,1)S(1)} %collective-permute-done.7.refs_4_), channel_id=1, source_target_pairs={{0,1},{1,0},{2,3},{3,2},{4,5},{5,4},{6,7},{7,6},{8,9},{9,8},{10,11... | collective-permute-start | bytes 3145736 | tf_op jit(solution)/shard_map/ppermute | solution.py:323
  199.7 98.6 %all-to-all-start.1 = ((bf16[32,512,128]{2,1,0:T(8,128)(2,1)}), bf16[32,512,128]{2,1,0:T(8,128)(2,1)}, u32[]{:S(2)}, u32[]{:S(2)}) async-start(bf16[32,512,128]{2,1,0:T(8,128)(2,1)} %bitcast.34), calls=%async_computation.1 | async-start | bytes 8388608 | tf_op jit(solution)/shard_map/all_to_all | solution.py:370
Sparse Core Ops, SparseCore 0:
  9.8 84.7 all-gather.2
